TPU v7x, 256 devices: a whole 4x4x8 slice. The times are simulated.
256 devices in a mesh: comp: 4 (over z_hi, core), lon: 16 (over y, z_lo), lat: 4 (over x).
Axes of the slice: x: 4, y: 4, z: 8 (z_hi: 2, z_lo: 4; z = z_hi * 4 + z_lo), core: 2. Of those that a mesh axis runs over, the one named last changes fastest.
Arguments:
- shell: float32 [8, 32, 1024, 512], P(None, None, ('comp', 'lon'), 'lat'), may hold values from -6 to 6
- resistivity: float32 [32, 1024, 512], P(None, ('comp', 'lon'), 'lat'), may hold values from 0.02 to 0.2
- jacobians: float32 [3, 8, 8], replicated, may hold values from -2 to 2
- current_weights: float32 [8], replicated, may hold values from -4 to 4
- footpoint: int32 [4, 1024, 1], P('lat', ('comp', 'lon')), may hold values from 0 to 15; in each aligned block of 16 rows (0 to 15, 16 to 31, ..., all dimensions but the last counted through in order) at most 2 rows name the same one
- footrow: int32 [4, 1024], P('lat', ('comp', 'lon')), may hold values from 0 to 15
- slab: float32 [40, 8, 1024, 512], P(None, None, ('comp', 'lon'), 'lat'), may hold values from -6 to 6
- conductance: float32 [1024, 512], P(('comp', 'lon'), 'lat'), may hold values from 0.5 to 2
- chemistry: float32 [40, 40], replicated, may hold values from -1 to 1
- coupling: float32 [40, 8], replicated, may hold values from -4 to 4
- potential_weights: float32 [40], replicated, may hold values from -1 to 1
Outputs:
- shell_next: float32 [8, 32, 1024, 512], P(None, None, ('comp', 'lon'), 'lat')
- slab_next: float32 [40, 8, 1024, 512], P(None, None, ('comp', 'lon'), 'lat')
- boundary_potential: float32 [1024, 512], P(('comp', 'lon'), 'lat')
Inputs may be any that keep to these rules, and one draw needn't show every extreme that they name: `footpoint`: within the 16 rows of one device, no value is named by more than 2 rows.
All inputs are finite; a program needn't handle non-finite values.
Results may differ from a plain program's by a relative error of at most 0.00007.
Values sent between devices are 32-bit elements; how exact they have to be, the bound alone decides.
No kernel may reach another device: no remote copies, remote signals or barrier semaphores. Data moves between devices by JAX's collectives and lax.ppermute only.
A program may use at most 128 MiB of HBM per device.

v0:
```python
import jax
import jax.numpy as jnp
from jax import lax
from jax.sharding import PartitionSpec as P

STEP = 0.2
HORIZ = 0.1
VERTICAL = 0.1
COUPLE = 0.1


def with_halo(block, sides, width, periodic):
    for axis, dim in sides:
        count = lax.axis_size(axis)
        forward = [(i, i + 1) for i in range(count - 1)]
        if periodic:
            forward.append((count - 1, 0))
        backward = [(target, source) for source, target in forward]
        low = lax.ppermute(
            lax.slice_in_dim(block, block.shape[dim] - width, None, axis=dim), axis, forward
        )
        high = lax.ppermute(lax.slice_in_dim(block, 0, width, axis=dim), axis, backward)
        block = jnp.concatenate([low, block, high], axis=dim)
    return block


def shell_update(state, extended, resist, jacobians):
    padded = jnp.pad(state, ((0, 0), (1, 1), (0, 0), (0, 0)))
    d_radial = 0.5 * (padded[:, 2:] - padded[:, :-2])
    d_azimuth = 0.5 * (extended[:, :, 2:, 1:-1] - extended[:, :, :-2, 1:-1])
    d_polar = 0.5 * (extended[:, :, 1:-1, 2:] - extended[:, :, 1:-1, :-2])
    laplace = padded[:, 2:] + padded[:, :-2] + extended[:, :, 2:, 1:-1] + extended[:, :, :-2, 1:-1]
    laplace = laplace + extended[:, :, 1:-1, 2:] + extended[:, :, 1:-1, :-2] - 6.0 * state
    flux = jnp.einsum("uv,vrpt->urpt", jacobians[0], d_radial, precision=lax.Precision.HIGHEST)
    flux = flux + jnp.einsum(
        "uv,vrpt->urpt", jacobians[1], d_azimuth, precision=lax.Precision.HIGHEST
    )
    flux = flux + jnp.einsum(
        "uv,vrpt->urpt", jacobians[2], d_polar, precision=lax.Precision.HIGHEST
    )
    return state + STEP * (resist[None] * laplace - flux)


def slab_update(fields, extended, conductance, chemistry, coupling, source):
    horizontal = (
        extended[:, :, 2:, 1:-1]
        + extended[:, :, :-2, 1:-1]
        + extended[:, :, 1:-1, 2:]
        + extended[:, :, 1:-1, :-2]
        - 4.0 * fields
    )
    padded = jnp.pad(fields, ((0, 0), (1, 1), (0, 0), (0, 0)))
    vertical = padded[:, 2:] + padded[:, :-2] - 2.0 * fields
    mixing = jnp.einsum("fg,gklt->fklt", chemistry, fields, precision=lax.Precision.HIGHEST)
    forcing = coupling[:, :, None, None] * source[None, None]
    return (
        fields
        + HORIZ * conductance[None, None] * horizontal
        + VERTICAL * vertical
        + COUPLE * (mixing + forcing)
    )


def extend_shell(array):
    wrapped = with_halo(array, ((("comp", "lon"), 2),), 1, True)
    return with_halo(wrapped, (("lat", 3),), 1, False)


def extend_slab(array):
    wrapped = with_halo(array, ((("comp", "lon"), 2),), 1, True)
    return with_halo(wrapped, (("lat", 3),), 1, False)


def shards(
    shell,
    resistivity,
    jacobians,
    current_weights,
    footpoint,
    footrow,
    slab,
    conductance,
    chemistry,
    coupling,
    potential_weights,
):
    shell_next = shell_update(shell, extend_shell(shell), resistivity, jacobians)
    currents = jnp.einsum(
        "v,vpt->pt", current_weights, shell_next[:, 0], precision=lax.Precision.HIGHEST
    )
    target_lon = footpoint[0, :, 0]
    target_row = footrow[0]
    blocks = lax.axis_size("lon")
    rows_here = target_lon.shape[0]
    capacity = max(2, 2 * rows_here // blocks)
    positions = jnp.arange(rows_here, dtype=jnp.int32)
    earlier = (target_lon[:, None] == target_lon[None, :]) & (
        positions[None, :] < positions[:, None]
    )
    slot_rank = jnp.sum(earlier.astype(jnp.int32), axis=1)
    bins = target_lon * capacity + slot_rank
    select = (bins[:, None] == jnp.arange(blocks * capacity, dtype=jnp.int32)[None, :]).astype(
        jnp.float32
    )
    send_rows = jnp.dot(select.T, currents, precision=lax.Precision.HIGHEST).reshape(
        blocks, capacity, -1
    )
    marked = (target_row + 1).astype(jnp.float32)
    send_target = (jnp.dot(select.T, marked, precision=lax.Precision.HIGHEST) - 1.0).reshape(
        blocks, capacity
    )
    got_rows, got_target = (
        lax.all_to_all(send_rows, "lon", split_axis=0, concat_axis=0, tiled=True),
        lax.all_to_all(send_target, "lon", split_axis=0, concat_axis=0, tiled=True),
    )
    lon_cells = slab.shape[2]
    landing = got_target.reshape(-1).astype(jnp.int32)
    place = (jnp.arange(lon_cells, dtype=jnp.int32)[:, None] == landing[None, :]).astype(
        jnp.float32
    )
    source = jnp.dot(
        place, got_rows.reshape(blocks * capacity, -1), precision=lax.Precision.HIGHEST
    )
    slab_mid = slab_update(slab, extend_slab(slab), conductance, chemistry, coupling, source)
    slab_next = slab_update(
        slab_mid, extend_slab(slab_mid), conductance, chemistry, coupling, source
    )
    potential = jnp.einsum(
        "f,flt->lt", potential_weights, slab_next[:, 0], precision=lax.Precision.HIGHEST
    )
    gathered = lax.all_gather(potential, "lon", axis=0, tiled=True)
    wanted = target_lon * lon_cells + target_row
    picker = (wanted[:, None] == jnp.arange(blocks * lon_cells, dtype=jnp.int32)[None, :]).astype(
        jnp.float32
    )
    boundary_potential = jnp.dot(picker, gathered, precision=lax.Precision.HIGHEST)
    return (shell_next, slab_next, boundary_potential)


def solution(mesh):
    placed = (
        P(None, None, ("comp", "lon"), "lat"),
        P(None, ("comp", "lon"), "lat"),
        P(),
        P(),
        P("lat", ("comp", "lon"), None),
        P("lat", ("comp", "lon")),
        P(None, None, ("comp", "lon"), "lat"),
        P(("comp", "lon"), "lat"),
        P(),
        P(),
        P(),
    )
    return jax.shard_map(
        shards,
        mesh=mesh,
        in_specs=placed,
        out_specs=(
            P(None, None, ("comp", "lon"), "lat"),
            P(None, None, ("comp", "lon"), "lat"),
            P(("comp", "lon"), "lat"),
        ),
        check_vma=False,
    )
```

profile of v0, /device:TPU:4, one launch (start us, length us, event | category | flops | bytes accessed | tf_op | source)
XLA Modules:
  0.0 199.1 jit_solution(8503670580991991544)
XLA Ops:
  0.6 0.0 copy-start
  0.7 2.8 %copy.98 = f32[8,32,16,128]{3,0,2,1:T(8,128)S(1)} copy(f32[8,32,16,128]{3,2,1,0:T(8,128)} %param.11) | data formatting | bytes 4194304 | tf_op args[0]
  3.5 0.0 copy-start.1
  3.5 7.8 %collective-permute-start = (f32[8,32,1,128]{3,0,2,1:T(8,128)S(1)}, f32[8,32,1,128]{3,0,2,1:T(8,128)S(1)}, u32[]{:S(2)}, u32[]{:S(2)}) collective-permute-start(f32[8,32,1,128]{3,0,2,1:T(8,128)S(1)} %get-tuple-element.26), channel_id=1, source_target_pairs={{4,0},{8,4},{12,8},{16,12},{20,16},{24,20},{28,24},{32,28},{36,32}... | collective-permute-start | bytes 393224 | tf_op jit(solution)/shard_map/ppermute | solution.py:22
  11.4 0.0 collective-permute-start.1
  11.4 0.2 convert_reduce_fusion.1
  11.6 0.1 fusion.35
  11.7 0.7 all_to_all.9
  12.4 6.4 %all-to-all-start = ((f32[16,1,2]{2,1,0:T(1,128)}), f32[16,1,2]{2,1,0:T(1,128)S(1)}, u32[]{:S(2)}, u32[]{:S(2)}) async-start(f32[16,1,2]{2,1,0:T(1,128)} %bitcast.16), calls=%async_computation | async-start | bytes 16384 | tf_op jit(solution)/shard_map/all_to_all | solution.py:114
  18.8 0.0 copy-start.7
  18.8 3.3 %copy.109 = f32[40,8,16,128]{3,0,2,1:T(8,128)S(1)} copy(f32[40,8,16,128]{3,2,1,0:T(8,128)} %param.17) | data formatting | bytes 5242880 | tf_op args[6]
  22.0 0.0 copy-start.3
  22.1 0.0 copy-start.8
  22.1 2.0 %collective-permute-start.5 = (f32[40,8,1,128]{3,0,2,1:T(8,128)S(1)}, f32[40,8,1,128]{3,0,2,1:T(8,128)S(1)}, u32[]{:S(2)}, u32[]{:S(2)}) collective-permute-start(f32[40,8,1,128]{3,0,2,1:T(8,128)S(1)} %get-tuple-element.22), channel_id=1, source_target_pairs={{0,4},{4,8},{8,12},{12,16},{16,20},{20,24},{24,28},{28,32},{32,36}... | collective-permute-start | bytes 491528 | tf_op jit(solution)/shard_map/ppermute | solution.py:19
  24.1 3.5 %collective-permute-start.4 = (f32[40,8,1,128]{3,0,2,1:T(8,128)S(1)}, f32[40,8,1,128]{3,0,2,1:T(8,128)}, u32[]{:S(2)}, u32[]{:S(2)}) collective-permute-start(f32[40,8,1,128]{3,0,2,1:T(8,128)S(1)} %get-tuple-element.21), channel_id=1, source_target_pairs={{4,0},{8,4},{12,8},{16,12},{20,16},{24,20},{28,24},{32,28},{36,32}... | collective-permute-start | bytes 491528 | tf_op jit(solution)/shard_map/ppermute | solution.py:22
  27.6 3.3 %fusion.32 = f32[32,16,128,8]{2,3,1,0:T(8,128)} fusion(f32[8,32,16,128]{3,0,2,1:T(8,128)S(1)} %copy.98, f32[3,8,8]{2,1,0:T(8,128)S(1)} %copy-done.7), kind=kOutput, calls=%fused_computation.58 | convolution fusion | flops 51380224 | bytes 4198400 | tf_op jit(solution)/shard_map/uv,vrpt->urpt/dot_general | solution.py:34
  31.0 0.0 all-to-all-done
  31.0 0.1 convert_element_type.27
  31.2 2.8 %constant_dynamic-update-slice_fusion.1 = f32[8,32,18,128]{3,0,2,1:T(8,128)S(1)} fusion(f32[8,32,18,128]{3,0,2,1:T(8,128)S(1)} %constant_dynamic-update-slice_fusion.2, f32[8,32,16,128]{3,2,1,0:T(8,128)} %param.11), kind=kLoop, calls=%fused_computation.76 | loop fusion | bytes 4194304
  34.0 2.9 %fusion.76 = (f32[8,32,18,1]{3,0,2,1:T(8,128)}, f32[8,32,18,1]{3,0,2,1:T(8,128)}) fusion(f32[8,32,18,128]{3,0,2,1:T(8,128)S(1)} %constant_dynamic-update-slice_fusion), kind=kLoop, calls=%fused_computation.119 | loop fusion | bytes 73728 | tf_op jit(solution)/shard_map/slice | solution.py:20
  36.9 2.6 %copy.93 = f32[8,32,18,1]{1,0,3,2:T(8,128)S(1)} copy(f32[8,32,18,1]{3,0,2,1:T(8,128)} %get-tuple-element.24) | data formatting | bytes 36864 | tf_op jit(solution)/shard_map/slice | solution.py:22
  39.5 2.6 %collective-permute-start.2 = (f32[8,32,18,1]{1,0,3,2:T(8,128)S(1)}, f32[8,32,18,1]{1,0,3,2:T(8,128)}, u32[]{:S(2)}, u32[]{:S(2)}) collective-permute-start(f32[8,32,18,1]{1,0,3,2:T(8,128)S(1)} %copy.93), channel_id=1, source_target_pairs={{1,0},{2,1},{3,2},{5,4},{6,5},{7,6},{9,8},{10,9},{11,10},{13,12},{... | collective-permute-start | bytes 55304 | tf_op jit(solution)/shard_map/ppermute | solution.py:22
  42.1 3.2 %copy.95 = f32[8,32,18,1]{1,0,3,2:T(8,128)} copy(f32[8,32,18,1]{3,0,2,1:T(8,128)} %get-tuple-element.23) | data formatting | bytes 36864 | tf_op jit(solution)/shard_map/slice | solution.py:20
  45.3 3.8 %collective-permute-start.3 = (f32[8,32,18,1]{1,0,3,2:T(8,128)}, f32[8,32,18,1]{1,0,3,2:T(8,128)}, u32[]{:S(2)}, u32[]{:S(2)}) collective-permute-start(f32[8,32,18,1]{1,0,3,2:T(8,128)} %copy.95), channel_id=1, source_target_pairs={{0,1},{1,2},{2,3},{4,5},{5,6},{6,7},{8,9},{9,10},{10,11},{12,13},{... | collective-permute-start | bytes 55304 | tf_op jit(solution)/shard_map/ppermute | solution.py:19
  49.2 5.5 %fusion.29 = f32[32,16,128,8]{2,3,1,0:T(8,128)} fusion(f32[8,32,1,128]{3,0,2,1:T(8,128)S(1)} %collective-permute-done, f32[8,32,16,128]{3,0,2,1:T(8,128)} %copy-done.1, f32[8,32,1,128]{3,0,2,1:T(8,128)S(1)} %collective-permute-done.1, f32[3,8,8]{2,1,0:T(8,128)S(1)} %copy-done.7), kind=kOutput, calls=%fused_computation.55 | convolution fusion | flops 52428800 | bytes 4460544 | tf_op jit(solution)/shard_map/uv,vrpt->urpt/dot_general | solution.py:35
  54.7 0.0 collective-permute-done.2
  54.7 3.3 %copy.94 = f32[8,32,18,1]{3,0,2,1:T(8,128)} copy(f32[8,32,18,1]{1,0,3,2:T(8,128)} %collective-permute-done.2) | data formatting | bytes 36864 | tf_op jit(solution)/shard_map/ppermute | solution.py:22
  58.0 3.3 %copy.96 = f32[8,32,18,1]{3,0,2,1:T(8,128)} copy(f32[8,32,18,1]{1,0,3,2:T(8,128)} %collective-permute-done.3) | data formatting | bytes 36864 | tf_op jit(solution)/shard_map/ppermute | solution.py:19
  61.2 11.2 %fusion.25 = f32[8,32,16,128]{3,0,2,1:T(8,128)S(1)} fusion(f32[8,32,16,128]{3,0,2,1:T(8,128)} %copy-done.1, f32[32,16,128,8]{2,3,1,0:T(8,128)} %fusion.32, f32[32,16,128,8]{2,3,1,0:T(8,128)} %fusion.29, f32[8,32,1,128]{3,0,2,1:T(8,128)S(1)} %collective-permute-done, f32[8,32,1,128]{3,0,2,1:T(8,128)S(1)} %collective-permute-done.1, ...), kind=kOutput, calls=%fused_computation.51 | convolution fusion | flops 61341696 | bytes 23072768 | tf_op jit(solution)/shard_map/uv,vrpt->urpt/dot_general | solution.py:38
  72.5 1.4 copy-done.2
  73.8 0.2 fusion.42
  74.0 0.9 fusion.50
  74.9 4.1 %all-to-all-start.1 = ((f32[16,2,128]{2,1,0:T(2,128)}), f32[16,2,128]{2,1,0:T(2,128)S(1)}, u32[]{:S(2)}, u32[]{:S(2)}) async-start(f32[16,2,128]{2,1,0:T(2,128)} %bitcast.21), calls=%async_computation.1 | async-start | bytes 32768 | tf_op jit(solution)/shard_map/all_to_all | solution.py:113
  79.0 3.3 %constant_dynamic-update-slice_fusion.4 = f32[40,8,18,128]{3,0,2,1:T(8,128)S(1)} fusion(f32[40,8,18,128]{3,0,2,1:T(8,128)S(1)} %constant_dynamic-update-slice_fusion.5, f32[40,8,16,128]{3,2,1,0:T(8,128)} %param.17), kind=kLoop, calls=%fused_computation.79 | loop fusion | bytes 5242880
  82.3 0.9 constant_dynamic-update-slice_fusion.3
  83.2 3.4 %fusion.73 = (f32[40,8,18,1]{3,0,2,1:T(8,128)}, f32[40,8,18,1]{3,0,2,1:T(8,128)}) fusion(f32[40,8,18,128]{3,0,2,1:T(8,128)S(1)} %constant_dynamic-update-slice_fusion.3), kind=kLoop, calls=%fused_computation.116 | loop fusion | bytes 92160 | tf_op jit(solution)/shard_map/slice | solution.py:22
  86.6 2.9 %copy.104 = f32[40,8,18,1]{0,1,3,2:T(8,128)S(1)} copy(f32[40,8,18,1]{3,0,2,1:T(8,128)} %get-tuple-element.17) | data formatting | bytes 46080 | tf_op jit(solution)/shard_map/slice | solution.py:22
  89.5 2.0 %collective-permute-start.6 = (f32[40,8,18,1]{0,1,3,2:T(8,128)S(1)}, f32[40,8,18,1]{0,1,3,2:T(8,128)S(1)}, u32[]{:S(2)}, u32[]{:S(2)}) collective-permute-start(f32[40,8,18,1]{0,1,3,2:T(8,128)S(1)} %copy.104), channel_id=1, source_target_pairs={{1,0},{2,1},{3,2},{5,4},{6,5},{7,6},{9,8},{10,9},{11,10},{13,12},{... | collective-permute-start | bytes 69128 | tf_op jit(solution)/shard_map/ppermute | solution.py:22
  91.5 2.9 %copy.106 = f32[40,8,18,1]{0,1,3,2:T(8,128)S(1)} copy(f32[40,8,18,1]{3,0,2,1:T(8,128)} %get-tuple-element.18) | data formatting | bytes 46080 | tf_op jit(solution)/shard_map/slice | solution.py:20
  94.4 4.1 %collective-permute-start.7 = (f32[40,8,18,1]{0,1,3,2:T(8,128)S(1)}, f32[40,8,18,1]{0,1,3,2:T(8,128)S(1)}, u32[]{:S(2)}, u32[]{:S(2)}) collective-permute-start(f32[40,8,18,1]{0,1,3,2:T(8,128)S(1)} %copy.106), channel_id=1, source_target_pairs={{0,1},{1,2},{2,3},{4,5},{5,6},{6,7},{8,9},{9,10},{10,11},{12,13},{... | collective-permute-start | bytes 69128 | tf_op jit(solution)/shard_map/ppermute | solution.py:19
  98.4 0.1 fusion.48
  98.6 0.0 collective-permute-done.6
  98.6 2.7 %copy.105 = f32[40,8,18,1]{3,0,2,1:T(8,128)} copy(f32[40,8,18,1]{0,1,3,2:T(8,128)S(1)} %collective-permute-done.6) | data formatting | bytes 46080 | tf_op jit(solution)/shard_map/ppermute | solution.py:22
  101.2 2.6 %copy.107 = f32[40,8,18,1]{3,0,2,1:T(8,128)} copy(f32[40,8,18,1]{0,1,3,2:T(8,128)S(1)} %collective-permute-done.7) | data formatting | bytes 46080 | tf_op jit(solution)/shard_map/ppermute | solution.py:19
  103.9 10.6 %fusion.4 = f32[40,8,16,128]{3,0,2,1:T(8,128)S(1)} fusion(f32[40,8,16,128]{3,0,2,1:T(8,128)} %copy-done.3, f32[40,8,18,128]{3,0,2,1:T(8,128)S(1)} %constant_dynamic-update-slice_fusion.3, f32[40,8,18,1]{3,0,2,1:T(8,128)} %copy.107, f32[40,8,18,1]{3,0,2,1:T(8,128)} %copy.105, f32[40,8,1,128]{3,0,2,1:T(8,128)S(1)} %collective-permute-done.5, ...), kind=kOutput, calls=%fused_computation.11 | convolution fusion | flops 327680000 | bytes 17063424 | tf_op jit(solution)/shard_map/fg,gklt->fklt/dot_general | solution.py:54
  114.5 0.0 copy-start.4
  114.5 5.3 %collective-permute-start.8 = (f32[40,8,1,128]{3,0,2,1:T(8,128)S(1)}, f32[40,8,1,128]{3,0,2,1:T(8,128)S(1)}, u32[]{:S(2)}, u32[]{:S(2)}) collective-permute-start(f32[40,8,1,128]{3,0,2,1:T(8,128)S(1)} %get-tuple-element.20), channel_id=1, source_target_pairs={{4,0},{8,4},{12,8},{16,12},{20,16},{24,20},{28,24},{32,28},{36,32}... | collective-permute-start | bytes 491528 | tf_op jit(solution)/shard_map/ppermute | solution.py:22
  119.9 2.8 %collective-permute-done.8 = f32[40,8,1,128]{3,0,2,1:T(8,128)S(1)} collective-permute-done((f32[40,8,1,128]{3,0,2,1:T(8,128)S(1)}, f32[40,8,1,128]{3,0,2,1:T(8,128)S(1)}, u32[]{:S(2)}, u32[]{:S(2)}) %collective-permute-start.8) | collective-permute-done | bytes 163872 | tf_op jit(solution)/shard_map/ppermute | solution.py:22
  122.7 5.5 %collective-permute-done.9 = f32[40,8,1,128]{3,0,2,1:T(8,128)S(1)} collective-permute-done((f32[40,8,1,128]{3,0,2,1:T(8,128)S(1)}, f32[40,8,1,128]{3,0,2,1:T(8,128)S(1)}, u32[]{:S(2)}, u32[]{:S(2)}) %collective-permute-start.9) | collective-permute-done | bytes 163872 | tf_op jit(solution)/shard_map/ppermute | solution.py:19
  128.2 0.2 pad_maximum_fusion
  128.4 2.5 %fusion.72 = (f32[40,8,18,1]{3,0,2,1:T(8,128)}, f32[40,8,18,1]{3,0,2,1:T(8,128)S(1)}) fusion(f32[40,8,18,128]{3,0,2,1:T(8,128)S(1)} %pad_maximum_fusion), kind=kLoop, calls=%fused_computation.115 | loop fusion | bytes 92160 | tf_op jit(solution)/shard_map/slice | solution.py:22
  130.9 2.9 %copy.114 = f32[40,8,18,1]{0,1,3,2:T(8,128)S(1)} copy(f32[40,8,18,1]{3,0,2,1:T(8,128)} %get-tuple-element.15) | data formatting | bytes 46080 | tf_op jit(solution)/shard_map/slice | solution.py:22
  133.8 2.0 collective-permute-start.10
  135.8 1.0 copy.116
  136.8 3.9 %collective-permute-start.11 = (f32[40,8,18,1]{0,1,3,2:T(8,128)S(1)}, f32[40,8,18,1]{0,1,3,2:T(8,128)S(1)}, u32[]{:S(2)}, u32[]{:S(2)}) collective-permute-start(f32[40,8,18,1]{0,1,3,2:T(8,128)S(1)} %copy.116), channel_id=1, source_target_pairs={{0,1},{1,2},{2,3},{4,5},{5,6},{6,7},{8,9},{9,10},{10,11},{12,13},{... | collective-permute-start | bytes 69128 | tf_op jit(solution)/shard_map/ppermute | solution.py:19
  140.7 3.3 %copy.118 = f32[8,32,16,128]{3,2,1,0:T(8,128)} copy(f32[8,32,16,128]{3,0,2,1:T(8,128)} %copy-done.2) | data formatting | bytes 4194304
  144.0 2.7 %copy.115 = f32[40,8,18,1]{3,0,2,1:T(8,128)} copy(f32[40,8,18,1]{0,1,3,2:T(8,128)S(1)} %collective-permute-done.10) | data formatting | bytes 46080 | tf_op jit(solution)/shard_map/ppermute | solution.py:22
  146.7 2.6 %copy.117 = f32[40,8,18,1]{3,0,2,1:T(8,128)} copy(f32[40,8,18,1]{0,1,3,2:T(8,128)S(1)} %collective-permute-done.11) | data formatting | bytes 46080 | tf_op jit(solution)/shard_map/ppermute | solution.py:19
  149.3 6.3 %fusion.9 = f32[40,8,16,128]{3,0,2,1:T(8,128)S(1)} fusion(f32[40,8,16,128]{3,0,2,1:T(8,128)S(1)} %copy-done.5, f32[40,8,18,1]{3,0,2,1:T(8,128)} %copy.117, f32[40,8,1,128]{3,0,2,1:T(8,128)S(1)} %collective-permute-done.8, f32[40,8,1,128]{3,0,2,1:T(8,128)S(1)} %collective-permute-done.9, f32[40,8,18,1]{3,0,2,1:T(8,128)} %copy.115, ...), kind=kOutput, calls=%fused_computation.16 | convolution fusion | flops 330301440 | bytes 8279040 | tf_op jit(solution)/shard_map/fg,gklt->fklt/dot_general | solution.py:54
  155.6 0.0 copy-start.10
  155.6 2.0 copy.119
  157.6 0.3 fusion.41
  157.9 40.5 %all_gather.3 = f32[256,128]{1,0:T(8,128)S(1)} all-gather(f32[16,128]{1,0:T(8,128)S(1)} %bitcast.79), channel_id=1, replica_groups=mesh['comp'=4,'lon'=16,'lat'=4] {'lon'}, dimensions={0}, use_global_device_ids=true | all-gather | bytes 139264 | tf_op jit(solution)/shard_map/all_gather | solution.py:131
  198.3 0.8 fusion.45
  (39 shorter events, 0.2 us)
Async XLA Ops:
  0.6 103.2 %copy-start = (f32[40,40]{1,0:T(8,128)S(1)}, f32[40,40]{1,0:T(8,128)}, u32[]{:S(2)}) copy-start(f32[40,40]{1,0:T(8,128)} %param.19) | copy-start | bytes 19204
  0.6 10.7 %copy-start.11 = (s32[1,16,1]{1,2,0:T(1,128)S(1)}, s32[1,16,1]{1,2,0:T(1,128)}, u32[]{:S(2)}) copy-start(s32[1,16,1]{1,2,0:T(1,128)} %param.15) | copy-start | bytes 196
  0.7 10.9 %copy-start.12 = (s32[1,16]{1,0:T(1,128)S(1)}, s32[1,16]{1,0:T(1,128)}, u32[]{:S(2)}) copy-start(s32[1,16]{1,0:T(1,128)} %param.16) | copy-start | bytes 196
  3.5 24.1 %copy-start.1 = (f32[8,32,16,128]{3,0,2,1:T(8,128)}, f32[8,32,16,128]{3,0,2,1:T(8,128)S(1)}, u32[]{:S(2)}) copy-start(f32[8,32,16,128]{3,0,2,1:T(8,128)S(1)} %copy.98) | copy-start | bytes 6291460
  3.5 30.4 %collective-permute-start = (f32[8,32,1,128]{3,0,2,1:T(8,128)S(1)}, f32[8,32,1,128]{3,0,2,1:T(8,128)S(1)}, u32[]{:S(2)}, u32[]{:S(2)}) collective-permute-start(f32[8,32,1,128]{3,0,2,1:T(8,128)S(1)} %get-tuple-element.26), channel_id=1, source_target_pairs={{4,0},{8,4},{12,8},{16,12},{20,16},{24,20},{28,24},{32,28},{36,32}... | collective-permute-start | bytes 393224 | tf_op jit(solution)/shard_map/ppermute | solution.py:22
  11.4 19.8 %collective-permute-start.1 = (f32[8,32,1,128]{3,0,2,1:T(8,128)S(1)}, f32[8,32,1,128]{3,0,2,1:T(8,128)S(1)}, u32[]{:S(2)}, u32[]{:S(2)}) collective-permute-start(f32[8,32,1,128]{3,0,2,1:T(8,128)S(1)} %get-tuple-element.25), channel_id=1, source_target_pairs={{0,4},{4,8},{8,12},{12,16},{16,20},{20,24},{24,28},{28,32},{32,36}... | collective-permute-start | bytes 393224 | tf_op jit(solution)/shard_map/ppermute | solution.py:19
  12.4 18.6 %all-to-all-start = ((f32[16,1,2]{2,1,0:T(1,128)}), f32[16,1,2]{2,1,0:T(1,128)S(1)}, u32[]{:S(2)}, u32[]{:S(2)}) async-start(f32[16,1,2]{2,1,0:T(1,128)} %bitcast.16), calls=%async_computation | async-start | bytes 16384 | tf_op jit(solution)/shard_map/all_to_all | solution.py:114
  18.8 8.9 %copy-start.7 = (f32[3,8,8]{2,1,0:T(8,128)S(1)}, f32[3,8,8]{2,1,0:T(8,128)}, u32[]{:S(2)}) copy-start(f32[3,8,8]{2,1,0:T(8,128)} %param.13) | copy-start | bytes 2308
  22.0 8.9 %copy-start.3 = (f32[40,8,16,128]{3,0,2,1:T(8,128)}, f32[40,8,16,128]{3,0,2,1:T(8,128)S(1)}, u32[]{:S(2)}) copy-start(f32[40,8,16,128]{3,0,2,1:T(8,128)S(1)} %copy.109) | copy-start | bytes 7864324
  22.1 8.9 %copy-start.8 = (f32[16,128]{1,0:T(8,128)S(1)}, f32[16,128]{1,0:T(8,128)}, u32[]{:S(2)}) copy-start(f32[16,128]{1,0:T(8,128)} %param.18) | copy-start | bytes 24580
  22.1 56.9 %collective-permute-start.5 = (f32[40,8,1,128]{3,0,2,1:T(8,128)S(1)}, f32[40,8,1,128]{3,0,2,1:T(8,128)S(1)}, u32[]{:S(2)}, u32[]{:S(2)}) collective-permute-start(f32[40,8,1,128]{3,0,2,1:T(8,128)S(1)} %get-tuple-element.22), channel_id=1, source_target_pairs={{0,4},{4,8},{8,12},{12,16},{16,20},{20,24},{24,28},{28,32},{32,36}... | collective-permute-start | bytes 491528 | tf_op jit(solution)/shard_map/ppermute | solution.py:19
  24.1 58.2 %collective-permute-start.4 = (f32[40,8,1,128]{3,0,2,1:T(8,128)S(1)}, f32[40,8,1,128]{3,0,2,1:T(8,128)}, u32[]{:S(2)}, u32[]{:S(2)}) collective-permute-start(f32[40,8,1,128]{3,0,2,1:T(8,128)S(1)} %get-tuple-element.21), channel_id=1, source_target_pairs={{4,0},{8,4},{12,8},{16,12},{20,16},{24,20},{28,24},{32,28},{36,32}... | collective-permute-start | bytes 491528 | tf_op jit(solution)/shard_map/ppermute | solution.py:22
  39.5 15.2 %collective-permute-start.2 = (f32[8,32,18,1]{1,0,3,2:T(8,128)S(1)}, f32[8,32,18,1]{1,0,3,2:T(8,128)}, u32[]{:S(2)}, u32[]{:S(2)}) collective-permute-start(f32[8,32,18,1]{1,0,3,2:T(8,128)S(1)} %copy.93), channel_id=1, source_target_pairs={{1,0},{2,1},{3,2},{5,4},{6,5},{7,6},{9,8},{10,9},{11,10},{13,12},{... | collective-permute-start | bytes 55304 | tf_op jit(solution)/shard_map/ppermute | solution.py:22
  45.3 12.6 %collective-permute-start.3 = (f32[8,32,18,1]{1,0,3,2:T(8,128)}, f32[8,32,18,1]{1,0,3,2:T(8,128)}, u32[]{:S(2)}, u32[]{:S(2)}) collective-permute-start(f32[8,32,18,1]{1,0,3,2:T(8,128)} %copy.95), channel_id=1, source_target_pairs={{0,1},{1,2},{2,3},{4,5},{5,6},{6,7},{8,9},{9,10},{10,11},{12,13},{... | collective-permute-start | bytes 55304 | tf_op jit(solution)/shard_map/ppermute | solution.py:19
  54.7 6.5 %copy-start.6 = (f32[32,16,128]{2,1,0:T(8,128)S(1)}, f32[32,16,128]{2,1,0:T(8,128)}, u32[]{:S(2)}) copy-start(f32[32,16,128]{2,1,0:T(8,128)} %param.12) | copy-start | bytes 786436
  61.2 12.6 %copy-start.9 = (f32[8]{0:T(128)S(1)}, f32[8]{0:T(128)}, u32[]{:S(2)}) copy-start(f32[8]{0:T(128)} %param.14) | copy-start | bytes 100
  72.5 1.4 copy-start.2
  74.9 23.5 %all-to-all-start.1 = ((f32[16,2,128]{2,1,0:T(2,128)}), f32[16,2,128]{2,1,0:T(2,128)S(1)}, u32[]{:S(2)}, u32[]{:S(2)}) async-start(f32[16,2,128]{2,1,0:T(2,128)} %bitcast.21), calls=%async_computation.1 | async-start | bytes 32768 | tf_op jit(solution)/shard_map/all_to_all | solution.py:113
  89.5 9.1 %collective-permute-start.6 = (f32[40,8,18,1]{0,1,3,2:T(8,128)S(1)}, f32[40,8,18,1]{0,1,3,2:T(8,128)S(1)}, u32[]{:S(2)}, u32[]{:S(2)}) collective-permute-start(f32[40,8,18,1]{0,1,3,2:T(8,128)S(1)} %copy.104), channel_id=1, source_target_pairs={{1,0},{2,1},{3,2},{5,4},{6,5},{7,6},{9,8},{10,9},{11,10},{13,12},{... | collective-permute-start | bytes 69128 | tf_op jit(solution)/shard_map/ppermute | solution.py:22
  94.4 6.9 %collective-permute-start.7 = (f32[40,8,18,1]{0,1,3,2:T(8,128)S(1)}, f32[40,8,18,1]{0,1,3,2:T(8,128)S(1)}, u32[]{:S(2)}, u32[]{:S(2)}) collective-permute-start(f32[40,8,18,1]{0,1,3,2:T(8,128)S(1)} %copy.106), channel_id=1, source_target_pairs={{0,1},{1,2},{2,3},{4,5},{5,6},{6,7},{8,9},{9,10},{10,11},{12,13},{... | collective-permute-start | bytes 69128 | tf_op jit(solution)/shard_map/ppermute | solution.py:19
  98.6 5.3 %copy-start.13 = (f32[40,8]{0,1:T(8,128)S(1)}, f32[40,8]{0,1:T(8,128)}, u32[]{:S(2)}) copy-start(f32[40,8]{0,1:T(8,128)} %param.20) | copy-start | bytes 3844
  114.5 13.9 %copy-start.4 = (f32[40,8,16,128]{3,0,2,1:T(8,128)}, f32[40,8,16,128]{3,0,2,1:T(8,128)S(1)}, u32[]{:S(2)}) copy-start(f32[40,8,16,128]{3,0,2,1:T(8,128)S(1)} %fusion.4) | copy-start | bytes 7864324
  114.5 8.2 %collective-permute-start.8 = (f32[40,8,1,128]{3,0,2,1:T(8,128)S(1)}, f32[40,8,1,128]{3,0,2,1:T(8,128)S(1)}, u32[]{:S(2)}, u32[]{:S(2)}) collective-permute-start(f32[40,8,1,128]{3,0,2,1:T(8,128)S(1)} %get-tuple-element.20), channel_id=1, source_target_pairs={{4,0},{8,4},{12,8},{16,12},{20,16},{24,20},{28,24},{32,28},{36,32}... | collective-permute-start | bytes 491528 | tf_op jit(solution)/shard_map/ppermute | solution.py:22
  119.9 8.3 %collective-permute-start.9 = (f32[40,8,1,128]{3,0,2,1:T(8,128)S(1)}, f32[40,8,1,128]{3,0,2,1:T(8,128)S(1)}, u32[]{:S(2)}, u32[]{:S(2)}) collective-permute-start(f32[40,8,1,128]{3,0,2,1:T(8,128)S(1)} %get-tuple-element.19), channel_id=1, source_target_pairs={{0,4},{4,8},{8,12},{12,16},{16,20},{20,24},{24,28},{28,32},{32,36}... | collective-permute-start | bytes 491528 | tf_op jit(solution)/shard_map/ppermute | solution.py:19
  133.8 10.2 %collective-permute-start.10 = (f32[40,8,18,1]{0,1,3,2:T(8,128)S(1)}, f32[40,8,18,1]{0,1,3,2:T(8,128)S(1)}, u32[]{:S(2)}, u32[]{:S(2)}) collective-permute-start(f32[40,8,18,1]{0,1,3,2:T(8,128)S(1)} %copy.114), channel_id=1, source_target_pairs={{1,0},{2,1},{3,2},{5,4},{6,5},{7,6},{9,8},{10,9},{11,10},{13,12},{... | collective-permute-start | bytes 69128 | tf_op jit(solution)/shard_map/ppermute | solution.py:22
  136.8 9.9 %collective-permute-start.11 = (f32[40,8,18,1]{0,1,3,2:T(8,128)S(1)}, f32[40,8,18,1]{0,1,3,2:T(8,128)S(1)}, u32[]{:S(2)}, u32[]{:S(2)}) collective-permute-start(f32[40,8,18,1]{0,1,3,2:T(8,128)S(1)} %copy.116), channel_id=1, source_target_pairs={{0,1},{1,2},{2,3},{4,5},{5,6},{6,7},{8,9},{9,10},{10,11},{12,13},{... | collective-permute-start | bytes 69128 | tf_op jit(solution)/shard_map/ppermute | solution.py:19
  144.0 5.3 %copy-start.5 = (f32[40,8,16,128]{3,0,2,1:T(8,128)S(1)}, f32[40,8,16,128]{3,0,2,1:T(8,128)}, u32[]{:S(2)}) copy-start(f32[40,8,16,128]{3,0,2,1:T(8,128)} %copy-done.4) | copy-start | bytes 7864324
  155.6 2.0 copy-start.10
where the time goes:
time: 200 us; the launch traced here: 199 us
  local copies, waits for them, and re-layouts  62 us (31%)
  starting transfers between devices  47.5 us (24%)
  blocking collectives  40.5 us (20%)
  matrix products  39.4 us (20%)
  waiting for transfers between devices  8.38 us (4%)
    all_gather x1, blocking collectives, shards(): gathered = lax.all_gather(potential, 'lon', axis=0, tiled=True)  40.5 us
    ppermute x6, starting transfers between devices, with_halo(): lax.ppermute(lax.slice_in_dim(block, 0, width, axis=dim), axis, backward)  23.3 us
    unnamed x36, local copies, waits for them, and re-layouts  18.9 us
    dot_general x2, matrix products, slab_update(): jnp.einsum('fg,gklt->fklt', chemistry, fields, precision=lax.Precision.HI...  16.9 us
    slice x6, local copies, waits for them, and re-layouts, with_halo(): lax.slice_in_dim(block, 0, width, axis=dim)  14.3 us
    ppermute x6, starting transfers between devices, with_halo(): lax.ppermute(lax.slice_in_dim(block, block.shape[dim] - width, None, axis...  13.8 us
    dot_general x1, matrix products, shell_update(): jnp.einsum('uv,vrpt->urpt', jacobians[2], d_polar, precision=lax.Precisio...  11.2 us
    slice x6, local copies, waits for them, and re-layouts, with_halo(): lax.slice_in_dim(block, block.shape[dim] - width, None, axis=dim)  10.1 us
  transfers between devices with their start and end apart: 14, of which 2 were waited for; matrix products, arithmetic and copies ran while one was open for 33% of the time, Pallas kernels for 0%

commit v1 on v0

v1 whole, which is shorter than its diff:
```python
import functools

import jax
import jax.numpy as jnp
from jax import lax
from jax.experimental import pallas as pl
from jax.experimental.pallas import tpu as pltpu
from jax.sharding import PartitionSpec as P

NV = 8
NF = 40
RAD = 32
PH = 16
TH = 128
LEV = 8
LON = 16
BLOCKS = 16
KF = LEV * NF
SHELL_ROWS = NV * RAD
F32 = jnp.float32
BF16 = jnp.bfloat16
VMEM = pl.BlockSpec(memory_space=pltpu.VMEM)
SMEM = pl.BlockSpec(memory_space=pltpu.SMEM)
PARAMS = pltpu.CompilerParams(vmem_limit_bytes=48 * 1024 * 1024)


def odd_lon():
    return lax.rem(lax.axis_index("lon"), 2) == 1


def odd_lat():
    return lax.rem(lax.axis_index("lat"), 2) == 1


def lanes(rows):
    return lax.broadcasted_iota(jnp.int32, (rows, TH), 1)


def slot_of(rows):
    return lax.rem(lanes(rows) + 1, TH) // 2


def edge_of(rows):
    lane = lanes(rows)
    return (lane == 0) | (lane == TH - 1)


def spin(x, shift):
    shift = shift % TH
    return x if shift == 0 else pltpu.roll(x, shift, 1)


def merged(first, second):
    odd = odd_lat()
    left = jnp.where(odd, first, second)
    right = jnp.where(odd, second, first)
    even_lane = lax.rem(lanes(left.shape[0]), 2) == 0
    return jnp.where(even_lane, spin(left, 1), spin(right, -1))


def pack_kernel(slab_ref, shell_ref, s2_ref, lon_a_ref, lon_b_ref, lat_ref):
    slot = slot_of(NF)
    for half in range(2):
        acc = jnp.zeros((NF, TH), F32)
        for k in range(half * 4, half * 4 + 4):
            for l in range(LON):
                x = slab_ref[pl.ds(k * LON + l, NF, stride=LEV * LON), :]
                s2_ref[l, k * NF : (k + 1) * NF, :] = x
                j = l + LON * (k % 4)
                acc = jnp.where(slot == j, spin(x, 2 * j), acc)
        lat_ref[half * NF : (half + 1) * NF, :] = acc
    slot = slot_of(PH)
    for v in range(NV):
        acc = jnp.zeros((PH, TH), F32)
        for r in range(RAD):
            x = shell_ref[(v * RAD + r) * PH : (v * RAD + r + 1) * PH, :]
            acc = jnp.where(slot == r, spin(x, 2 * r), acc)
        lat_ref[2 * NF + v * PH : 2 * NF + (v + 1) * PH, :] = acc
    odd = odd_lon()
    low, high = s2_ref[0], s2_ref[LON - 1]
    lon_a_ref[0:KF, :] = jnp.where(odd, low, high)
    lon_b_ref[0:KF, :] = jnp.where(odd, high, low)
    for v in range(NV):
        low = shell_ref[pl.ds(v * RAD * PH, RAD, stride=PH), :]
        high = shell_ref[pl.ds(v * RAD * PH + PH - 1, RAD, stride=PH), :]
        at = KF + v * RAD
        lon_a_ref[at : at + RAD, :] = jnp.where(odd, low, high)
        lon_b_ref[at : at + RAD, :] = jnp.where(odd, high, low)


def mixing_matrix(chem):
    rows = (lax.broadcasted_iota(jnp.int32, (2 * NF, NF), 0) % NF) == lax.broadcasted_iota(
        jnp.int32, (2 * NF, NF), 1
    )
    cols = lax.broadcasted_iota(jnp.int32, (NF, 6 * NF), 0) == (
        lax.broadcasted_iota(jnp.int32, (NF, 6 * NF), 1) % NF
    )
    wide = jnp.dot(
        jnp.dot(
            rows.astype(F32), chem, precision=lax.Precision.HIGHEST, preferred_element_type=F32
        ),
        cols.astype(F32),
        precision=lax.Precision.HIGHEST,
        preferred_element_type=F32,
    )
    i = lax.broadcasted_iota(jnp.int32, (2 * NF, 6 * NF), 0)
    j = lax.broadcasted_iota(jnp.int32, (2 * NF, 6 * NF), 1)
    wide = jnp.where((i // NF) == ((j // NF) % 2), 0.1 * wide, 0.0)
    high = wide.astype(BF16).astype(F32)
    return jnp.where(j < 4 * NF, high, wide - high).astype(BF16)


def step_kernel(x_ref, cond_ref, chem_ref, o_ref):
    lhs = mixing_matrix(chem_ref[...])
    lane = lanes(2 * NF)
    zero = jnp.zeros((NF, TH), F32)

    def body(g, carry):
        for kp in range(LEV // 2):
            rows = slice(2 * NF * kp, 2 * NF * (kp + 1))
            xs = [x_ref[2 * g, rows, :], x_ref[2 * g + 1, rows, :]]
            below = x_ref[jnp.maximum(2 * g - 1, 0), rows, :] * jnp.where(g > 0, 1.0, 0.0)
            above = x_ref[jnp.minimum(2 * g + 2, LON - 1), rows, :] * jnp.where(
                g < LON // 2 - 1, 1.0, 0.0
            )
            near = [below + xs[1], xs[0] + above]
            both = jnp.concatenate(xs, axis=1)
            high = both.astype(BF16)
            low = (both - high.astype(F32)).astype(BF16)
            mixed = jnp.dot(
                lhs, jnp.concatenate([high, low, high], axis=0), preferred_element_type=F32
            )
            for i in range(2):
                x = xs[i]
                l = 2 * g + i
                if kp == 0:
                    down = jnp.concatenate([zero, x[:NF]], axis=0)
                else:
                    down = x_ref[l, 2 * NF * kp - NF : 2 * NF * kp + NF, :]
                if kp == LEV // 2 - 1:
                    up = jnp.concatenate([x[NF:], zero], axis=0)
                else:
                    up = x_ref[l, 2 * NF * kp + NF : 2 * NF * kp + 3 * NF, :]
                sides = jnp.where(lane == 0, 0.0, spin(x, 1)) + jnp.where(
                    lane == TH - 1, 0.0, spin(x, -1)
                )
                c = 0.1 * cond_ref[pl.ds(l, 1), :]
                o_ref[l, rows, :] = (
                    x * (0.8 - 4.0 * c)
                    + c * (near[i] + sides)
                    + 0.1 * (up + down)
                    + mixed[:, i * TH : (i + 1) * TH]
                )
        return carry

    lax.fori_loop(0, LON // 2, body, 0)


def shell_kernel(x_ref, res_ref, jac_ref, o_ref):
    lane = lanes(PH)
    row = lax.broadcasted_iota(jnp.int32, (PH, TH), 0)

    def body(r, carry):
        keep_low = jnp.where(r > 0, 1.0, 0.0)
        keep_high = jnp.where(r < RAD - 1, 1.0, 0.0)
        flux = [None] * NV
        for v in range(NV):
            x = x_ref[v, r]
            below = x_ref[v, jnp.maximum(r - 1, 0)] * keep_low
            above = x_ref[v, jnp.minimum(r + 1, RAD - 1)] * keep_high
            west = jnp.where(row == 0, 0.0, pltpu.roll(x, 1, 0))
            east = jnp.where(row == PH - 1, 0.0, pltpu.roll(x, PH - 1, 0))
            south = jnp.where(lane == 0, 0.0, spin(x, 1))
            north = jnp.where(lane == TH - 1, 0.0, spin(x, -1))
            around = (below + above) + (west + east) + (south + north)
            o_ref[v, r] = x + (0.2 * res_ref[r]) * (around - 6.0 * x)
            parts = (above - below, east - west, north - south)
            for u in range(NV):
                for d in range(3):
                    term = jac_ref[d, u, v] * parts[d]
                    flux[u] = term if flux[u] is None else flux[u] + term
        for u in range(NV):
            o_ref[u, r] = o_ref[u, r] - 0.1 * flux[u]
        return carry

    lax.fori_loop(0, RAD, body, 0)


def rank_rows(fp_ref, count_ref, visit):
    for b in range(BLOCKS):
        count_ref[b] = 0
    for p in range(PH):
        block = fp_ref[0, p, 0]
        rank = count_ref[block]
        count_ref[block] = rank + 1
        visit(p, block, rank)


def current_kernel(
    part_ref, res_ref, jac_ref, weight_ref, fp_ref, row_ref, lon_a_ref, lon_b_ref, lat_a_ref, lat_b_ref,
    send_ref, cur_ref, count_ref,
):
    w = [weight_ref[v] for v in range(NV)]
    wj = [[sum(w[u] * jac_ref[d, u, v] for u in range(NV)) for v in range(NV)] for d in (1, 2)]
    res = 0.2 * res_ref[0]
    odd = odd_lon()
    cur = sum(w[v] * part_ref[v, 0] for v in range(NV))
    rows_a = [lon_a_ref[KF + v * RAD : KF + v * RAD + 1, :] for v in range(NV)]
    rows_b = [lon_b_ref[KF + v * RAD : KF + v * RAD + 1, :] for v in range(NV)]
    low = [jnp.where(odd, a, b) for a, b in zip(rows_a, rows_b)]
    high = [jnp.where(odd, b, a) for a, b in zip(rows_a, rows_b)]
    row = lax.broadcasted_iota(jnp.int32, (PH, TH), 0)
    lane = lanes(PH)
    plain = sum(w[v] * low[v] for v in range(NV))
    turned = 0.1 * sum(wj[0][v] * low[v] for v in range(NV))
    cur = cur + jnp.where(row == 0, res * plain + turned, 0.0)
    plain = sum(w[v] * high[v] for v in range(NV))
    turned = 0.1 * sum(wj[0][v] * high[v] for v in range(NV))
    cur = cur + jnp.where(row == PH - 1, res * plain - turned, 0.0)
    side = [
        merged(
            lat_a_ref[2 * NF + v * PH : 2 * NF + (v + 1) * PH, :],
            lat_b_ref[2 * NF + v * PH : 2 * NF + (v + 1) * PH, :],
        )
        for v in range(NV)
    ]
    plain = sum(w[v] * side[v] for v in range(NV))
    turned = 0.1 * sum(wj[1][v] * side[v] for v in range(NV))
    cur = cur + jnp.where(lane == 0, res * plain + turned, 0.0)
    cur = cur + jnp.where(lane == TH - 1, res * plain - turned, 0.0)
    cur_ref[...] = cur
    send_ref[...] = jnp.zeros(send_ref.shape, F32)

    def visit(p, block, rank):
        send_ref[block, pl.ds(rank, 1), :] = cur_ref[p : p + 1, :]
        send_ref[block, pl.ds(2 + rank, 1), :] = jnp.full((1, TH), row_ref[0, p], jnp.int32).astype(F32)

    rank_rows(fp_ref, count_ref, visit)


def slab_edges(lat_a, lat_b):
    return [
        merged(lat_a[h * NF : (h + 1) * NF, :], lat_b[h * NF : (h + 1) * NF, :]) for h in range(2)
    ]


def levels_of(coupling_ref):
    return [
        jnp.broadcast_to(0.1 * coupling_ref[:, k : k + 1], (NF, TH)) for k in range(LEV)
    ]


def gather_source(got_ref):
    row = lax.broadcasted_iota(jnp.int32, (LON, TH), 0).astype(F32)
    source = jnp.zeros((LON, TH), F32)
    for b in range(BLOCKS):
        for s in range(2):
            source = source + jnp.where(
                row == got_ref[b, 2 + s : 3 + s, :], got_ref[b, s : s + 1, :], 0.0
            )
    return source


def fixed_tile(x_ref, l, k, c, edge, sides, levels, source, ends):
    rows = slice(k * NF, (k + 1) * NF)
    j = l + LON * (k % 4)
    h = jnp.where(edge, spin(sides[k // 4], -2 * j), 0.0)
    if l == 0:
        h = h + ends[0][rows]
    if l == LON - 1:
        h = h + ends[1][rows]
    return x_ref[l, rows, :] + c * h + levels[k] * source


def middle_kernel(
    x_ref, lon_a_ref, lon_b_ref, lat_a_ref, lat_b_ref, cond_ref, coupling_ref, got_ref,
    o_ref, source_ref, next_a_ref, next_b_ref, lat_ref,
):
    source = gather_source(got_ref)
    source_ref[...] = source
    odd = odd_lon()
    ends = [
        jnp.where(odd, lon_a_ref[0:KF, :], lon_b_ref[0:KF, :]),
        jnp.where(odd, lon_b_ref[0:KF, :], lon_a_ref[0:KF, :]),
    ]
    sides = slab_edges(lat_a_ref, lat_b_ref)
    levels = levels_of(coupling_ref)
    edge = edge_of(NF)
    slot = slot_of(NF)
    for half in range(2):
        acc = jnp.zeros((NF, TH), F32)
        for l in range(LON):
            c = 0.1 * cond_ref[l : l + 1, :]
            for k in range(half * 4, half * 4 + 4):
                x = fixed_tile(x_ref, l, k, c, edge, sides, levels, source_ref[l : l + 1, :], ends)
                o_ref[l, k * NF : (k + 1) * NF, :] = x
                j = l + LON * (k % 4)
                acc = jnp.where(slot == j, spin(x, 2 * j), acc)
        lat_ref[half * NF : (half + 1) * NF, :] = acc
    low, high = o_ref[0], o_ref[LON - 1]
    next_a_ref[...] = jnp.where(odd, low, high)
    next_b_ref[...] = jnp.where(odd, high, low)


def ends_of(lon_a_ref, lon_b_ref, rows):
    odd = odd_lon()
    a, b = lon_a_ref[0:rows, :], lon_b_ref[0:rows, :]
    return [jnp.where(odd, a, b), jnp.where(odd, b, a)]


def potential_kernel(
    x_ref, lon_a_ref, lon_b_ref, lat_a_ref, lat_b_ref, cond_ref, coupling_ref, weight_ref, source_ref, got_ref,
    send_ref, pot_ref,
):
    ends = ends_of(lon_a_ref, lon_b_ref, NF)
    sides = [merged(lat_a_ref[0:NF, :], lat_b_ref[0:NF, :])]
    levels = [jnp.broadcast_to(0.1 * coupling_ref[:, 0:1], (NF, TH))]
    edge = edge_of(NF)
    diagonal = lax.broadcasted_iota(jnp.int32, (NF, NF), 0) == lax.broadcasted_iota(
        jnp.int32, (NF, NF), 1
    )
    weight = jnp.sum(
        jnp.where(diagonal, jnp.broadcast_to(weight_ref[...], (NF, NF)), 0.0), axis=1, keepdims=True
    )
    weight = jnp.broadcast_to(weight, (NF, TH))
    for l in range(LON):
        c = 0.1 * cond_ref[l : l + 1, :]
        x = fixed_tile(x_ref, l, 0, c, edge, sides, levels, source_ref[l : l + 1, :], ends)
        pot_ref[l : l + 1, :] = jnp.sum(weight * x, axis=0, keepdims=True)
    potential = pot_ref[...]
    row = lax.broadcasted_iota(jnp.int32, (LON, TH), 0).astype(F32)
    for b in range(BLOCKS):
        for s in range(2):
            send_ref[b, s : s + 1, :] = jnp.sum(
                jnp.where(row == got_ref[b, 2 + s : 3 + s, :], potential, 0.0), axis=0, keepdims=True
            )
        send_ref[b, 2:8, :] = jnp.zeros((6, TH), F32)


def finish_kernel(
    x_ref, lon_a_ref, lon_b_ref, lat_a_ref, lat_b_ref, cond_ref, coupling_ref, source_ref, o_ref
):
    ends = ends_of(lon_a_ref, lon_b_ref, KF)
    sides = slab_edges(lat_a_ref, lat_b_ref)
    levels = levels_of(coupling_ref)
    edge = edge_of(NF)
    for l in range(LON):
        c = 0.1 * cond_ref[l : l + 1, :]
        for k in range(LEV):
            o_ref[pl.ds(k * LON + l, NF, stride=LEV * LON), :] = fixed_tile(
                x_ref, l, k, c, edge, sides, levels, source_ref[l : l + 1, :], ends
            )


def shell_edge_kernel(
    part_ref, res_ref, jac_ref, lon_a_ref, lon_b_ref, lat_a_ref, lat_b_ref, o_ref, corr_ref
):
    odd = odd_lon()
    slot = slot_of(PH)
    edge = edge_of(PH)
    even_lane = lax.rem(lanes(PH), 2) == 0
    packed = jnp.zeros((PH, TH), F32)
    for r in range(RAD):
        packed = jnp.where(slot == r, spin(res_ref[r * PH : (r + 1) * PH, :], 2 * r), packed)
    side = [
        merged(
            lat_a_ref[2 * NF + v * PH : 2 * NF + (v + 1) * PH, :],
            lat_b_ref[2 * NF + v * PH : 2 * NF + (v + 1) * PH, :],
        )
        for v in range(NV)
    ]
    for u in range(NV):
        turned = 0.1 * sum(jac_ref[2, u, v] * side[v] for v in range(NV))
        corr = 0.2 * packed * side[u] + jnp.where(even_lane, turned, -turned)
        for r in range(RAD):
            rows = slice((u * RAD + r) * PH, (u * RAD + r + 1) * PH)
            o_ref[rows, :] = part_ref[rows, :] + jnp.where(edge, spin(corr, -2 * r), 0.0)
    for last in range(2):
        near = 0.2 * res_ref[pl.ds(last * (PH - 1), RAD, stride=PH), :]
        rows = []
        for v in range(NV):
            at = KF + v * RAD
            a, b = lon_a_ref[at : at + RAD, :], lon_b_ref[at : at + RAD, :]
            rows.append(jnp.where(odd, b, a) if last else jnp.where(odd, a, b))
        for u in range(NV):
            turned = 0.1 * sum(jac_ref[1, u, v] * rows[v] for v in range(NV))
            where = pl.ds(u * RAD * PH + last * (PH - 1), RAD, stride=PH)
            added = near * rows[u] + (-turned if last else turned)
            o_ref[where, :] = o_ref[where, :] + added


def pick_kernel(got_ref, fp_ref, o_ref, count_ref):
    def visit(p, block, rank):
        o_ref[p : p + 1, :] = got_ref[block, pl.ds(rank, 1), :]

    rank_rows(fp_ref, count_ref, visit)


def call(kernel, name, ins, outs, specs=None, scratch=(), flops=0, moved=0):
    shapes = [jax.ShapeDtypeStruct(s, F32) for s in outs]
    single = len(shapes) == 1
    return pl.pallas_call(
        kernel,
        out_shape=shapes[0] if single else shapes,
        in_specs=specs or [VMEM] * len(ins),
        out_specs=VMEM if single else [VMEM] * len(shapes),
        scratch_shapes=list(scratch),
        compiler_params=PARAMS,
        cost_estimate=pl.CostEstimate(flops=flops, bytes_accessed=moved, transcendentals=0),
        name=name,
    )(*ins)


def swaps(count, first, periodic):
    pairs = []
    for i in range(first, count, 2):
        if i + 1 < count or periodic:
            j = (i + 1) % count
            pairs += [(i, j), (j, i)]
    return pairs


def exchange(lon_a, lon_b, lat):
    ring = ("comp", "lon")
    size = lax.axis_size("comp") * lax.axis_size("lon")
    width = lax.axis_size("lat")
    got_lat = [lax.ppermute(lat, "lat", swaps(width, first, False)) for first in (0, 1)]
    got_lon = [
        lax.ppermute(block, ring, swaps(size, first, True))
        for first, block in enumerate((lon_a, lon_b))
    ]
    return (*got_lon, *got_lat)


def shards(
    shell,
    resistivity,
    jacobians,
    current_weights,
    footpoint,
    footrow,
    slab,
    conductance,
    chemistry,
    coupling,
    potential_weights,
):
    slab_rows = slab.reshape(NF * LEV * LON, TH)
    shell_rows = shell.reshape(SHELL_ROWS * PH, TH)
    s2, lon_a, lon_b, lat = call(
        pack_kernel,
        "pack",
        (slab_rows, shell_rows),
        [(LON, KF, TH), (KF + SHELL_ROWS, TH), (KF + SHELL_ROWS, TH), (2 * NF + NV * PH, TH)],
        moved=8_000_000,
    )
    halos = exchange(lon_a, lon_b, lat)
    part = call(
        shell_kernel,
        "shell",
        (shell, resistivity, jacobians),
        [shell.shape],
        specs=[VMEM, VMEM, SMEM],
        flops=30_000_000,
        moved=5_000_000,
    )
    middle = call(
        step_kernel, "step", (s2, conductance, chemistry), [(LON, KF, TH)], flops=60_000_000, moved=5_000_000
    )
    first = pl.BlockSpec((NV, 1, PH, TH), lambda i: (0, 0, 0, 0))
    send = pl.pallas_call(
        current_kernel,
        grid=(1,),
        out_shape=jax.ShapeDtypeStruct((BLOCKS, 8, TH), F32),
        in_specs=[first, pl.BlockSpec((1, PH, TH), lambda i: (0, 0, 0)), SMEM, SMEM, SMEM, SMEM]
        + [VMEM] * 4,
        out_specs=VMEM,
        scratch_shapes=[pltpu.VMEM((PH, TH), F32), pltpu.SMEM((BLOCKS,), jnp.int32)],
        compiler_params=PARAMS,
        name="current",
    )(part, resistivity, jacobians, current_weights, footpoint, footrow, *halos)
    got = lax.all_to_all(send, "lon", split_axis=0, concat_axis=0, tiled=True)
    middle, source, lon_a, lon_b, lat = call(
        middle_kernel,
        "middle",
        (middle, *halos, conductance, coupling, got),
        [(LON, KF, TH), (LON, TH), (KF, TH), (KF, TH), (2 * NF, TH)],
        moved=6_000_000,
    )
    ends = exchange(lon_a, lon_b, lat)
    shell_next = call(
        shell_edge_kernel,
        "shell_edge",
        (part.reshape(SHELL_ROWS * PH, TH), resistivity.reshape(RAD * PH, TH), jacobians, *halos),
        [(SHELL_ROWS * PH, TH)],
        specs=[VMEM, VMEM, SMEM] + [VMEM] * 4,
        scratch=[pltpu.VMEM((PH, TH), F32)],
        moved=4_000_000,
    ).reshape(shell.shape)
    last = call(
        step_kernel, "step", (middle, conductance, chemistry), [(LON, KF, TH)], flops=60_000_000, moved=5_000_000
    )
    asked = call(
        potential_kernel,
        "potential",
        (last, *ends, conductance, coupling, potential_weights.reshape(1, NF), source, got),
        [(BLOCKS, 8, TH)],
        scratch=[pltpu.VMEM((LON, TH), F32)],
    )
    back = lax.all_to_all(asked, "lon", split_axis=0, concat_axis=0, tiled=True)
    slab_next = call(
        finish_kernel,
        "finish",
        (last, *ends, conductance, coupling, source),
        [(NF * LEV * LON, TH)],
        moved=5_000_000,
    ).reshape(slab.shape)
    boundary = call(
        pick_kernel,
        "pick",
        (back, footpoint),
        [(PH, TH)],
        specs=[VMEM, SMEM],
        scratch=[pltpu.SMEM((BLOCKS,), jnp.int32)],
    )
    return shell_next, slab_next, boundary


def solution(mesh):
    ring = ("comp", "lon")
    placed = (
        P(None, None, ring, "lat"),
        P(None, ring, "lat"),
        P(),
        P(),
        P("lat", ring, None),
        P("lat", ring),
        P(None, None, ring, "lat"),
        P(ring, "lat"),
        P(),
        P(),
        P(),
    )
    return jax.shard_map(
        shards,
        mesh=mesh,
        in_specs=placed,
        out_specs=(P(None, None, ring, "lat"), P(None, None, ring, "lat"), P(ring, "lat")),
        check_vma=False,
    )
```

time: 200 us -> 89.7 us (0.45)
  the two profiles are of different devices: /device:TPU:4 before, /device:TPU:1 now
where the time goes in v1:
time: 89.7 us; the launch traced here: 89.1 us
  Pallas kernels  39.3 us (44%)
  starting transfers between devices  33.2 us (37%)
  local copies, waits for them, and re-layouts  14.9 us (17%)
  between operations  0.94 us (1%)
    pallas_call x9, Pallas kernels, call(): pl.pallas_call(kernel, out_shape=shapes[0] if single else shapes, in_spec...  37.9 us
    unnamed x64, local copies, waits for them, and re-layouts  14.9 us
    ppermute x4, starting transfers between devices, exchange(): lax.ppermute(block, ring, swaps(size, first, True))  14.6 us
    ppermute x4, starting transfers between devices, exchange(): lax.ppermute(lat, 'lat', swaps(width, first, False))  8.14 us
    all_to_all x1, starting transfers between devices, shards(): back = lax.all_to_all(asked, 'lon', split_axis=0, concat_axis=0, tiled=True)  5.68 us
    all_to_all x1, starting transfers between devices, shards(): got = lax.all_to_all(send, 'lon', split_axis=0, concat_axis=0, tiled=True)  4.8 us
  transfers between devices with their start and end apart: 10, of which 1 were waited for; matrix products, arithmetic and copies ran while one was open for 2% of the time, Pallas kernels for 23%

profile of v1, /device:TPU:1, one launch (start us, length us, event | category | flops | bytes accessed | tf_op | source)
XLA Modules:
  0.0 89.1 jit_solution(10004908800511240091)
XLA Ops:
  0.6 0.0 copy-start.30
  0.6 0.0 copy-start.3
  0.7 1.6 %copy-done.3 = f32[8,32,16,128]{3,2,1,0:T(8,128)S(1)} copy-done((f32[8,32,16,128]{3,2,1,0:T(8,128)S(1)}, f32[8,32,16,128]{3,2,1,0:T(8,128)}, u32[]{:S(2)}) %copy-start.3) | copy-done | bytes 2097176
  2.2 5.0 %pack.1 = (f32[16,320,128]{2,1,0:T(8,128)S(1)}, f32[576,128]{1,0:T(8,128)}, f32[576,128]{1,0:T(8,128)}, f32[208,128]{1,0:T(8,128)}) custom-call(f32[5120,128]{1,0:T(8,128)} %bitcast.11, f32[4096,128]{1,0:T(8,128)S(1)} %bitcast.8), custom_call_target="tpu_custom_call" | custom-call | bytes 8000000 | tf_op jit(solution)/shard_map/pack/pallas_call | solution.py:402
  7.3 1.5 %copy-done.5 = f32[16,320,128]{2,1,0:T(8,128)} copy-done((f32[16,320,128]{2,1,0:T(8,128)}, f32[16,320,128]{2,1,0:T(8,128)S(1)}, u32[]{:S(2)}) %copy-start.5) | copy-done | bytes 2621464
  8.8 2.5 %collective-permute-start = (f32[576,128]{1,0:T(8,128)}, f32[576,128]{1,0:T(8,128)S(1)}, u32[]{:S(2)}, u32[]{:S(2)}) collective-permute-start(f32[576,128]{1,0:T(8,128)} %get-tuple-element.12), channel_id=1, source_target_pairs={{0,4},{4,0},{8,12},{12,8},{16,20},{20,16},{24,28},{28,24},{32,36},... | collective-permute-start | bytes 884744 | tf_op jit(solution)/shard_map/ppermute | solution.py:429
  11.2 5.8 %collective-permute-start.1 = (f32[576,128]{1,0:T(8,128)}, f32[576,128]{1,0:T(8,128)S(1)}, u32[]{:S(2)}, u32[]{:S(2)}) collective-permute-start(f32[576,128]{1,0:T(8,128)} %get-tuple-element.13), channel_id=1, source_target_pairs={{4,8},{8,4},{12,16},{16,12},{20,24},{24,20},{28,32},{32,28},{36,40... | collective-permute-start | bytes 884744 | tf_op jit(solution)/shard_map/ppermute | solution.py:429
  17.1 1.3 %collective-permute-start.3 = (f32[208,128]{1,0:T(8,128)}, f32[208,128]{1,0:T(8,128)}, u32[]{:S(2)}, u32[]{:S(2)}) collective-permute-start(f32[208,128]{1,0:T(8,128)} %get-tuple-element.14), channel_id=1, source_target_pairs={{1,2},{2,1},{5,6},{6,5},{9,10},{10,9},{13,14},{14,13},{17,18},{18,... | collective-permute-start | bytes 319496 | tf_op jit(solution)/shard_map/ppermute | solution.py:427
  18.4 3.1 %collective-permute-start.2 = (f32[208,128]{1,0:T(8,128)}, f32[208,128]{1,0:T(8,128)}, u32[]{:S(2)}, u32[]{:S(2)}) collective-permute-start(f32[208,128]{1,0:T(8,128)} %get-tuple-element.14), channel_id=1, source_target_pairs={{0,1},{1,0},{2,3},{3,2},{4,5},{5,4},{6,7},{7,6},{8,9},{9,8},{10,11... | collective-permute-start | bytes 319496 | tf_op jit(solution)/shard_map/ppermute | solution.py:427
  21.5 0.0 copy-done.30
  21.5 0.1 copy.14.fp_ref
  21.6 0.0 copy-done.4
  21.6 0.0 copy-done.7
  21.6 0.0 copy-done.21
  21.6 7.6 %shell.1.part_ref = f32[8,32,16,128]{3,2,1,0:T(8,128)S(1)} custom-call(f32[8,32,16,128]{3,2,1,0:T(8,128)S(1)} %copy-done.4, f32[32,16,128]{2,1,0:T(8,128)S(1)} %copy-done.7, f32[3,8,8]{2,1,0:T(8,128)S(1)} %copy-done.21), custom_call_target="tpu_custom_call" | custom-call | flops 30000000 | bytes 5000000 | tf_op jit(solution)/shard_map/shell/pallas_call | solution.py:402
  29.2 0.0 copy-start.6
  29.2 0.0 copy-start.16
  29.2 0.0 collective-permute-done.3.lat_b_ref
  29.2 0.0 collective-permute-done.2.lat_a_ref
  29.2 0.0 collective-permute-done.lon_a_ref
  29.3 0.0 collective-permute-done.1.lon_b_ref
  29.3 0.0 copy-done.27
  29.3 0.0 copy-done.28
  29.3 1.3 %current.1 = f32[16,8,128]{2,1,0:T(8,128)S(1)} custom-call(f32[8,32,16,128]{3,2,1,0:T(8,128)S(1)} %shell.1.part_ref, f32[32,16,128]{2,1,0:T(8,128)S(1)} %copy-done.7, f32[3,8,8]{2,1,0:T(8,128)S(1)} %copy-done.21, f32[8]{0:T(128)S(1)} %copy-done.27, s32[1,16,1]{2,1,0:T(8,128)S(1)} %copy.14.fp_ref, s32[1,16]{1,0:T(1,128)S(1)} %copy-done.28, ...), custom_call_target="tpu_custom_call" | custom-call | tf_op jit(solution)/shard_map/current/pallas_call | solution.py:471
  30.6 0.0 copy-start
  30.6 1.3 %copy-done = f32[8,32,16,128]{3,2,1,0:T(8,128)} copy-done((f32[8,32,16,128]{3,2,1,0:T(8,128)}, f32[8,32,16,128]{3,2,1,0:T(8,128)S(1)}, u32[]{:S(2)}) %copy-start) | copy-done | bytes 2097176
  31.9 0.6 copy-done.15
  32.6 4.8 %all-to-all-start = ((f32[16,8,128]{2,1,0:T(8,128)}), f32[16,8,128]{2,1,0:T(8,128)S(1)}, u32[]{:S(2)}, u32[]{:S(2)}) async-start(f32[16,8,128]{2,1,0:T(8,128)} %copy-done.15), calls=%async_computation | async-start | bytes 131072 | tf_op jit(solution)/shard_map/all_to_all | solution.py:482
  37.4 1.4 %copy.15.coupling_ref = f32[40,8]{1,0:T(8,128)} copy(f32[40,8]{0,1:T(8,128)} %param.20) | data formatting | bytes 2560 | tf_op args[9]
  38.7 0.0 copy-done.6
  38.7 0.0 copy-done.16
  38.7 0.7 copy-done.23
  39.5 2.7 %step.2.x_ref = f32[16,320,128]{2,1,0:T(8,128)S(1)} custom-call(f32[16,320,128]{2,1,0:T(8,128)S(1)} %copy-done.6, f32[16,128]{1,0:T(8,128)S(1)} %copy-done.16, f32[40,40]{1,0:T(8,128)S(1)} %copy-done.23), custom_call_target="tpu_custom_call" | custom-call | flops 60000000 | bytes 5000000 | tf_op jit(solution)/shard_map/step/pallas_call | solution.py:402
  42.2 0.0 copy-start.2
  42.2 1.5 %copy-done.2 = f32[16,320,128]{2,1,0:T(8,128)} copy-done((f32[16,320,128]{2,1,0:T(8,128)}, f32[16,320,128]{2,1,0:T(8,128)S(1)}, u32[]{:S(2)}) %copy-start.2) | copy-done | bytes 2621464
  43.7 0.7 all-to-all-done.got_ref
  44.4 0.7 copy-done.12
  45.1 10.7 %middle.1 = (f32[16,320,128]{2,1,0:T(8,128)S(1)}, f32[16,128]{1,0:T(8,128)S(1)}, f32[320,128]{1,0:T(8,128)S(1)}, f32[320,128]{1,0:T(8,128)S(1)}, f32[80,128]{1,0:T(8,128)S(1)}) custom-call(f32[16,320,128]{2,1,0:T(8,128)} %copy-done.2, f32[576,128]{1,0:T(8,128)S(1)} %collective-permute-done.lon_a_ref, f32[576,128]{1,0:T(8,128)S(1)} %collective-permute-done.1.lon_b_ref, ...), custom_call_target="tpu_custom_call" | custom-call | bytes 6000000 | tf_op jit(solution)/shard_map/middle/pallas_call | solution.py:402
  55.8 0.0 copy-start.25
  55.8 0.8 collective-permute-start.4
  56.6 5.5 %collective-permute-start.5 = (f32[320,128]{1,0:T(8,128)S(1)}, f32[320,128]{1,0:T(8,128)S(1)}, u32[]{:S(2)}, u32[]{:S(2)}) collective-permute-start(f32[320,128]{1,0:T(8,128)S(1)} %get-tuple-element.18), channel_id=1, source_target_pairs={{4,8},{8,4},{12,16},{16,12},{20,24},{24,20},{28,32},{32,28},{36,40... | collective-permute-start | bytes 491528 | tf_op jit(solution)/shard_map/ppermute | solution.py:429
  62.1 0.7 collective-permute-start.7
  62.8 3.1 %collective-permute-start.6 = (f32[80,128]{1,0:T(8,128)S(1)}, f32[80,128]{1,0:T(8,128)S(1)}, u32[]{:S(2)}, u32[]{:S(2)}) collective-permute-start(f32[80,128]{1,0:T(8,128)S(1)} %get-tuple-element.19), channel_id=1, source_target_pairs={{0,1},{1,0},{2,3},{3,2},{4,5},{5,4},{6,7},{7,6},{8,9},{9,8},{10,11... | collective-permute-start | bytes 122888 | tf_op jit(solution)/shard_map/ppermute | solution.py:427
  65.9 2.8 %step.3.x_ref = f32[16,320,128]{2,1,0:T(8,128)S(1)} custom-call(f32[16,320,128]{2,1,0:T(8,128)S(1)} %get-tuple-element.16.x_ref, f32[16,128]{1,0:T(8,128)S(1)} %copy-done.16, f32[40,40]{1,0:T(8,128)S(1)} %copy-done.24), custom_call_target="tpu_custom_call" | custom-call | flops 60000000 | bytes 5000000 | tf_op jit(solution)/shard_map/step/pallas_call | solution.py:402
  68.7 0.0 collective-permute-done.7.lat_b_ref
  68.7 0.0 collective-permute-done.6.lat_a_ref
  68.7 0.0 collective-permute-done.4.lon_a_ref
  68.7 0.0 collective-permute-done.5.lon_b_ref
  68.8 0.3 potential.1
  69.1 0.0 copy-start.8
  69.1 0.7 copy-done.8
  69.7 0.7 copy-done.10
  70.4 0.6 copy-done.14
  71.0 0.6 copy-done.17
  71.6 0.6 copy-done.19
  72.2 5.7 %all-to-all-start.1 = ((f32[16,8,128]{2,1,0:T(8,128)}), f32[16,8,128]{2,1,0:T(8,128)S(1)}, u32[]{:S(2)}, u32[]{:S(2)}) async-start(f32[16,8,128]{2,1,0:T(8,128)} %copy-done.14), calls=%async_computation.1 | async-start | bytes 131072 | tf_op jit(solution)/shard_map/all_to_all | solution.py:510
  77.9 0.0 copy-start.1
  77.9 1.6 %copy-done.1 = f32[8,32,16,128]{3,2,1,0:T(8,128)S(1)} copy-done((f32[8,32,16,128]{3,2,1,0:T(8,128)S(1)}, f32[8,32,16,128]{3,2,1,0:T(8,128)}, u32[]{:S(2)}) %copy-start.1) | copy-done | bytes 2097176
  79.5 0.7 copy-done.22
  80.3 0.0 copy-start.26
  80.3 3.3 %shell_edge.1 = f32[4096,128]{1,0:T(8,128)} custom-call(f32[4096,128]{1,0:T(8,128)S(1)} %bitcast.7, f32[512,128]{1,0:T(8,128)S(1)} %bitcast.9, f32[3,8,8]{2,1,0:T(8,128)S(1)} %copy-done.22, f32[576,128]{1,0:T(8,128)S(1)} %collective-permute-done.lon_a_ref, f32[576,128]{1,0:T(8,128)S(1)} %collective-permute-done.1.lon_b_ref, ...), custom_call_target="tpu_custom_call" | custom-call | bytes 4000000 | tf_op jit(solution)/shard_map/shell_edge/pallas_call | solution.py:402
  83.6 4.1 %finish.1 = f32[5120,128]{1,0:T(8,128)} custom-call(f32[16,320,128]{2,1,0:T(8,128)S(1)} %step.3.x_ref, f32[320,128]{1,0:T(8,128)S(1)} %copy-done.9, f32[320,128]{1,0:T(8,128)S(1)} %copy-done.11, f32[80,128]{1,0:T(8,128)S(1)} %copy-done.20, f32[80,128]{1,0:T(8,128)S(1)} %copy-done.18, f32[16,128]{1,0:T(8,128)S(1)} %copy-done.16, f32[40,8]{1,0:T(8,128)S(1)} %copy-done.13, ...), custom_call_target="tpu_custom_call" | custom-call | bytes 5000000 | tf_op jit(solution)/shard_map/finish/pallas_call | solution.py:402
  87.7 0.0 all-to-all-done.1.got_ref
  87.7 1.3 %pick.1 = f32[16,128]{1,0:T(8,128)} custom-call(f32[16,8,128]{2,1,0:T(8,128)S(1)} %all-to-all-done.1.got_ref, s32[1,16,1]{2,1,0:T(8,128)S(1)} %copy.14.fp_ref), custom_call_target="tpu_custom_call" | custom-call | tf_op jit(solution)/shard_map/pick/pallas_call | solution.py:402
  (30 shorter events, 0.1 us)
Async XLA Ops:
  0.6 20.8 %copy-start.30 = (s32[1,16,1]{1,2,0:T(1,128)S(1)}, s32[1,16,1]{1,2,0:T(1,128)}, u32[]{:S(2)}) copy-start(s32[1,16,1]{1,2,0:T(1,128)} %param.15) | copy-start | bytes 196
  0.6 1.6 %copy-start.3 = (f32[8,32,16,128]{3,2,1,0:T(8,128)S(1)}, f32[8,32,16,128]{3,2,1,0:T(8,128)}, u32[]{:S(2)}) copy-start(f32[8,32,16,128]{3,2,1,0:T(8,128)} %x_ref.1) | copy-start | bytes 6291460
  2.2 19.3 %copy-start.4 = (f32[8,32,16,128]{3,2,1,0:T(8,128)S(1)}, f32[8,32,16,128]{3,2,1,0:T(8,128)}, u32[]{:S(2)}) copy-start(f32[8,32,16,128]{3,2,1,0:T(8,128)} %x_ref.1) | copy-start | bytes 6291460
  2.2 19.3 %copy-start.7 = (f32[32,16,128]{2,1,0:T(8,128)S(1)}, f32[32,16,128]{2,1,0:T(8,128)}, u32[]{:S(2)}) copy-start(f32[32,16,128]{2,1,0:T(8,128)} %res_ref.3) | copy-start | bytes 786436
  2.2 19.3 %copy-start.21 = (f32[3,8,8]{2,1,0:T(8,128)S(1)}, f32[3,8,8]{2,1,0:T(8,128)}, u32[]{:S(2)}) copy-start(f32[3,8,8]{2,1,0:T(8,128)} %jac_ref.5) | copy-start | bytes 2308
  7.3 1.5 %copy-start.5 = (f32[16,320,128]{2,1,0:T(8,128)}, f32[16,320,128]{2,1,0:T(8,128)S(1)}, u32[]{:S(2)}) copy-start(f32[16,320,128]{2,1,0:T(8,128)S(1)} %get-tuple-element.15.x_ref) | copy-start | bytes 7864324
  8.8 20.5 %copy-start.27 = (f32[8]{0:T(128)S(1)}, f32[8]{0:T(128)}, u32[]{:S(2)}) copy-start(f32[8]{0:T(128)} %weight_ref.1) | copy-start | bytes 100
  8.8 20.5 %copy-start.28 = (s32[1,16]{1,0:T(1,128)S(1)}, s32[1,16]{1,0:T(1,128)}, u32[]{:S(2)}) copy-start(s32[1,16]{1,0:T(1,128)} %row_ref.1) | copy-start | bytes 196
  8.8 20.5 %collective-permute-start = (f32[576,128]{1,0:T(8,128)}, f32[576,128]{1,0:T(8,128)S(1)}, u32[]{:S(2)}, u32[]{:S(2)}) collective-permute-start(f32[576,128]{1,0:T(8,128)} %get-tuple-element.12), channel_id=1, source_target_pairs={{0,4},{4,0},{8,12},{12,8},{16,20},{20,16},{24,28},{28,24},{32,36},... | collective-permute-start | bytes 884744 | tf_op jit(solution)/shard_map/ppermute | solution.py:429
  11.2 18.0 %collective-permute-start.1 = (f32[576,128]{1,0:T(8,128)}, f32[576,128]{1,0:T(8,128)S(1)}, u32[]{:S(2)}, u32[]{:S(2)}) collective-permute-start(f32[576,128]{1,0:T(8,128)} %get-tuple-element.13), channel_id=1, source_target_pairs={{4,8},{8,4},{12,16},{16,12},{20,24},{24,20},{28,32},{32,28},{36,40... | collective-permute-start | bytes 884744 | tf_op jit(solution)/shard_map/ppermute | solution.py:429
  17.1 12.2 %collective-permute-start.3 = (f32[208,128]{1,0:T(8,128)}, f32[208,128]{1,0:T(8,128)}, u32[]{:S(2)}, u32[]{:S(2)}) collective-permute-start(f32[208,128]{1,0:T(8,128)} %get-tuple-element.14), channel_id=1, source_target_pairs={{1,2},{2,1},{5,6},{6,5},{9,10},{10,9},{13,14},{14,13},{17,18},{18,... | collective-permute-start | bytes 319496 | tf_op jit(solution)/shard_map/ppermute | solution.py:427
  18.4 10.9 %collective-permute-start.2 = (f32[208,128]{1,0:T(8,128)}, f32[208,128]{1,0:T(8,128)}, u32[]{:S(2)}, u32[]{:S(2)}) collective-permute-start(f32[208,128]{1,0:T(8,128)} %get-tuple-element.14), channel_id=1, source_target_pairs={{0,1},{1,0},{2,3},{3,2},{4,5},{5,4},{6,7},{7,6},{8,9},{9,8},{10,11... | collective-permute-start | bytes 319496 | tf_op jit(solution)/shard_map/ppermute | solution.py:427
  29.2 9.5 %copy-start.6 = (f32[16,320,128]{2,1,0:T(8,128)S(1)}, f32[16,320,128]{2,1,0:T(8,128)}, u32[]{:S(2)}) copy-start(f32[16,320,128]{2,1,0:T(8,128)} %copy-done.5) | copy-start | bytes 7864324
  29.2 9.5 %copy-start.16 = (f32[16,128]{1,0:T(8,128)S(1)}, f32[16,128]{1,0:T(8,128)}, u32[]{:S(2)}) copy-start(f32[16,128]{1,0:T(8,128)} %cond_ref.9) | copy-start | bytes 24580
  30.6 1.3 %copy-start = (f32[8,32,16,128]{3,2,1,0:T(8,128)}, f32[8,32,16,128]{3,2,1,0:T(8,128)S(1)}, u32[]{:S(2)}) copy-start(f32[8,32,16,128]{3,2,1,0:T(8,128)S(1)} %shell.1.part_ref) | copy-start | bytes 6291460
  31.9 0.6 copy-start.15
  32.6 11.8 %all-to-all-start = ((f32[16,8,128]{2,1,0:T(8,128)}), f32[16,8,128]{2,1,0:T(8,128)S(1)}, u32[]{:S(2)}, u32[]{:S(2)}) async-start(f32[16,8,128]{2,1,0:T(8,128)} %copy-done.15), calls=%async_computation | async-start | bytes 131072 | tf_op jit(solution)/shard_map/all_to_all | solution.py:482
  38.7 0.7 copy-start.23
  42.2 1.5 %copy-start.2 = (f32[16,320,128]{2,1,0:T(8,128)}, f32[16,320,128]{2,1,0:T(8,128)S(1)}, u32[]{:S(2)}) copy-start(f32[16,320,128]{2,1,0:T(8,128)S(1)} %step.2.x_ref) | copy-start | bytes 7864324
  44.4 0.7 copy-start.12
  45.1 20.8 %copy-start.24 = (f32[40,40]{1,0:T(8,128)S(1)}, f32[40,40]{1,0:T(8,128)}, u32[]{:S(2)}) copy-start(f32[40,40]{1,0:T(8,128)} %chem_ref.3) | copy-start | bytes 19204
  55.8 13.0 %copy-start.25 = (f32[16,128]{1,0:T(8,128)}, f32[16,128]{1,0:T(8,128)S(1)}, u32[]{:S(2)}) copy-start(f32[16,128]{1,0:T(8,128)S(1)} %get-tuple-element.20.source_ref) | copy-start | bytes 24580
  55.8 12.9 %collective-permute-start.4 = (f32[320,128]{1,0:T(8,128)S(1)}, f32[320,128]{1,0:T(8,128)S(1)}, u32[]{:S(2)}, u32[]{:S(2)}) collective-permute-start(f32[320,128]{1,0:T(8,128)S(1)} %get-tuple-element.17), channel_id=1, source_target_pairs={{0,4},{4,0},{8,12},{12,8},{16,20},{20,16},{24,28},{28,24},{32,36},... | collective-permute-start | bytes 491528 | tf_op jit(solution)/shard_map/ppermute | solution.py:429
  56.6 12.2 %collective-permute-start.5 = (f32[320,128]{1,0:T(8,128)S(1)}, f32[320,128]{1,0:T(8,128)S(1)}, u32[]{:S(2)}, u32[]{:S(2)}) collective-permute-start(f32[320,128]{1,0:T(8,128)S(1)} %get-tuple-element.18), channel_id=1, source_target_pairs={{4,8},{8,4},{12,16},{16,12},{20,24},{24,20},{28,32},{32,28},{36,40... | collective-permute-start | bytes 491528 | tf_op jit(solution)/shard_map/ppermute | solution.py:429
  62.1 6.6 %collective-permute-start.7 = (f32[80,128]{1,0:T(8,128)S(1)}, f32[80,128]{1,0:T(8,128)S(1)}, u32[]{:S(2)}, u32[]{:S(2)}) collective-permute-start(f32[80,128]{1,0:T(8,128)S(1)} %get-tuple-element.19), channel_id=1, source_target_pairs={{1,2},{2,1},{5,6},{6,5},{9,10},{10,9},{13,14},{14,13},{17,18},{18,... | collective-permute-start | bytes 122888 | tf_op jit(solution)/shard_map/ppermute | solution.py:427
  62.8 5.9 %collective-permute-start.6 = (f32[80,128]{1,0:T(8,128)S(1)}, f32[80,128]{1,0:T(8,128)S(1)}, u32[]{:S(2)}, u32[]{:S(2)}) collective-permute-start(f32[80,128]{1,0:T(8,128)S(1)} %get-tuple-element.19), channel_id=1, source_target_pairs={{0,1},{1,0},{2,3},{3,2},{4,5},{5,4},{6,7},{7,6},{8,9},{9,8},{10,11... | collective-permute-start | bytes 122888 | tf_op jit(solution)/shard_map/ppermute | solution.py:427
  65.9 2.9 %copy-start.29 = (f32[40]{0:T(128)S(1)}, f32[40]{0:T(128)}, u32[]{:S(2)}) copy-start(f32[40]{0:T(128)} %param.21) | copy-start | bytes 484
  69.1 0.7 copy-start.8
  69.7 0.7 copy-start.10
  70.4 0.6 copy-start.14
  71.0 0.6 copy-start.17
  71.6 0.6 copy-start.19
  72.2 15.5 %all-to-all-start.1 = ((f32[16,8,128]{2,1,0:T(8,128)}), f32[16,8,128]{2,1,0:T(8,128)S(1)}, u32[]{:S(2)}, u32[]{:S(2)}) async-start(f32[16,8,128]{2,1,0:T(8,128)} %copy-done.14), calls=%async_computation.1 | async-start | bytes 131072 | tf_op jit(solution)/shard_map/all_to_all | solution.py:510
  77.9 1.6 %copy-start.1 = (f32[8,32,16,128]{3,2,1,0:T(8,128)S(1)}, f32[8,32,16,128]{3,2,1,0:T(8,128)}, u32[]{:S(2)}) copy-start(f32[8,32,16,128]{3,2,1,0:T(8,128)} %copy-done) | copy-start | bytes 6291460
  79.5 0.7 copy-start.22
  80.2 3.3 %copy-start.9 = (f32[320,128]{1,0:T(8,128)S(1)}, f32[320,128]{1,0:T(8,128)}, u32[]{:S(2)}) copy-start(f32[320,128]{1,0:T(8,128)} %copy-done.8) | copy-start | bytes 491524
  80.2 3.3 %copy-start.11 = (f32[320,128]{1,0:T(8,128)S(1)}, f32[320,128]{1,0:T(8,128)}, u32[]{:S(2)}) copy-start(f32[320,128]{1,0:T(8,128)} %copy-done.10) | copy-start | bytes 491524
  80.2 3.3 %copy-start.13 = (f32[40,8]{1,0:T(8,128)S(1)}, f32[40,8]{1,0:T(8,128)}, u32[]{:S(2)}) copy-start(f32[40,8]{1,0:T(8,128)} %copy.15.coupling_ref) | copy-start | bytes 3844
  80.2 3.3 %copy-start.18 = (f32[80,128]{1,0:T(8,128)S(1)}, f32[80,128]{1,0:T(8,128)}, u32[]{:S(2)}) copy-start(f32[80,128]{1,0:T(8,128)} %copy-done.17) | copy-start | bytes 122884
  80.2 3.3 %copy-start.20 = (f32[80,128]{1,0:T(8,128)S(1)}, f32[80,128]{1,0:T(8,128)}, u32[]{:S(2)}) copy-start(f32[80,128]{1,0:T(8,128)} %copy-done.19) | copy-start | bytes 122884
  80.3 3.3 %copy-start.26 = (f32[16,128]{1,0:T(8,128)S(1)}, f32[16,128]{1,0:T(8,128)}, u32[]{:S(2)}) copy-start(f32[16,128]{1,0:T(8,128)} %copy-done.25) | copy-start | bytes 24580

commit v2 on v1

v2 whole, which is shorter than its diff:
```python
import functools

import jax
import jax.numpy as jnp
from jax import lax
from jax.experimental import pallas as pl
from jax.experimental.pallas import tpu as pltpu
from jax.sharding import PartitionSpec as P

NV = 8
NF = 40
RAD = 32
PH = 16
TH = 128
LEV = 8
LON = 16
BLOCKS = 16
KF = LEV * NF
SHELL_ROWS = NV * RAD
F32 = jnp.float32
BF16 = jnp.bfloat16
VMEM = pl.BlockSpec(memory_space=pltpu.VMEM)
SMEM = pl.BlockSpec(memory_space=pltpu.SMEM)
HBM = pl.BlockSpec(memory_space=pltpu.HBM)
DMA = pltpu.SemaphoreType.DMA
PARAMS = pltpu.CompilerParams(vmem_limit_bytes=24 * 1024 * 1024)


def go(source, target, sem):
    copy = pltpu.make_async_copy(source, target, sem)
    copy.start()
    return copy


def odd_lon():
    return lax.rem(lax.axis_index("lon"), 2) == 1


def odd_lat():
    return lax.rem(lax.axis_index("lat"), 2) == 1


def lanes(rows):
    return lax.broadcasted_iota(jnp.int32, (rows, TH), 1)


def slot_of(rows):
    return lax.rem(lanes(rows) + 1, TH) // 2


def edge_of(rows):
    lane = lanes(rows)
    return (lane == 0) | (lane == TH - 1)


def spin(x, shift):
    shift = shift % TH
    return x if shift == 0 else pltpu.roll(x, shift, 1)


def merged(first, second):
    odd = odd_lat()
    left = jnp.where(odd, first, second)
    right = jnp.where(odd, second, first)
    even_lane = lax.rem(lanes(left.shape[0]), 2) == 0
    return jnp.where(even_lane, spin(left, 1), spin(right, -1))


def load_level(slab_ref, s2_ref, sems, k):
    for l in range(LON):
        go(slab_ref.at[:, k, l, :], s2_ref.at[l, k * NF : (k + 1) * NF, :], sems.at[k])


def wait_level(s2_ref, sems, k):
    part = s2_ref.at[:, k * NF : (k + 1) * NF, :]
    pltpu.make_async_copy(part, part, sems.at[k]).wait()


def pack_level(s2_ref, k, slot, acc):
    for l in range(LON):
        j = l + LON * (k % 4)
        acc = jnp.where(slot == j, spin(s2_ref[l, k * NF : (k + 1) * NF, :], 2 * j), acc)
    return acc


def pack_kernel(slab_ref, shell_ref, lon_a_ref, lon_b_ref, lat_ref, s2_ref, sh_ref, slab_sems, shell_sems):
    copies = [
        go(
            shell_ref.at[v * RAD * PH : (v + 1) * RAD * PH],
            sh_ref.at[v * RAD * PH : (v + 1) * RAD * PH],
            shell_sems.at[v],
        )
        for v in range(NV)
    ]
    odd = odd_lon()
    slot = slot_of(PH)
    for v in range(NV):
        load_level(slab_ref, s2_ref, slab_sems, v)
        copies[v].wait()
        acc = jnp.zeros((PH, TH), F32)
        for r in range(RAD):
            x = sh_ref[(v * RAD + r) * PH : (v * RAD + r + 1) * PH, :]
            acc = jnp.where(slot == r, spin(x, 2 * r), acc)
        lat_ref[2 * NF + v * PH : 2 * NF + (v + 1) * PH, :] = acc
        low = sh_ref[pl.ds(v * RAD * PH, RAD, stride=PH), :]
        high = sh_ref[pl.ds(v * RAD * PH + PH - 1, RAD, stride=PH), :]
        at = KF + v * RAD
        lon_a_ref[at : at + RAD, :] = jnp.where(odd, low, high)
        lon_b_ref[at : at + RAD, :] = jnp.where(odd, high, low)
    slot = slot_of(NF)
    for half in range(2):
        acc = jnp.zeros((NF, TH), F32)
        for k in range(4 * half, 4 * half + 4):
            wait_level(s2_ref, slab_sems, k)
            acc = pack_level(s2_ref, k, slot, acc)
        lat_ref[half * NF : (half + 1) * NF, :] = acc
    low, high = s2_ref[0], s2_ref[LON - 1]
    lon_a_ref[0:KF, :] = jnp.where(odd, low, high)
    lon_b_ref[0:KF, :] = jnp.where(odd, high, low)


def mixing_matrix(chem):
    rows = (lax.broadcasted_iota(jnp.int32, (2 * NF, NF), 0) % NF) == lax.broadcasted_iota(
        jnp.int32, (2 * NF, NF), 1
    )
    cols = lax.broadcasted_iota(jnp.int32, (NF, 6 * NF), 0) == (
        lax.broadcasted_iota(jnp.int32, (NF, 6 * NF), 1) % NF
    )
    wide = jnp.dot(
        jnp.dot(
            rows.astype(F32), chem, precision=lax.Precision.HIGHEST, preferred_element_type=F32
        ),
        cols.astype(F32),
        precision=lax.Precision.HIGHEST,
        preferred_element_type=F32,
    )
    i = lax.broadcasted_iota(jnp.int32, (2 * NF, 6 * NF), 0)
    j = lax.broadcasted_iota(jnp.int32, (2 * NF, 6 * NF), 1)
    wide = jnp.where((i // NF) == ((j // NF) % 2), 0.1 * wide, 0.0)
    high = wide.astype(BF16).astype(F32)
    return jnp.where(j < 4 * NF, high, wide - high).astype(BF16)


def step(x_ref, cond_ref, chem_ref, o_ref):
    lhs = mixing_matrix(chem_ref[...])
    lane = lanes(2 * NF)
    zero = jnp.zeros((NF, TH), F32)

    def body(g, carry):
        for kp in range(LEV // 2):
            rows = slice(2 * NF * kp, 2 * NF * (kp + 1))
            xs = [x_ref[2 * g, rows, :], x_ref[2 * g + 1, rows, :]]
            below = x_ref[jnp.maximum(2 * g - 1, 0), rows, :] * jnp.where(g > 0, 1.0, 0.0)
            above = x_ref[jnp.minimum(2 * g + 2, LON - 1), rows, :] * jnp.where(
                g < LON // 2 - 1, 1.0, 0.0
            )
            near = [below + xs[1], xs[0] + above]
            both = jnp.concatenate(xs, axis=1)
            high = both.astype(BF16)
            low = (both - high.astype(F32)).astype(BF16)
            mixed = jnp.dot(
                lhs, jnp.concatenate([high, low, high], axis=0), preferred_element_type=F32
            )
            for i in range(2):
                x = xs[i]
                l = 2 * g + i
                if kp == 0:
                    down = jnp.concatenate([zero, x[:NF]], axis=0)
                else:
                    down = x_ref[l, 2 * NF * kp - NF : 2 * NF * kp + NF, :]
                if kp == LEV // 2 - 1:
                    up = jnp.concatenate([x[NF:], zero], axis=0)
                else:
                    up = x_ref[l, 2 * NF * kp + NF : 2 * NF * kp + 3 * NF, :]
                sides = jnp.where(lane == 0, 0.0, spin(x, 1)) + jnp.where(
                    lane == TH - 1, 0.0, spin(x, -1)
                )
                c = 0.1 * cond_ref[pl.ds(l, 1), :]
                o_ref[l, rows, :] = (
                    x * (0.8 - 4.0 * c)
                    + c * (near[i] + sides)
                    + 0.1 * (up + down)
                    + mixed[:, i * TH : (i + 1) * TH]
                )
        return carry

    lax.fori_loop(0, LON // 2, body, 0)


def shell_matrices(jac_ref):
    size = NV * PH
    spread = (
        lax.broadcasted_iota(jnp.int32, (size, NV), 0) // PH
        == lax.broadcasted_iota(jnp.int32, (size, NV), 1)
    ).astype(F32)
    gather = (
        lax.broadcasted_iota(jnp.int32, (NV, size), 0)
        == lax.broadcasted_iota(jnp.int32, (NV, size), 1) // PH
    ).astype(F32)
    i = lax.broadcasted_iota(jnp.int32, (size, size), 0)
    j = lax.broadcasted_iota(jnp.int32, (size, size), 1)
    apart = (j % PH) - (i % PH)

    def wide(d):
        half = jnp.dot(
            spread, jac_ref[d], precision=lax.Precision.HIGHEST, preferred_element_type=F32
        )
        return 0.1 * jnp.dot(
            half, gather, precision=lax.Precision.HIGHEST, preferred_element_type=F32
        )

    turn = wide(1)
    parts = [
        jnp.where(apart == 1, turn, jnp.where(apart == -1, -turn, 0.0)),
        jnp.where(apart == 0, wide(0), 0.0),
        jnp.where(apart == 0, wide(2), 0.0),
    ]
    high = [part.astype(BF16) for part in parts]
    low = [(part - h.astype(F32)).astype(BF16) for part, h in zip(parts, high)]
    same = (i // PH) == (j // PH)
    sums = jnp.where(same & ((apart == 1) | (apart == -1)), 1.0, 0.0).astype(BF16)
    return jnp.concatenate(high + high + low, axis=1), jnp.concatenate([sums, sums], axis=1)


def halves(x):
    high = x.astype(BF16)
    return high, (x - high.astype(F32)).astype(BF16)


def shell_part(x_ref, res_ref, jac_ref, o_ref, done):
    flux_of, sums_of = shell_matrices(jac_ref)
    lane = lanes(NV * PH)

    def rows_of(r):
        return jnp.concatenate([x_ref[v, r] for v in range(NV)], axis=0)

    def body(g, carry):
        r = 2 * g
        below = rows_of(jnp.maximum(r - 1, 0)) * jnp.where(g > 0, 1.0, 0.0)
        x = [rows_of(r), rows_of(r + 1)]
        above = rows_of(jnp.minimum(r + 2, RAD - 1)) * jnp.where(g < RAD // 2 - 1, 1.0, 0.0)
        radial = jnp.concatenate([x[1] - below, above - x[0]], axis=1)
        south = [jnp.where(lane == 0, 0.0, spin(a, 1)) for a in x]
        north = [jnp.where(lane == TH - 1, 0.0, spin(a, -1)) for a in x]
        polar = jnp.concatenate([n - s for n, s in zip(north, south)], axis=1)
        xh, xl = halves(jnp.concatenate(x, axis=1))
        rh, rl = halves(radial)
        ph, pl_ = halves(polar)
        flux = jnp.dot(
            flux_of,
            jnp.concatenate([xh, rh, ph, xl, rl, pl_, xh, rh, ph], axis=0),
            preferred_element_type=F32,
        )
        sums = jnp.dot(
            sums_of, jnp.concatenate([xh, xl], axis=0), preferred_element_type=F32
        )
        around = [below + x[1], x[0] + above]
        for i in range(2):
            at = slice(i * TH, (i + 1) * TH)
            lap = (around[i] + sums[:, at]) + (south[i] + north[i]) - 6.0 * x[i]
            res = 0.2 * res_ref[pl.ds(pl.multiple_of((r + i) * PH, PH), PH), :]
            for v in range(NV):
                rows = slice(v * PH, (v + 1) * PH)
                o_ref[v, r + i] = x[i][rows] + res * lap[rows] - flux[rows, at]
        done(r)
        return carry

    lax.fori_loop(0, RAD // 2, body, 0)


def interior_kernel(
    slab_ref, shell_ref, res_ref, jac_ref, cond_ref, chem_ref,
    m_ref, part_ref, first_ref, near_ref,
    s2_ref, sh_ref, so_ref, rs_ref, slab_sems, sems,
):
    one = go(shell_ref, sh_ref, sems.at[0])
    two = go(res_ref, rs_ref, sems.at[1])
    for k in range(LEV):
        load_level(slab_ref, s2_ref, slab_sems, k)
    two.wait()
    slot = slot_of(PH)
    packed = jnp.zeros((PH, TH), F32)
    for r in range(RAD):
        packed = jnp.where(slot == r, spin(rs_ref[r * PH : (r + 1) * PH, :], 2 * r), packed)
    near_ref[0:PH, :] = rs_ref[0:PH, :]
    near_ref[PH : 2 * PH, :] = packed
    for last in range(2):
        at = 2 * PH + last * RAD
        near_ref[at : at + RAD, :] = rs_ref[pl.ds(last * (PH - 1), RAD, stride=PH), :]
    one.wait()

    def send_shell(r):
        go(so_ref.at[:, pl.ds(r, 2)], part_ref.at[:, pl.ds(r, 2)], sems.at[2])

    shell_part(sh_ref, rs_ref, jac_ref, so_ref, send_shell)
    first_ref[...] = so_ref[:, 0]
    for k in range(LEV):
        wait_level(s2_ref, slab_sems, k)
    step(s2_ref, cond_ref, chem_ref, m_ref)
    pltpu.make_async_copy(so_ref, part_ref, sems.at[2]).wait()


def rank_rows(fp_ref, count_ref, visit):
    for b in range(BLOCKS):
        count_ref[b] = 0
    for p in range(PH):
        block = fp_ref[0, p, 0]
        rank = count_ref[block]
        count_ref[block] = rank + 1
        visit(p, block, rank)


def current_kernel(
    part_ref, res_all_ref, jac_ref, weight_ref, fp_ref, row_ref, lon_a_all, lon_b_all, lat_a_all, lat_b_all,
    send_ref, where_ref, cur_ref, count_ref,
):
    lon_a_ref, lon_b_ref = lon_a_all.at[KF:, :], lon_b_all.at[KF:, :]
    lat_a_ref, lat_b_ref = lat_a_all.at[2 * NF :, :], lat_b_all.at[2 * NF :, :]
    send_ref[...] = jnp.zeros(send_ref.shape, F32)
    w = [weight_ref[v] for v in range(NV)]
    wj = [[sum(w[u] * jac_ref[d, u, v] for u in range(NV)) for v in range(NV)] for d in (1, 2)]
    odd = odd_lon()
    cur = sum(w[v] * part_ref[v] for v in range(NV))
    res = 0.2 * res_all_ref[0:PH, :]
    rows_a = [lon_a_ref[v * RAD : v * RAD + 1, :] for v in range(NV)]
    rows_b = [lon_b_ref[v * RAD : v * RAD + 1, :] for v in range(NV)]
    low = [jnp.where(odd, a, b) for a, b in zip(rows_a, rows_b)]
    high = [jnp.where(odd, b, a) for a, b in zip(rows_a, rows_b)]
    row = lax.broadcasted_iota(jnp.int32, (PH, TH), 0)
    lane = lanes(PH)
    plain = sum(w[v] * low[v] for v in range(NV))
    turned = 0.1 * sum(wj[0][v] * low[v] for v in range(NV))
    cur = cur + jnp.where(row == 0, res * plain + turned, 0.0)
    plain = sum(w[v] * high[v] for v in range(NV))
    turned = 0.1 * sum(wj[0][v] * high[v] for v in range(NV))
    cur = cur + jnp.where(row == PH - 1, res * plain - turned, 0.0)
    side = [
        merged(
            lat_a_ref[v * PH : (v + 1) * PH, :],
            lat_b_ref[v * PH : (v + 1) * PH, :],
        )
        for v in range(NV)
    ]
    plain = sum(w[v] * side[v] for v in range(NV))
    turned = 0.1 * sum(wj[1][v] * side[v] for v in range(NV))
    cur = cur + jnp.where(lane == 0, res * plain + turned, 0.0)
    cur = cur + jnp.where(lane == TH - 1, res * plain - turned, 0.0)
    cur_ref[...] = cur

    def visit(p, block, rank):
        where_ref[p : p + 1, :] = jnp.full((1, TH), 2 * block + rank, jnp.int32).astype(F32)
        send_ref[block, pl.ds(rank, 1), :] = cur_ref[p : p + 1, :]
        send_ref[block, pl.ds(2 + rank, 1), :] = jnp.full((1, TH), row_ref[0, p], jnp.int32).astype(F32)

    rank_rows(fp_ref, count_ref, visit)


def slab_edges(lat_a, lat_b):
    return [
        merged(lat_a[h * NF : (h + 1) * NF, :], lat_b[h * NF : (h + 1) * NF, :]) for h in range(2)
    ]


def column(row):
    diagonal = lax.broadcasted_iota(jnp.int32, (NF, NF), 0) == lax.broadcasted_iota(
        jnp.int32, (NF, NF), 1
    )
    return jnp.broadcast_to(
        jnp.sum(
            jnp.where(diagonal, jnp.broadcast_to(row, (NF, NF)), 0.0), axis=1, keepdims=True
        ),
        (NF, TH),
    )


def put_levels(coupling_ref, level_ref, count):
    for k in range(count):
        level_ref[k * NF : (k + 1) * NF, :] = column(0.1 * coupling_ref[k : k + 1, :])


def gather_source(got_ref):
    row = lax.broadcasted_iota(jnp.int32, (LON, TH), 0).astype(F32)
    source = jnp.zeros((LON, TH), F32)
    for b in range(BLOCKS):
        for s in range(2):
            source = source + jnp.where(
                row == got_ref[b, 2 + s : 3 + s, :], got_ref[b, s : s + 1, :], 0.0
            )
    return source


def fixed_tile(x, l, k, c, edge, side_ref, level_ref, source, end_ref):
    rows = slice(k * NF, (k + 1) * NF)
    j = l + LON * (k % 4)
    h = jnp.where(edge, spin(side_ref[(k // 4) * NF : (k // 4 + 1) * NF, :], -2 * j), 0.0)
    if l == 0:
        h = h + end_ref[0, rows, :]
    if l == LON - 1:
        h = h + end_ref[1, rows, :]
    return x + c * h + level_ref[rows, :] * source


def put_edges(lon_a_ref, lon_b_ref, lat_a_ref, lat_b_ref, side_ref, end_ref):
    odd = odd_lon()
    a, b = lon_a_ref[...], lon_b_ref[...]
    end_ref[0] = jnp.where(odd, a, b)
    end_ref[1] = jnp.where(odd, b, a)
    for at in range(0, side_ref.shape[0], NF):
        side_ref[at : at + NF, :] = merged(lat_a_ref[at : at + NF, :], lat_b_ref[at : at + NF, :])


def middle_kernel(
    x_ref, lon_a_all, lon_b_all, lat_a_all, lat_b_all, cond_ref, coupling_ref, weight_ref, got_ref,
    o_ref, source_ref, next_a_ref, next_b_ref, lat_ref, level_ref,
    side_ref, end_ref,
):
    lon_a_ref, lon_b_ref = lon_a_all.at[0:KF, :], lon_b_all.at[0:KF, :]
    lat_a_ref, lat_b_ref = lat_a_all.at[0 : 2 * NF, :], lat_b_all.at[0 : 2 * NF, :]
    put_levels(coupling_ref, level_ref, LEV)
    level_ref[KF : KF + NF, :] = column(weight_ref[...])
    source_ref[...] = gather_source(got_ref)
    put_edges(lon_a_ref, lon_b_ref, lat_a_ref, lat_b_ref, side_ref, end_ref)
    edge = edge_of(NF)
    slot = slot_of(NF)
    for l in range(LON):
        c = 0.1 * cond_ref[l : l + 1, :]
        source = source_ref[l : l + 1, :]
        for k in range(LEV):
            rows = slice(k * NF, (k + 1) * NF)
            x = fixed_tile(x_ref[l, rows, :], l, k, c, edge, side_ref, level_ref, source, end_ref)
            o_ref[l, rows, :] = x
    for half in range(2):
        acc = jnp.zeros((NF, TH), F32)
        for k in range(4 * half, 4 * half + 4):
            acc = pack_level(o_ref, k, slot, acc)
        lat_ref[half * NF : (half + 1) * NF, :] = acc
    odd = odd_lon()
    low, high = o_ref[0], o_ref[LON - 1]
    next_a_ref[...] = jnp.where(odd, low, high)
    next_b_ref[...] = jnp.where(odd, high, low)


def second_kernel(x_ref, cond_ref, chem_ref, m_ref):
    step(x_ref, cond_ref, chem_ref, m_ref)


def potential_kernel(
    x_ref, lon_a_all, lon_b_all, lat_a_all, lat_b_all, cond_ref, level_ref, source_ref, got_ref,
    send_ref,
    pot_ref, side_ref, end_ref,
):
    lon_a_ref, lon_b_ref = lon_a_all.at[0:NF, :], lon_b_all.at[0:NF, :]
    lat_a_ref, lat_b_ref = lat_a_all.at[0:NF, :], lat_b_all.at[0:NF, :]
    edge = edge_of(NF)
    weight = level_ref[KF : KF + NF, :]
    put_edges(lon_a_ref, lon_b_ref, lat_a_ref, lat_b_ref, side_ref, end_ref)
    for l in range(LON):
        c = 0.1 * cond_ref[l : l + 1, :]
        x = fixed_tile(
            x_ref[l, 0:NF, :], l, 0, c, edge, side_ref, level_ref, source_ref[l : l + 1, :], end_ref
        )
        pot_ref[l : l + 1, :] = jnp.sum(weight * x, axis=0, keepdims=True)
    potential = pot_ref[...]
    row = lax.broadcasted_iota(jnp.int32, (LON, TH), 0).astype(F32)
    for b in range(BLOCKS):
        for s in range(2):
            send_ref[b, s : s + 1, :] = jnp.sum(
                jnp.where(row == got_ref[b, 2 + s : 3 + s, :], potential, 0.0), axis=0, keepdims=True
            )
        send_ref[b, 2:8, :] = jnp.zeros((6, TH), F32)


def finish_kernel(
    x_ref, lon_a_ref, lon_b_ref, lat_a_ref, lat_b_ref, cond_ref, level_ref, source_ref,
    o_ref,
    y_ref, side_ref, end_ref, sem,
):
    edge = edge_of(NF)
    put_edges(lon_a_ref, lon_b_ref, lat_a_ref, lat_b_ref, side_ref, end_ref)
    for l in range(LON):
        c = 0.1 * cond_ref[l : l + 1, :]
        source = source_ref[l : l + 1, :]
        for k in range(LEV):
            rows = slice(k * NF, (k + 1) * NF)
            y_ref[l, rows, :] = fixed_tile(
                x_ref[l, rows, :], l, k, c, edge, side_ref, level_ref, source, end_ref
            )
            go(y_ref.at[l, rows, :], o_ref.at[:, k, l, :], sem)
    pltpu.make_async_copy(y_ref, y_ref, sem).wait()


def shell_edge_kernel(
    part_ref, near_ref, jac_ref, lon_a_all, lon_b_all, lat_a_all, lat_b_all,
    o_ref,
    x_ref, y_ref, corr_ref, add_ref, part_sems, sem,
):
    size = RAD * PH
    loads = [
        go(part_ref.at[v * size : (v + 1) * size], x_ref.at[v * size : (v + 1) * size], part_sems.at[v])
        for v in range(NV)
    ]
    lon_a_ref, lon_b_ref = lon_a_all.at[KF:, :], lon_b_all.at[KF:, :]
    lat_a_ref, lat_b_ref = lat_a_all.at[2 * NF :, :], lat_b_all.at[2 * NF :, :]
    odd = odd_lon()
    edge = edge_of(PH)
    even_lane = lax.rem(lanes(PH), 2) == 0
    packed = 0.2 * near_ref[PH : 2 * PH, :]
    side = [
        merged(lat_a_ref[v * PH : (v + 1) * PH, :], lat_b_ref[v * PH : (v + 1) * PH, :])
        for v in range(NV)
    ]
    for u in range(NV):
        turned = 0.1 * sum(jac_ref[2, u, v] * side[v] for v in range(NV))
        corr_ref[u] = packed * side[u] + jnp.where(even_lane, turned, -turned)
    for last in range(2):
        at = 2 * PH + last * RAD
        near = 0.2 * near_ref[at : at + RAD, :]
        ends = []
        for v in range(NV):
            a, b = lon_a_ref[v * RAD : (v + 1) * RAD, :], lon_b_ref[v * RAD : (v + 1) * RAD, :]
            ends.append(jnp.where(odd, b, a) if last else jnp.where(odd, a, b))
        for u in range(NV):
            turned = 0.1 * sum(jac_ref[1, u, v] * ends[v] for v in range(NV))
            add_ref[last, u] = near * ends[u] + (-turned if last else turned)
    for u in range(NV):
        loads[u].wait()
        corr = corr_ref[u]
        for r in range(RAD):
            rows = slice((u * RAD + r) * PH, (u * RAD + r + 1) * PH)
            y_ref[rows, :] = x_ref[rows, :] + jnp.where(edge, spin(corr, -2 * r), 0.0)
        for last in range(2):
            where = pl.ds(u * size + last * (PH - 1), RAD, stride=PH)
            y_ref[where, :] = y_ref[where, :] + add_ref[last, u]
        go(y_ref.at[u * size : (u + 1) * size], o_ref.at[u * size : (u + 1) * size], sem)
    pltpu.make_async_copy(y_ref, y_ref, sem).wait()


def pick_kernel(got_ref, where_ref, o_ref):
    where = where_ref[...]
    picked = jnp.zeros((PH, TH), F32)
    for b in range(BLOCKS):
        for s in range(2):
            picked = picked + jnp.where(where == float(2 * b + s), got_ref[b, s : s + 1, :], 0.0)
    o_ref[...] = picked


def call(kernel, name, ins, outs, specs, kept=(), scratch=(), flops=0, moved=0):
    ins = [
        pltpu.with_memory_space_constraint(x, pltpu.HBM) if spec is HBM else x
        for x, spec in zip(ins, specs)
    ]
    shapes = [
        pltpu.HBM(shape, F32) if i in kept else jax.ShapeDtypeStruct(shape, F32)
        for i, shape in enumerate(outs)
    ]
    places = [HBM if i in kept else VMEM for i in range(len(outs))]
    single = len(shapes) == 1
    return pl.pallas_call(
        kernel,
        out_shape=shapes[0] if single else shapes,
        in_specs=specs,
        out_specs=places[0] if single else places,
        scratch_shapes=list(scratch),
        compiler_params=PARAMS,
        cost_estimate=pl.CostEstimate(flops=flops, bytes_accessed=moved, transcendentals=0),
        name=name,
    )(*ins)


def swaps(count, first, periodic):
    pairs = []
    for i in range(first, count, 2):
        if i + 1 < count or periodic:
            j = (i + 1) % count
            pairs += [(i, j), (j, i)]
    return pairs


def exchange(lon_a, lon_b, lat):
    ring = ("comp", "lon")
    size = lax.axis_size("comp") * lax.axis_size("lon")
    width = lax.axis_size("lat")
    got_lat = [lax.ppermute(lat, "lat", swaps(width, first, False)) for first in (0, 1)]
    got_lon = [
        lax.ppermute(block, ring, swaps(size, first, True))
        for first, block in enumerate((lon_a, lon_b))
    ]
    return (*got_lon, *got_lat)


def shards(
    shell,
    resistivity,
    jacobians,
    current_weights,
    footpoint,
    footrow,
    slab,
    conductance,
    chemistry,
    coupling,
    potential_weights,
):
    coupling = coupling.T
    slab_scratch = pltpu.VMEM((LON, KF, TH), F32)
    shell_scratch = pltpu.VMEM(shell.shape, F32)
    flat_scratch = pltpu.VMEM((SHELL_ROWS * PH, TH), F32)

    def rows(count):
        return pltpu.VMEM((count, TH), F32)

    lon_a, lon_b, lat = call(
        pack_kernel,
        "pack",
        (slab, shell.reshape(SHELL_ROWS * PH, TH)),
        [(KF + SHELL_ROWS, TH), (KF + SHELL_ROWS, TH), (2 * NF + NV * PH, TH)],
        [HBM, HBM],
        scratch=[slab_scratch, flat_scratch, DMA((LEV,)), DMA((NV,))],
        moved=8_000_000,
    )
    halos = exchange(lon_a, lon_b, lat)
    middle, part, first, near = call(
        interior_kernel,
        "interior",
        (slab, shell, resistivity.reshape(RAD * PH, TH), jacobians, conductance, chemistry),
        [(LON, KF, TH), shell.shape, (NV, PH, TH), (2 * PH + 2 * RAD, TH)],
        [HBM, HBM, HBM, VMEM, VMEM, VMEM],
        kept=(1,),
        scratch=[
            slab_scratch,
            shell_scratch,
            shell_scratch,
            rows(RAD * PH),
            DMA((LEV,)),
            DMA((3,)),
        ],
        flops=90_000_000,
        moved=20_000_000,
    )
    send, where = call(
        current_kernel,
        "current",
        (first, near, jacobians, current_weights, footpoint, footrow, *halos),
        [(BLOCKS, 8, TH), (PH, TH)],
        [VMEM, VMEM, SMEM, SMEM, SMEM, SMEM] + [VMEM] * 4,
        scratch=[rows(PH), pltpu.SMEM((BLOCKS,), jnp.int32)],
    )
    got = lax.all_to_all(send, "lon", split_axis=0, concat_axis=0, tiled=True)
    shell_next = call(
        shell_edge_kernel,
        "shell_edge",
        (part.reshape(SHELL_ROWS * PH, TH), near, jacobians, *halos),
        [(SHELL_ROWS * PH, TH)],
        [HBM, VMEM, SMEM] + [VMEM] * 4,
        kept=(0,),
        scratch=[
            flat_scratch,
            flat_scratch,
            pltpu.VMEM((NV, PH, TH), F32),
            pltpu.VMEM((2, NV, RAD, TH), F32),
            DMA((NV,)),
            DMA,
        ],
        flops=10_000_000,
        moved=8_000_000,
    ).reshape(shell.shape)
    got, shell_next = lax.optimization_barrier((got, shell_next))
    edges = [rows(2 * NF), pltpu.VMEM((2, KF, TH), F32)]
    middle, source, lon_a, lon_b, lat, levels = call(
        middle_kernel,
        "middle",
        (middle, *halos, conductance, coupling, potential_weights.reshape(1, NF), got),
        [(LON, KF, TH), (LON, TH), (KF, TH), (KF, TH), (2 * NF, TH), (KF + NF, TH)],
        [VMEM] * 9,
        scratch=edges,
        moved=8_000_000,
    )
    ends = exchange(lon_a, lon_b, lat)
    last = call(
        second_kernel,
        "second",
        (middle, conductance, chemistry),
        [(LON, KF, TH)],
        [VMEM] * 3,
        flops=60_000_000,
        moved=10_000_000,
    )
    asked = call(
        potential_kernel,
        "potential",
        (last, *ends, conductance, levels, source, got),
        [(BLOCKS, 8, TH)],
        [VMEM] * 9,
        scratch=[rows(LON), rows(NF), pltpu.VMEM((2, NF, TH), F32)],
    )
    back = lax.all_to_all(asked, "lon", split_axis=0, concat_axis=0, tiled=True)
    slab_next = call(
        finish_kernel,
        "finish",
        (last, *ends, conductance, levels, source),
        [slab.shape],
        [VMEM] * 8,
        kept=(0,),
        scratch=[slab_scratch, *edges, DMA],
        moved=8_000_000,
    )
    boundary = call(pick_kernel, "pick", (back, where), [(PH, TH)], [VMEM] * 2)
    return shell_next, slab_next, boundary


def solution(mesh):
    ring = ("comp", "lon")
    placed = (
        P(None, None, ring, "lat"),
        P(None, ring, "lat"),
        P(),
        P(),
        P("lat", ring, None),
        P("lat", ring),
        P(None, None, ring, "lat"),
        P(ring, "lat"),
        P(),
        P(),
        P(),
    )
    return jax.shard_map(
        shards,
        mesh=mesh,
        in_specs=placed,
        out_specs=(P(None, None, ring, "lat"), P(None, None, ring, "lat"), P(ring, "lat")),
        check_vma=False,
    )
```

time: 89.7 us -> 72 us (0.80)
  local copies, waits for them, and re-layouts: 14.9 us -> 3.71 us
  Pallas kernels: 39.3 us -> 29.6 us
  waiting for transfers between devices: 0.72 us -> 8.34 us
  starting transfers between devices: 33.2 us -> 28.9 us
    unnamed x64 -> x27, local copies, waits for them, and re-layouts: 14.9 us -> 3.71 us
    pallas_call x9, Pallas kernels: 37.9 us -> 29.6 us  [call(): pl.pallas_call(kernel, out_shape=shapes[0] if single else shapes, in_spec...]
    all_to_all x1, waiting for transfers between devices: 0.01 us -> 4.49 us  [shards(): back = lax.all_to_all(asked, 'lon', split_axis=0, concat_axis=0, tiled=True)]
    ppermute x4, starting transfers between devices: 8.14 us -> 6.42 us  [exchange(): lax.ppermute(lat, 'lat', swaps(width, first, False))]
    all_to_all x1, waiting for transfers between devices: 0.69 us -> 2.32 us  [shards(): got = lax.all_to_all(send, 'lon', split_axis=0, concat_axis=0, tiled=True)]
    ppermute x4, starting transfers between devices: 14.6 us -> 13.1 us  [exchange(): lax.ppermute(block, ring, swaps(size, first, True))]
    ppermute x4, waiting for transfers between devices: 0.01 us -> 1.53 us  [exchange(): lax.ppermute(block, ring, swaps(size, first, True))]
    pallas_call x1 -> x0, Pallas kernels: 1.32 us -> none  [shards(): pl.pallas_call(current_kernel, grid=(1,), out_shape=jax.ShapeDtypeStruct(...]
  transfers between devices with their start and end apart: 10 -> 10, of which waited for: 1 -> 3; matrix products, arithmetic and copies ran while one was open for 2% -> 0% of each run, Pallas kernels for 23% -> 29%
where the time goes in v2:
time: 72 us; the launch traced here: 71.5 us
  Pallas kernels  29.6 us (41%)
  starting transfers between devices  28.9 us (40%)
  waiting for transfers between devices  8.34 us (12%)
  local copies, waits for them, and re-layouts  3.71 us (5%)
  between operations  0.89 us (1%)
    pallas_call x9, Pallas kernels, call(): pl.pallas_call(kernel, out_shape=shapes[0] if single else shapes, in_spec...  29.6 us
    ppermute x4, starting transfers between devices, exchange(): lax.ppermute(block, ring, swaps(size, first, True))  13.1 us
    ppermute x4, starting transfers between devices, exchange(): lax.ppermute(lat, 'lat', swaps(width, first, False))  6.42 us
    all_to_all x1, starting transfers between devices, shards(): got = lax.all_to_all(send, 'lon', split_axis=0, concat_axis=0, tiled=True)  4.78 us
    all_to_all x1, starting transfers between devices, shards(): back = lax.all_to_all(asked, 'lon', split_axis=0, concat_axis=0, tiled=True)  4.67 us
    all_to_all x1, waiting for transfers between devices, shards(): back = lax.all_to_all(asked, 'lon', split_axis=0, concat_axis=0, tiled=True)  4.49 us
    unnamed x27, local copies, waits for them, and re-layouts  3.71 us
    all_to_all x1, waiting for transfers between devices, shards(): got = lax.all_to_all(send, 'lon', split_axis=0, concat_axis=0, tiled=True)  2.32 us
  transfers between devices with their start and end apart: 10, of which 3 were waited for; matrix products, arithmetic and copies ran while one was open for 0% of the time, Pallas kernels for 29%

profile of v2, /device:TPU:1, one launch (start us, length us, event | category | flops | bytes accessed | tf_op | source)
XLA Modules:
  0.0 71.5 jit_solution(3591804150143164705)
XLA Ops:
  0.6 0.0 copy-start.12
  0.6 0.0 copy-start.2
  0.7 0.0 copy-start.3
  0.7 0.0 copy-start.5
  0.7 4.4 %pack.1 = (f32[576,128]{1,0:T(8,128)}, f32[576,128]{1,0:T(8,128)}, f32[208,128]{1,0:T(8,128)}) custom-call(f32[40,8,16,128]{3,2,1,0:T(8,128)} %slab_ref.3, f32[4096,128]{1,0:T(8,128)} %bitcast.8), custom_call_target="tpu_custom_call" | custom-call | bytes 8000000 | tf_op jit(solution)/shard_map/pack/pallas_call | solution.py:558
  5.0 0.0 copy-start.9
  5.1 0.0 copy-start.10
  5.1 2.6 %collective-permute-start = (f32[576,128]{1,0:T(8,128)}, f32[576,128]{1,0:T(8,128)S(1)}, u32[]{:S(2)}, u32[]{:S(2)}) collective-permute-start(f32[576,128]{1,0:T(8,128)} %get-tuple-element.22), channel_id=1, source_target_pairs={{0,4},{4,0},{8,12},{12,8},{16,20},{20,16},{24,28},{28,24},{32,36},... | collective-permute-start | bytes 884744 | tf_op jit(solution)/shard_map/ppermute | solution.py:585
  7.6 5.8 %collective-permute-start.1 = (f32[576,128]{1,0:T(8,128)}, f32[576,128]{1,0:T(8,128)S(1)}, u32[]{:S(2)}, u32[]{:S(2)}) collective-permute-start(f32[576,128]{1,0:T(8,128)} %get-tuple-element.23), channel_id=1, source_target_pairs={{4,8},{8,4},{12,16},{16,12},{20,24},{24,20},{28,32},{32,28},{36,40... | collective-permute-start | bytes 884744 | tf_op jit(solution)/shard_map/ppermute | solution.py:585
  13.4 0.7 collective-permute-start.3
  14.1 3.7 %collective-permute-start.2 = (f32[208,128]{1,0:T(8,128)}, f32[208,128]{1,0:T(8,128)S(1)}, u32[]{:S(2)}, u32[]{:S(2)}) collective-permute-start(f32[208,128]{1,0:T(8,128)} %get-tuple-element.24), channel_id=1, source_target_pairs={{0,1},{1,0},{2,3},{3,2},{4,5},{5,4},{6,7},{7,6},{8,9},{9,8},{10,11... | collective-permute-start | bytes 319496 | tf_op jit(solution)/shard_map/ppermute | solution.py:583
  17.9 0.0 copy-done.12
  17.9 0.1 copy.14.fp_ref
  17.9 0.0 copy-done.2
  17.9 0.0 copy-done.3
  18.0 0.0 copy-done.5
  18.0 12.6 %interior.1 = (f32[16,320,128]{2,1,0:T(8,128)S(1)}, f32[8,32,16,128]{3,2,1,0:T(8,128)}, f32[8,16,128]{2,1,0:T(8,128)S(1)}, f32[96,128]{1,0:T(8,128)S(1)}) custom-call(f32[40,8,16,128]{3,2,1,0:T(8,128)} %slab_ref.3, f32[8,32,16,128]{3,2,1,0:T(8,128)} %shell_ref.1, f32[512,128]{1,0:T(8,128)} %bitcast.11, f32[3,8,8]{2,1,0:T(8,128)S(1)} %copy-done.3, ...), custom_call_target="tpu_custom_call" | custom-call | flops 90000000 | bytes 20000000 | tf_op jit(solution)/shard_map/interior/pallas_call | solution.py:558
  30.6 0.0 collective-permute-done.3.lat_b_all
  30.6 0.0 collective-permute-done.2.lat_a_all
  30.6 0.0 collective-permute-done.lon_a_all
  30.6 0.0 collective-permute-done.1.lon_b_all
  30.6 0.0 copy-done.9
  30.6 0.0 copy-done.10
  30.6 1.1 %current.1 = (f32[16,8,128]{2,1,0:T(8,128)S(1)}, f32[16,128]{1,0:T(8,128)S(1)}) custom-call(f32[8,16,128]{2,1,0:T(8,128)S(1)} %get-tuple-element.20.part_ref, f32[96,128]{1,0:T(8,128)S(1)} %get-tuple-element.21.res_all_ref.near_ref, f32[3,8,8]{2,1,0:T(8,128)S(1)} %copy-done.3, f32[8]{0:T(128)S(1)} %copy-done.9, s32[1,16,1]{2,1,0:T(8,128)S(1)} %copy.14.fp_ref, ...), custom_call_target="tpu_custom_call" | custom-call | tf_op jit(solution)/shard_map/current/pallas_call | solution.py:558
  31.8 0.0 copy-start.7
  31.8 0.6 copy-done.7
  32.4 4.8 %all-to-all-start = ((f32[16,8,128]{2,1,0:T(8,128)}), f32[16,8,128]{2,1,0:T(8,128)S(1)}, u32[]{:S(2)}, u32[]{:S(2)}) async-start(f32[16,8,128]{2,1,0:T(8,128)} %copy-done.7), calls=%async_computation | async-start | bytes 131072 | tf_op jit(solution)/shard_map/all_to_all | solution.py:648
  37.2 0.0 copy-start.4
  37.2 0.7 copy-done.4
  37.9 3.9 %shell_edge.1 = f32[4096,128]{1,0:T(8,128)} custom-call(f32[4096,128]{1,0:T(8,128)} %bitcast.10, f32[96,128]{1,0:T(8,128)S(1)} %get-tuple-element.21.res_all_ref.near_ref, f32[3,8,8]{2,1,0:T(8,128)S(1)} %copy-done.4, f32[576,128]{1,0:T(8,128)S(1)} %collective-permute-done.lon_a_all, f32[576,128]{1,0:T(8,128)S(1)} %collective-permute-done.1.lon_b_all, ...), custom_call_target="tpu_custom_call" | custom-call | flops 10000000 | bytes 8000000 | tf_op jit(solution)/shard_map/shell_edge/pallas_call | solution.py:558
  41.8 0.0 copy-start.6
  41.8 2.3 %all-to-all-done.got_ref = f32[16,8,128]{2,1,0:T(8,128)S(1)} async-done(((f32[16,8,128]{2,1,0:T(8,128)}), f32[16,8,128]{2,1,0:T(8,128)S(1)}, u32[]{:S(2)}, u32[]{:S(2)}) %all-to-all-start) | async-done | bytes 65568 | tf_op jit(solution)/shard_map/all_to_all | solution.py:648
  44.2 0.0 copy-start.8
  44.2 0.7 copy-done.8
  44.8 0.0 copy-start.11
  44.8 0.7 copy-done.11
  45.5 1.6 %middle.1 = (f32[16,320,128]{2,1,0:T(8,128)S(1)}, f32[16,128]{1,0:T(8,128)S(1)}, f32[320,128]{1,0:T(8,128)S(1)}, f32[320,128]{1,0:T(8,128)S(1)}, f32[80,128]{1,0:T(8,128)S(1)}, /*index=5*/f32[360,128]{1,0:T(8,128)S(1)}) custom-call(f32[16,320,128]{2,1,0:T(8,128)S(1)} %get-tuple-element.28.x_ref, f32[576,128]{1,0:T(8,128)S(1)} %collective-permute-done.lon_a_all, ...), custom_call_target="tpu_custom_call" | custom-call | bytes 8000000 | tf_op jit(solution)/shard_map/middle/pallas_call | solution.py:558
  47.1 0.0 copy-start
  47.1 0.4 collective-permute-start.4
  47.6 4.2 %collective-permute-start.5 = (f32[320,128]{1,0:T(8,128)S(1)}, f32[320,128]{1,0:T(8,128)S(1)}, u32[]{:S(2)}, u32[]{:S(2)}) collective-permute-start(f32[320,128]{1,0:T(8,128)S(1)} %get-tuple-element.32), channel_id=1, source_target_pairs={{4,8},{8,4},{12,16},{16,12},{20,24},{24,20},{28,32},{32,28},{36,40... | collective-permute-start | bytes 491528 | tf_op jit(solution)/shard_map/ppermute | solution.py:585
  51.8 0.7 collective-permute-start.7
  52.5 1.4 %collective-permute-start.6 = (f32[80,128]{1,0:T(8,128)S(1)}, f32[80,128]{1,0:T(8,128)S(1)}, u32[]{:S(2)}, u32[]{:S(2)}) collective-permute-start(f32[80,128]{1,0:T(8,128)S(1)} %get-tuple-element.33), channel_id=1, source_target_pairs={{0,1},{1,0},{2,3},{3,2},{4,5},{5,4},{6,7},{7,6},{8,9},{9,8},{10,11... | collective-permute-start | bytes 122888 | tf_op jit(solution)/shard_map/ppermute | solution.py:583
  53.9 0.0 copy-done.6
  53.9 2.9 %second.1.x_ref = f32[16,320,128]{2,1,0:T(8,128)S(1)} custom-call(f32[16,320,128]{2,1,0:T(8,128)S(1)} %get-tuple-element.30.x_ref, f32[16,128]{1,0:T(8,128)S(1)} %copy-done.2, f32[40,40]{1,0:T(8,128)S(1)} %copy-done.6), custom_call_target="tpu_custom_call" | custom-call | flops 60000000 | bytes 10000000 | tf_op jit(solution)/shard_map/second/pallas_call | solution.py:558
  56.7 0.0 collective-permute-done.7.lat_b_ref.lat_b_all
  56.7 0.0 collective-permute-done.6.lat_a_ref.lat_a_all
  56.7 0.0 collective-permute-done.4.lon_a_ref.lon_a_all
  56.8 1.5 %collective-permute-done.5.lon_b_ref.lon_b_all = f32[320,128]{1,0:T(8,128)S(1)} collective-permute-done((f32[320,128]{1,0:T(8,128)S(1)}, f32[320,128]{1,0:T(8,128)S(1)}, u32[]{:S(2)}, u32[]{:S(2)}) %collective-permute-start.5) | collective-permute-done | bytes 163872 | tf_op jit(solution)/shard_map/ppermute | solution.py:585
  58.3 0.0 copy-done
  58.3 0.9 %potential.1 = f32[16,8,128]{2,1,0:T(8,128)} custom-call(f32[16,320,128]{2,1,0:T(8,128)S(1)} %second.1.x_ref, f32[320,128]{1,0:T(8,128)S(1)} %collective-permute-done.4.lon_a_ref.lon_a_all, f32[320,128]{1,0:T(8,128)S(1)} %collective-permute-done.5.lon_b_ref.lon_b_all, f32[80,128]{1,0:T(8,128)S(1)} %collective-permute-done.6.lat_a_ref.lat_a_all, ...), custom_call_target="tpu_custom_call" | custom-call | tf_op jit(solution)/shard_map/potential/pallas_call | solution.py:558
  59.2 4.7 %all-to-all-start.1 = ((f32[16,8,128]{2,1,0:T(8,128)}), f32[16,8,128]{2,1,0:T(8,128)S(1)}, u32[]{:S(2)}, u32[]{:S(2)}) async-start(f32[16,8,128]{2,1,0:T(8,128)} %potential.1), calls=%async_computation.1 | async-start | bytes 131072 | tf_op jit(solution)/shard_map/all_to_all | solution.py:696
  63.9 0.0 copy-start.1
  63.9 0.9 %copy-done.1 = f32[360,128]{1,0:T(8,128)S(1)} copy-done((f32[360,128]{1,0:T(8,128)S(1)}, f32[360,128]{1,0:T(8,128)}, u32[]{:S(2)}) %copy-start.1) | copy-done | bytes 184344
  64.8 1.6 %finish.1 = f32[40,8,16,128]{3,2,1,0:T(8,128)} custom-call(f32[16,320,128]{2,1,0:T(8,128)S(1)} %second.1.x_ref, f32[320,128]{1,0:T(8,128)S(1)} %collective-permute-done.4.lon_a_ref.lon_a_all, f32[320,128]{1,0:T(8,128)S(1)} %collective-permute-done.5.lon_b_ref.lon_b_all, f32[80,128]{1,0:T(8,128)S(1)} %collective-permute-done.6.lat_a_ref.lat_a_all, ...), custom_call_target="tpu_custom_call" | custom-call | bytes 8000000 | tf_op jit(solution)/shard_map/finish/pallas_call | solution.py:558
  66.4 4.5 %all-to-all-done.1.got_ref = f32[16,8,128]{2,1,0:T(8,128)S(1)} async-done(((f32[16,8,128]{2,1,0:T(8,128)}), f32[16,8,128]{2,1,0:T(8,128)S(1)}, u32[]{:S(2)}, u32[]{:S(2)}) %all-to-all-start.1) | async-done | bytes 65568 | tf_op jit(solution)/shard_map/all_to_all | solution.py:696
  70.9 0.6 pick.1
Async XLA Ops:
  0.6 17.2 %copy-start.12 = (s32[1,16,1]{1,2,0:T(1,128)S(1)}, s32[1,16,1]{1,2,0:T(1,128)}, u32[]{:S(2)}) copy-start(s32[1,16,1]{1,2,0:T(1,128)} %param.15) | copy-start | bytes 196
  0.6 17.3 %copy-start.2 = (f32[16,128]{1,0:T(8,128)S(1)}, f32[16,128]{1,0:T(8,128)}, u32[]{:S(2)}) copy-start(f32[16,128]{1,0:T(8,128)} %cond_ref.9) | copy-start | bytes 24580
  0.7 17.3 %copy-start.3 = (f32[3,8,8]{2,1,0:T(8,128)S(1)}, f32[3,8,8]{2,1,0:T(8,128)}, u32[]{:S(2)}) copy-start(f32[3,8,8]{2,1,0:T(8,128)} %jac_ref.5) | copy-start | bytes 2308
  0.7 17.3 %copy-start.5 = (f32[40,40]{1,0:T(8,128)S(1)}, f32[40,40]{1,0:T(8,128)}, u32[]{:S(2)}) copy-start(f32[40,40]{1,0:T(8,128)} %chem_ref.3) | copy-start | bytes 19204
  5.0 25.6 %copy-start.9 = (f32[8]{0:T(128)S(1)}, f32[8]{0:T(128)}, u32[]{:S(2)}) copy-start(f32[8]{0:T(128)} %weight_ref.1) | copy-start | bytes 100
  5.1 25.6 %copy-start.10 = (s32[1,16]{1,0:T(1,128)S(1)}, s32[1,16]{1,0:T(1,128)}, u32[]{:S(2)}) copy-start(s32[1,16]{1,0:T(1,128)} %row_ref.1) | copy-start | bytes 196
  5.1 25.5 %collective-permute-start = (f32[576,128]{1,0:T(8,128)}, f32[576,128]{1,0:T(8,128)S(1)}, u32[]{:S(2)}, u32[]{:S(2)}) collective-permute-start(f32[576,128]{1,0:T(8,128)} %get-tuple-element.22), channel_id=1, source_target_pairs={{0,4},{4,0},{8,12},{12,8},{16,20},{20,16},{24,28},{28,24},{32,36},... | collective-permute-start | bytes 884744 | tf_op jit(solution)/shard_map/ppermute | solution.py:585
  7.6 23.0 %collective-permute-start.1 = (f32[576,128]{1,0:T(8,128)}, f32[576,128]{1,0:T(8,128)S(1)}, u32[]{:S(2)}, u32[]{:S(2)}) collective-permute-start(f32[576,128]{1,0:T(8,128)} %get-tuple-element.23), channel_id=1, source_target_pairs={{4,8},{8,4},{12,16},{16,12},{20,24},{24,20},{28,32},{32,28},{36,40... | collective-permute-start | bytes 884744 | tf_op jit(solution)/shard_map/ppermute | solution.py:585
  13.4 17.1 %collective-permute-start.3 = (f32[208,128]{1,0:T(8,128)}, f32[208,128]{1,0:T(8,128)S(1)}, u32[]{:S(2)}, u32[]{:S(2)}) collective-permute-start(f32[208,128]{1,0:T(8,128)} %get-tuple-element.24), channel_id=1, source_target_pairs={{1,2},{2,1},{5,6},{6,5},{9,10},{10,9},{13,14},{14,13},{17,18},{18,... | collective-permute-start | bytes 319496 | tf_op jit(solution)/shard_map/ppermute | solution.py:583
  14.1 16.5 %collective-permute-start.2 = (f32[208,128]{1,0:T(8,128)}, f32[208,128]{1,0:T(8,128)S(1)}, u32[]{:S(2)}, u32[]{:S(2)}) collective-permute-start(f32[208,128]{1,0:T(8,128)} %get-tuple-element.24), channel_id=1, source_target_pairs={{0,1},{1,0},{2,3},{3,2},{4,5},{5,4},{6,7},{7,6},{8,9},{9,8},{10,11... | collective-permute-start | bytes 319496 | tf_op jit(solution)/shard_map/ppermute | solution.py:583
  31.8 0.6 copy-start.7
  32.4 11.8 %all-to-all-start = ((f32[16,8,128]{2,1,0:T(8,128)}), f32[16,8,128]{2,1,0:T(8,128)S(1)}, u32[]{:S(2)}, u32[]{:S(2)}) async-start(f32[16,8,128]{2,1,0:T(8,128)} %copy-done.7), calls=%async_computation | async-start | bytes 131072 | tf_op jit(solution)/shard_map/all_to_all | solution.py:648
  37.2 0.7 copy-start.4
  41.8 12.0 %copy-start.6 = (f32[40,40]{1,0:T(8,128)S(1)}, f32[40,40]{1,0:T(8,128)}, u32[]{:S(2)}) copy-start(f32[40,40]{1,0:T(8,128)} %chem_ref.3) | copy-start | bytes 19204
  44.2 0.7 copy-start.8
  44.8 0.7 copy-start.11
  47.1 11.1 %copy-start = (f32[360,128]{1,0:T(8,128)}, f32[360,128]{1,0:T(8,128)S(1)}, u32[]{:S(2)}) copy-start(f32[360,128]{1,0:T(8,128)S(1)} %get-tuple-element.34.level_ref) | copy-start | bytes 552964
  47.1 9.6 %collective-permute-start.4 = (f32[320,128]{1,0:T(8,128)S(1)}, f32[320,128]{1,0:T(8,128)S(1)}, u32[]{:S(2)}, u32[]{:S(2)}) collective-permute-start(f32[320,128]{1,0:T(8,128)S(1)} %get-tuple-element.31), channel_id=1, source_target_pairs={{0,4},{4,0},{8,12},{12,8},{16,20},{20,16},{24,28},{28,24},{32,36},... | collective-permute-start | bytes 491528 | tf_op jit(solution)/shard_map/ppermute | solution.py:585
  47.6 10.7 %collective-permute-start.5 = (f32[320,128]{1,0:T(8,128)S(1)}, f32[320,128]{1,0:T(8,128)S(1)}, u32[]{:S(2)}, u32[]{:S(2)}) collective-permute-start(f32[320,128]{1,0:T(8,128)S(1)} %get-tuple-element.32), channel_id=1, source_target_pairs={{4,8},{8,4},{12,16},{16,12},{20,24},{24,20},{28,32},{32,28},{36,40... | collective-permute-start | bytes 491528 | tf_op jit(solution)/shard_map/ppermute | solution.py:585
  51.8 4.9 %collective-permute-start.7 = (f32[80,128]{1,0:T(8,128)S(1)}, f32[80,128]{1,0:T(8,128)S(1)}, u32[]{:S(2)}, u32[]{:S(2)}) collective-permute-start(f32[80,128]{1,0:T(8,128)S(1)} %get-tuple-element.33), channel_id=1, source_target_pairs={{1,2},{2,1},{5,6},{6,5},{9,10},{10,9},{13,14},{14,13},{17,18},{18,... | collective-permute-start | bytes 122888 | tf_op jit(solution)/shard_map/ppermute | solution.py:583
  52.5 4.2 %collective-permute-start.6 = (f32[80,128]{1,0:T(8,128)S(1)}, f32[80,128]{1,0:T(8,128)S(1)}, u32[]{:S(2)}, u32[]{:S(2)}) collective-permute-start(f32[80,128]{1,0:T(8,128)S(1)} %get-tuple-element.33), channel_id=1, source_target_pairs={{0,1},{1,0},{2,3},{3,2},{4,5},{5,4},{6,7},{7,6},{8,9},{9,8},{10,11... | collective-permute-start | bytes 122888 | tf_op jit(solution)/shard_map/ppermute | solution.py:583
  59.2 11.7 %all-to-all-start.1 = ((f32[16,8,128]{2,1,0:T(8,128)}), f32[16,8,128]{2,1,0:T(8,128)S(1)}, u32[]{:S(2)}, u32[]{:S(2)}) async-start(f32[16,8,128]{2,1,0:T(8,128)} %potential.1), calls=%async_computation.1 | async-start | bytes 131072 | tf_op jit(solution)/shard_map/all_to_all | solution.py:696
  63.9 0.9 %copy-start.1 = (f32[360,128]{1,0:T(8,128)S(1)}, f32[360,128]{1,0:T(8,128)}, u32[]{:S(2)}) copy-start(f32[360,128]{1,0:T(8,128)} %copy-done) | copy-start | bytes 552964

commit v3 on v2

--- a/solution.py
+++ b/solution.py
@@ -66,13 +66,17 @@
     return jnp.where(even_lane, spin(left, 1), spin(right, -1))
 
 
-def load_level(slab_ref, s2_ref, sems, k):
+def load_level(slab_ref, s2_ref, sem, k):
     for l in range(LON):
-        go(slab_ref.at[:, k, l, :], s2_ref.at[l, k * NF : (k + 1) * NF, :], sems.at[k])
+        go(slab_ref.at[:, k, l, :], s2_ref.at[l, k * NF : (k + 1) * NF, :], sem)
+
+
+def level_rows(ref, k):
+    return ref.at[:, k * NF : (k + 1) * NF, :]
 
 
 def wait_level(s2_ref, sems, k):
-    part = s2_ref.at[:, k * NF : (k + 1) * NF, :]
+    part = level_rows(s2_ref, k)
     pltpu.make_async_copy(part, part, sems.at[k]).wait()
 
 
@@ -83,7 +87,10 @@
     return acc
 
 
-def pack_kernel(slab_ref, shell_ref, lon_a_ref, lon_b_ref, lat_ref, s2_ref, sh_ref, slab_sems, shell_sems):
+def pack_kernel(
+    slab_ref, shell_ref, lon_a_ref, lon_b_ref, lat_ref,
+    s2_ref, sh_ref, slab_sems, shell_sems,
+):
     copies = [
         go(
             shell_ref.at[v * RAD * PH : (v + 1) * RAD * PH],
@@ -95,7 +102,7 @@
     odd = odd_lon()
     slot = slot_of(PH)
     for v in range(NV):
-        load_level(slab_ref, s2_ref, slab_sems, v)
+        load_level(slab_ref, s2_ref, slab_sems.at[v], v)
         copies[v].wait()
         acc = jnp.zeros((PH, TH), F32)
         for r in range(RAD):
@@ -184,7 +191,7 @@
                 )
         return carry
 
-    lax.fori_loop(0, LON // 2, body, 0)
+    lax.fori_loop(0, LON // 2, body, 0, unroll=4)
 
 
 def shell_matrices(jac_ref):
@@ -193,21 +200,17 @@
         lax.broadcasted_iota(jnp.int32, (size, NV), 0) // PH
         == lax.broadcasted_iota(jnp.int32, (size, NV), 1)
     ).astype(F32)
-    gather = (
-        lax.broadcasted_iota(jnp.int32, (NV, size), 0)
-        == lax.broadcasted_iota(jnp.int32, (NV, size), 1) // PH
-    ).astype(F32)
+    columns = lax.broadcasted_iota(jnp.int32, (3 * NV, 3 * size), 1)
+    gather = (lax.broadcasted_iota(jnp.int32, (3 * NV, 3 * size), 0) == columns // PH).astype(F32)
     i = lax.broadcasted_iota(jnp.int32, (size, size), 0)
     j = lax.broadcasted_iota(jnp.int32, (size, size), 1)
     apart = (j % PH) - (i % PH)
+    exact = dict(precision=lax.Precision.HIGHEST, preferred_element_type=F32)
+    three = jnp.concatenate([jac_ref[d] for d in range(3)], axis=1)
+    spread_out = 0.1 * jnp.dot(jnp.dot(spread, three, **exact), gather, **exact)
 
     def wide(d):
-        half = jnp.dot(
-            spread, jac_ref[d], precision=lax.Precision.HIGHEST, preferred_element_type=F32
-        )
-        return 0.1 * jnp.dot(
-            half, gather, precision=lax.Precision.HIGHEST, preferred_element_type=F32
-        )
+        return spread_out[:, d * size : (d + 1) * size]
 
     turn = wide(1)
     parts = [
@@ -265,18 +268,18 @@
         done(r)
         return carry
 
-    lax.fori_loop(0, RAD // 2, body, 0)
+    lax.fori_loop(0, RAD // 2, body, 0, unroll=4)
 
 
 def interior_kernel(
     slab_ref, shell_ref, res_ref, jac_ref, cond_ref, chem_ref,
     m_ref, part_ref, first_ref, near_ref,
-    s2_ref, sh_ref, so_ref, rs_ref, slab_sems, sems,
+    s2_ref, sh_ref, so_ref, rs_ref, sems,
 ):
     one = go(shell_ref, sh_ref, sems.at[0])
     two = go(res_ref, rs_ref, sems.at[1])
     for k in range(LEV):
-        load_level(slab_ref, s2_ref, slab_sems, k)
+        load_level(slab_ref, s2_ref, sems.at[3], k)
     two.wait()
     slot = slot_of(PH)
     packed = jnp.zeros((PH, TH), F32)
@@ -294,8 +297,7 @@
 
     shell_part(sh_ref, rs_ref, jac_ref, so_ref, send_shell)
     first_ref[...] = so_ref[:, 0]
-    for k in range(LEV):
-        wait_level(s2_ref, slab_sems, k)
+    pltpu.make_async_copy(s2_ref, s2_ref, sems.at[3]).wait()
     step(s2_ref, cond_ref, chem_ref, m_ref)
     pltpu.make_async_copy(so_ref, part_ref, sems.at[2]).wait()
 
@@ -410,18 +412,18 @@
 
 
 def middle_kernel(
-    x_ref, lon_a_all, lon_b_all, lat_a_all, lat_b_all, cond_ref, coupling_ref, weight_ref, got_ref,
-    o_ref, source_ref, next_a_ref, next_b_ref, lat_ref, level_ref,
-    side_ref, end_ref,
+    x_ref, lon_a_all, lon_b_all, lat_a_all, lat_b_all, cond_ref, level_all, got_ref,
+    o_ref, source_ref, next_a_ref, next_b_ref, lat_ref,
+    level_ref, side_ref, end_ref, sem,
 ):
+    copy = go(level_all, level_ref, sem)
     lon_a_ref, lon_b_ref = lon_a_all.at[0:KF, :], lon_b_all.at[0:KF, :]
     lat_a_ref, lat_b_ref = lat_a_all.at[0 : 2 * NF, :], lat_b_all.at[0 : 2 * NF, :]
-    put_levels(coupling_ref, level_ref, LEV)
-    level_ref[KF : KF + NF, :] = column(weight_ref[...])
     source_ref[...] = gather_source(got_ref)
     put_edges(lon_a_ref, lon_b_ref, lat_a_ref, lat_b_ref, side_ref, end_ref)
     edge = edge_of(NF)
     slot = slot_of(NF)
+    copy.wait()
     for l in range(LON):
         c = 0.1 * cond_ref[l : l + 1, :]
         source = source_ref[l : l + 1, :]
@@ -440,8 +442,15 @@
     next_b_ref[...] = jnp.where(odd, high, low)
 
 
-def second_kernel(x_ref, cond_ref, chem_ref, m_ref):
+def second_kernel(
+    x_ref, cond_ref, chem_ref, coupling_ref, weight_ref, m_ref, level_ref, near_ref, last_ref, sems
+):
+    copies = [go(coupling_ref, near_ref, sems.at[0]), go(weight_ref, last_ref, sems.at[1])]
     step(x_ref, cond_ref, chem_ref, m_ref)
+    for copy in copies:
+        copy.wait()
+    put_levels(near_ref, level_ref, LEV)
+    level_ref[KF : KF + NF, :] = column(last_ref[...])
 
 
 def potential_kernel(
@@ -489,16 +498,40 @@
     pltpu.make_async_copy(y_ref, y_ref, sem).wait()
 
 
+def shell_edge_tile(u, x_ref, y_ref, o_ref, corr, adds, edge, sem):
+    size = RAD * PH
+    for r in range(RAD):
+        rows = slice((u * RAD + r) * PH, (u * RAD + r + 1) * PH)
+        y_ref[rows, :] = x_ref[rows, :] + jnp.where(edge, spin(corr, -2 * r), 0.0)
+    for last in range(2):
+        where = pl.ds(u * size + last * (PH - 1), RAD, stride=PH)
+        y_ref[where, :] = y_ref[where, :] + adds[last]
+    go(y_ref.at[u * size : (u + 1) * size], o_ref.at[u * size : (u + 1) * size], sem)
+
+
+def load_part(part_ref, x_ref, part_sems, these):
+    size = RAD * PH
+    return {
+        u: go(
+            part_ref.at[u * size : (u + 1) * size], x_ref.at[u * size : (u + 1) * size], part_sems.at[u]
+        )
+        for u in these
+    }
+
+
+def wait_half(y_ref, first, sem):
+    half = NV // 2 * RAD * PH
+    part = y_ref.at[first * half : (first + 1) * half]
+    pltpu.make_async_copy(part, part, sem).wait()
+
+
 def shell_edge_kernel(
-    part_ref, near_ref, jac_ref, lon_a_all, lon_b_all, lat_a_all, lat_b_all,
-    o_ref,
-    x_ref, y_ref, corr_ref, add_ref, part_sems, sem,
+    part_ref, near_ref, jac_ref, lon_a_all, lon_b_all, lat_a_all, lat_b_all, coupling_ref,
+    o_ref, keep_ref, level_all,
+    x_ref, y_ref, add_ref, cols_ref, level_ref, part_sems, sems,
 ):
-    size = RAD * PH
-    loads = [
-        go(part_ref.at[v * size : (v + 1) * size], x_ref.at[v * size : (v + 1) * size], part_sems.at[v])
-        for v in range(NV)
-    ]
+    copy = go(coupling_ref, cols_ref, sems.at[2])
+    loads = load_part(part_ref, x_ref, part_sems, range(NV // 2))
     lon_a_ref, lon_b_ref = lon_a_all.at[KF:, :], lon_b_all.at[KF:, :]
     lat_a_ref, lat_b_ref = lat_a_all.at[2 * NF :, :], lat_b_all.at[2 * NF :, :]
     odd = odd_lon()
@@ -511,7 +544,9 @@
     ]
     for u in range(NV):
         turned = 0.1 * sum(jac_ref[2, u, v] * side[v] for v in range(NV))
-        corr_ref[u] = packed * side[u] + jnp.where(even_lane, turned, -turned)
+        add_ref[u, 2 * RAD : 2 * RAD + PH, :] = packed * side[u] + jnp.where(
+            even_lane, turned, -turned
+        )
     for last in range(2):
         at = 2 * PH + last * RAD
         near = 0.2 * near_ref[at : at + RAD, :]
@@ -521,18 +556,34 @@
             ends.append(jnp.where(odd, b, a) if last else jnp.where(odd, a, b))
         for u in range(NV):
             turned = 0.1 * sum(jac_ref[1, u, v] * ends[v] for v in range(NV))
-            add_ref[last, u] = near * ends[u] + (-turned if last else turned)
-    for u in range(NV):
+            add_ref[u, last * RAD : (last + 1) * RAD, :] = near * ends[u] + (
+                -turned if last else turned
+            )
+    keep = go(add_ref.at[NV // 2 :], keep_ref, sems.at[1])
+    for u in range(NV // 2):
         loads[u].wait()
-        corr = corr_ref[u]
-        for r in range(RAD):
-            rows = slice((u * RAD + r) * PH, (u * RAD + r + 1) * PH)
-            y_ref[rows, :] = x_ref[rows, :] + jnp.where(edge, spin(corr, -2 * r), 0.0)
-        for last in range(2):
-            where = pl.ds(u * size + last * (PH - 1), RAD, stride=PH)
-            y_ref[where, :] = y_ref[where, :] + add_ref[last, u]
-        go(y_ref.at[u * size : (u + 1) * size], o_ref.at[u * size : (u + 1) * size], sem)
-    pltpu.make_async_copy(y_ref, y_ref, sem).wait()
+        corr = add_ref[u, 2 * RAD : 2 * RAD + PH, :]
+        adds = [add_ref[u, last * RAD : (last + 1) * RAD, :] for last in range(2)]
+        shell_edge_tile(u, x_ref, y_ref, o_ref, corr, adds, edge, sems.at[0])
+    copy.wait()
+    put_levels(cols_ref, level_ref, LEV)
+    copy = go(level_ref, level_all, sems.at[2])
+    wait_half(y_ref, 0, sems.at[0])
+    keep.wait()
+    copy.wait()
+
+
+def shell_rest_kernel(half_ref, part_ref, keep_ref, o_ref, x_ref, y_ref, add_ref, part_sems, sems):
+    keep = go(keep_ref, add_ref, sems.at[1])
+    loads = load_part(part_ref, x_ref, part_sems, range(NV // 2, NV))
+    edge = edge_of(PH)
+    keep.wait()
+    for u in range(NV // 2, NV):
+        loads[u].wait()
+        corr = add_ref[u - NV // 2, 2 * RAD : 2 * RAD + PH, :]
+        adds = [add_ref[u - NV // 2, last * RAD : (last + 1) * RAD, :] for last in range(2)]
+        shell_edge_tile(u, x_ref, y_ref, o_ref, corr, adds, edge, sems.at[0])
+    wait_half(y_ref, 1, sems.at[0])
 
 
 def pick_kernel(got_ref, where_ref, o_ref):
@@ -544,7 +595,7 @@
     o_ref[...] = picked
 
 
-def call(kernel, name, ins, outs, specs, kept=(), scratch=(), flops=0, moved=0):
+def call(kernel, name, ins, outs, specs, kept=(), scratch=(), flops=0, moved=0, aliases=None):
     ins = [
         pltpu.with_memory_space_constraint(x, pltpu.HBM) if spec is HBM else x
         for x, spec in zip(ins, specs)
@@ -562,6 +613,7 @@
         out_specs=places[0] if single else places,
         scratch_shapes=list(scratch),
         compiler_params=PARAMS,
+        input_output_aliases=aliases or {},
         cost_estimate=pl.CostEstimate(flops=flops, bytes_accessed=moved, transcendentals=0),
         name=name,
     )(*ins)
@@ -615,7 +667,12 @@
         (slab, shell.reshape(SHELL_ROWS * PH, TH)),
         [(KF + SHELL_ROWS, TH), (KF + SHELL_ROWS, TH), (2 * NF + NV * PH, TH)],
         [HBM, HBM],
-        scratch=[slab_scratch, flat_scratch, DMA((LEV,)), DMA((NV,))],
+        scratch=[
+            slab_scratch,
+            flat_scratch,
+            DMA((LEV,)),
+            DMA((NV,)),
+        ],
         moved=8_000_000,
     )
     halos = exchange(lon_a, lon_b, lat)
@@ -631,8 +688,7 @@
             shell_scratch,
             shell_scratch,
             rows(RAD * PH),
-            DMA((LEV,)),
-            DMA((3,)),
+            DMA((4,)),
         ],
         flops=90_000_000,
         moved=20_000_000,
@@ -646,42 +702,45 @@
         scratch=[rows(PH), pltpu.SMEM((BLOCKS,), jnp.int32)],
     )
     got = lax.all_to_all(send, "lon", split_axis=0, concat_axis=0, tiled=True)
-    shell_next = call(
+    part = part.reshape(SHELL_ROWS * PH, TH)
+    shell_next, keep, levels = call(
         shell_edge_kernel,
         "shell_edge",
-        (part.reshape(SHELL_ROWS * PH, TH), near, jacobians, *halos),
-        [(SHELL_ROWS * PH, TH)],
-        [HBM, VMEM, SMEM] + [VMEM] * 4,
-        kept=(0,),
+        (part, near, jacobians, *halos, coupling),
+        [(SHELL_ROWS * PH, TH), (NV // 2, 2 * RAD + PH, TH), (KF, TH)],
+        [HBM, VMEM, SMEM] + [VMEM] * 4 + [HBM],
+        kept=(0, 1, 2),
         scratch=[
             flat_scratch,
             flat_scratch,
-            pltpu.VMEM((NV, PH, TH), F32),
-            pltpu.VMEM((2, NV, RAD, TH), F32),
+            pltpu.VMEM((NV, 2 * RAD + PH, TH), F32),
+            pltpu.VMEM((LEV, NF), F32),
+            rows(KF),
             DMA((NV,)),
-            DMA,
+            DMA((3,)),
         ],
         flops=10_000_000,
         moved=8_000_000,
-    ).reshape(shell.shape)
-    got, shell_next = lax.optimization_barrier((got, shell_next))
+    )
+    got, shell_next, levels = lax.optimization_barrier((got, shell_next, levels))
     edges = [rows(2 * NF), pltpu.VMEM((2, KF, TH), F32)]
-    middle, source, lon_a, lon_b, lat, levels = call(
+    middle, source, lon_a, lon_b, lat = call(
         middle_kernel,
         "middle",
-        (middle, *halos, conductance, coupling, potential_weights.reshape(1, NF), got),
-        [(LON, KF, TH), (LON, TH), (KF, TH), (KF, TH), (2 * NF, TH), (KF + NF, TH)],
-        [VMEM] * 9,
-        scratch=edges,
+        (middle, *halos, conductance, levels, got),
+        [(LON, KF, TH), (LON, TH), (KF, TH), (KF, TH), (2 * NF, TH)],
+        [VMEM] * 6 + [HBM, VMEM],
+        scratch=[rows(KF), *edges, DMA],
         moved=8_000_000,
     )
     ends = exchange(lon_a, lon_b, lat)
-    last = call(
+    last, levels = call(
         second_kernel,
         "second",
-        (middle, conductance, chemistry),
-        [(LON, KF, TH)],
-        [VMEM] * 3,
+        (middle, conductance, chemistry, coupling, potential_weights.reshape(1, NF)),
+        [(LON, KF, TH), (KF + NF, TH)],
+        [VMEM] * 3 + [HBM] * 2,
+        scratch=[pltpu.VMEM((LEV, NF), F32), pltpu.VMEM((1, NF), F32), DMA((2,))],
         flops=60_000_000,
         moved=10_000_000,
     )
@@ -693,6 +752,7 @@
         [VMEM] * 9,
         scratch=[rows(LON), rows(NF), pltpu.VMEM((2, NF, TH), F32)],
     )
+    asked, shell_next = lax.optimization_barrier((asked, shell_next))
     back = lax.all_to_all(asked, "lon", split_axis=0, concat_axis=0, tiled=True)
     slab_next = call(
         finish_kernel,
@@ -704,6 +764,24 @@
         scratch=[slab_scratch, *edges, DMA],
         moved=8_000_000,
     )
+    shell_next = call(
+        shell_rest_kernel,
+        "shell_rest",
+        (shell_next, part, keep),
+        [(SHELL_ROWS * PH, TH)],
+        [HBM] * 3,
+        kept=(0,),
+        scratch=[
+            flat_scratch,
+            flat_scratch,
+            pltpu.VMEM((NV // 2, 2 * RAD + PH, TH), F32),
+            DMA((NV,)),
+            DMA((2,)),
+        ],
+        flops=10_000_000,
+        moved=8_000_000,
+        aliases={0: 0},
+    ).reshape(shell.shape)
     boundary = call(pick_kernel, "pick", (back, where), [(PH, TH)], [VMEM] * 2)
     return shell_next, slab_next, boundary
 

time: 72 us -> 69.4 us (0.964)
  starting transfers between devices: 28.9 us -> 32.9 us
  waiting for transfers between devices: 8.34 us -> 5.85 us
  local copies, waits for them, and re-layouts: 3.71 us -> 1.44 us
  Pallas kernels: 29.6 us -> 28 us
    all_to_all x1, starting transfers between devices: 4.67 us -> 7.56 us  [shards(): back = lax.all_to_all(asked, 'lon', split_axis=0, concat_axis=0, tiled=True)]
    unnamed x27 -> x19, local copies, waits for them, and re-layouts: 3.71 us -> 1.44 us
    all_to_all x1, waiting for transfers between devices: 4.49 us -> 2.82 us  [shards(): back = lax.all_to_all(asked, 'lon', split_axis=0, concat_axis=0, tiled=True)]
    pallas_call x9 -> x10, Pallas kernels: 29.6 us -> 28 us  [call(): pl.pallas_call(kernel, out_shape=shapes[0] if single else shapes, in_spec...]
    ppermute x4, waiting for transfers between devices: 1.53 us -> 0.01 us  [exchange(): lax.ppermute(block, ring, swaps(size, first, True))]
    ppermute x4, starting transfers between devices: 6.42 us -> 7.74 us  [exchange(): lax.ppermute(lat, 'lat', swaps(width, first, False))]
  transfers between devices with their start and end apart: 10 -> 10, of which waited for: 3 -> 2; matrix products, arithmetic and copies ran while one was open for 0% -> 0% of each run, Pallas kernels for 29% -> 27%
where the time goes in v3:
time: 69.4 us; the launch traced here: 69 us
  starting transfers between devices  32.9 us (47%)
  Pallas kernels  28 us (40%)
  waiting for transfers between devices  5.85 us (8%)
  local copies, waits for them, and re-layouts  1.44 us (2%)
  between operations  0.89 us (1%)
    pallas_call x10, Pallas kernels, call(): pl.pallas_call(kernel, out_shape=shapes[0] if single else shapes, in_spec...  28 us
    ppermute x4, starting transfers between devices, exchange(): lax.ppermute(block, ring, swaps(size, first, True))  12.8 us
    ppermute x4, starting transfers between devices, exchange(): lax.ppermute(lat, 'lat', swaps(width, first, False))  7.74 us
    all_to_all x1, starting transfers between devices, shards(): back = lax.all_to_all(asked, 'lon', split_axis=0, concat_axis=0, tiled=True)  7.56 us
    all_to_all x1, starting transfers between devices, shards(): got = lax.all_to_all(send, 'lon', split_axis=0, concat_axis=0, tiled=True)  4.8 us
    all_to_all x1, waiting for transfers between devices, shards(): got = lax.all_to_all(send, 'lon', split_axis=0, concat_axis=0, tiled=True)  3.01 us
    all_to_all x1, waiting for transfers between devices, shards(): back = lax.all_to_all(asked, 'lon', split_axis=0, concat_axis=0, tiled=True)  2.82 us
    unnamed x19, local copies, waits for them, and re-layouts  1.44 us
  transfers between devices with their start and end apart: 10, of which 2 were waited for; matrix products, arithmetic and copies ran while one was open for 0% of the time, Pallas kernels for 27%

profile of v3, /device:TPU:1, one launch (start us, length us, event | category | flops | bytes accessed | tf_op | source)
XLA Modules:
  0.0 69.0 jit_solution(2268371915861816771)
XLA Ops:
  0.6 0.0 copy-start.8
  0.6 0.0 copy-start
  0.7 0.0 copy-start.1
  0.7 0.0 copy-start.3
  0.7 4.4 %pack.1 = (f32[576,128]{1,0:T(8,128)}, f32[576,128]{1,0:T(8,128)}, f32[208,128]{1,0:T(8,128)}) custom-call(f32[40,8,16,128]{3,2,1,0:T(8,128)} %slab_ref.3, f32[4096,128]{1,0:T(8,128)} %bitcast.6), custom_call_target="tpu_custom_call" | custom-call | bytes 8000000 | tf_op jit(solution)/shard_map/pack/pallas_call | solution.py:609
  5.1 0.0 copy-start.6
  5.1 0.0 copy-start.7
  5.1 2.6 %collective-permute-start = (f32[576,128]{1,0:T(8,128)}, f32[576,128]{1,0:T(8,128)S(1)}, u32[]{:S(2)}, u32[]{:S(2)}) collective-permute-start(f32[576,128]{1,0:T(8,128)} %get-tuple-element.28), channel_id=1, source_target_pairs={{0,4},{4,0},{8,12},{12,8},{16,20},{20,16},{24,28},{28,24},{32,36},... | collective-permute-start | bytes 884744 | tf_op jit(solution)/shard_map/ppermute | solution.py:637
  7.6 5.8 %collective-permute-start.1 = (f32[576,128]{1,0:T(8,128)}, f32[576,128]{1,0:T(8,128)S(1)}, u32[]{:S(2)}, u32[]{:S(2)}) collective-permute-start(f32[576,128]{1,0:T(8,128)} %get-tuple-element.29), channel_id=1, source_target_pairs={{4,8},{8,4},{12,16},{16,12},{20,24},{24,20},{28,32},{32,28},{36,40... | collective-permute-start | bytes 884744 | tf_op jit(solution)/shard_map/ppermute | solution.py:637
  13.5 0.7 collective-permute-start.3
  14.1 3.7 %collective-permute-start.2 = (f32[208,128]{1,0:T(8,128)}, f32[208,128]{1,0:T(8,128)S(1)}, u32[]{:S(2)}, u32[]{:S(2)}) collective-permute-start(f32[208,128]{1,0:T(8,128)} %get-tuple-element.30), channel_id=1, source_target_pairs={{0,1},{1,0},{2,3},{3,2},{4,5},{5,4},{6,7},{7,6},{8,9},{9,8},{10,11... | collective-permute-start | bytes 319496 | tf_op jit(solution)/shard_map/ppermute | solution.py:635
  17.9 0.0 copy-done.8
  17.9 0.1 copy.15.fp_ref
  18.0 0.0 copy-done
  18.0 0.0 copy-done.1
  18.0 0.0 copy-done.3
  18.0 8.2 %interior.1 = (f32[16,320,128]{2,1,0:T(8,128)S(1)}, f32[8,32,16,128]{3,2,1,0:T(8,128)}, f32[8,16,128]{2,1,0:T(8,128)S(1)}, f32[96,128]{1,0:T(8,128)S(1)}) custom-call(f32[40,8,16,128]{3,2,1,0:T(8,128)} %slab_ref.3, f32[8,32,16,128]{3,2,1,0:T(8,128)} %shell_ref.1, f32[512,128]{1,0:T(8,128)} %bitcast.10, f32[3,8,8]{2,1,0:T(8,128)S(1)} %copy-done.1, ...), custom_call_target="tpu_custom_call" | custom-call | flops 90000000 | bytes 20000000 | tf_op jit(solution)/shard_map/interior/pallas_call | solution.py:609
  26.2 0.0 collective-permute-done.3.lat_b_all
  26.2 0.0 collective-permute-done.2.lat_a_all
  26.2 0.0 collective-permute-done.lon_a_all
  26.3 0.0 collective-permute-done.1.lon_b_all
  26.3 0.0 copy-done.6
  26.3 0.0 copy-done.7
  26.3 1.1 %current.1 = (f32[16,8,128]{2,1,0:T(8,128)S(1)}, f32[16,128]{1,0:T(8,128)S(1)}) custom-call(f32[8,16,128]{2,1,0:T(8,128)S(1)} %get-tuple-element.31.part_ref, f32[96,128]{1,0:T(8,128)S(1)} %get-tuple-element.32.res_all_ref.near_ref, f32[3,8,8]{2,1,0:T(8,128)S(1)} %copy-done.1, f32[8]{0:T(128)S(1)} %copy-done.6, s32[1,16,1]{2,1,0:T(8,128)S(1)} %copy.15.fp_ref, ...), custom_call_target="tpu_custom_call" | custom-call | tf_op jit(solution)/shard_map/current/pallas_call | solution.py:609
  27.4 0.0 copy-start.5
  27.4 0.6 copy-done.5
  28.0 4.8 %all-to-all-start = ((f32[16,8,128]{2,1,0:T(8,128)}), f32[16,8,128]{2,1,0:T(8,128)S(1)}, u32[]{:S(2)}, u32[]{:S(2)}) async-start(f32[16,8,128]{2,1,0:T(8,128)} %copy-done.5), calls=%async_computation | async-start | bytes 131072 | tf_op jit(solution)/shard_map/all_to_all | solution.py:704
  32.8 0.0 copy-start.2
  32.8 0.7 %copy-done.2 = f32[3,8,8]{2,1,0:T(8,128)S(1)} copy-done((f32[3,8,8]{2,1,0:T(8,128)S(1)}, f32[3,8,8]{2,1,0:T(8,128)}, u32[]{:S(2)}) %copy-start.2) | copy-done | bytes 792
  33.5 3.2 %shell_edge.1 = (f32[4096,128]{1,0:T(8,128)}, f32[4,80,128]{2,1,0:T(8,128)}, f32[320,128]{1,0:T(8,128)}) custom-call(f32[4096,128]{1,0:T(8,128)} %bitcast.7, f32[96,128]{1,0:T(8,128)S(1)} %get-tuple-element.32.res_all_ref.near_ref, f32[3,8,8]{2,1,0:T(8,128)S(1)} %copy-done.2, f32[576,128]{1,0:T(8,128)S(1)} %collective-permute-done.lon_a_all, ...), custom_call_target="tpu_custom_call" | custom-call | flops 10000000 | bytes 8000000 | tf_op jit(solution)/shard_map/shell_edge/pallas_call | solution.py:609
  36.8 0.0 copy-start.4
  36.8 3.0 %all-to-all-done.got_ref = f32[16,8,128]{2,1,0:T(8,128)S(1)} async-done(((f32[16,8,128]{2,1,0:T(8,128)}), f32[16,8,128]{2,1,0:T(8,128)S(1)}, u32[]{:S(2)}, u32[]{:S(2)}) %all-to-all-start) | async-done | bytes 65568 | tf_op jit(solution)/shard_map/all_to_all | solution.py:704
  39.8 2.5 %middle.1 = (f32[16,320,128]{2,1,0:T(8,128)S(1)}, f32[16,128]{1,0:T(8,128)S(1)}, f32[320,128]{1,0:T(8,128)S(1)}, f32[320,128]{1,0:T(8,128)S(1)}, f32[80,128]{1,0:T(8,128)S(1)}) custom-call(f32[16,320,128]{2,1,0:T(8,128)S(1)} %get-tuple-element.27.x_ref, f32[576,128]{1,0:T(8,128)S(1)} %collective-permute-done.lon_a_all, ...), custom_call_target="tpu_custom_call" | custom-call | bytes 8000000 | tf_op jit(solution)/shard_map/middle/pallas_call | solution.py:609
  42.3 0.4 collective-permute-start.4
  42.7 3.9 %collective-permute-start.5 = (f32[320,128]{1,0:T(8,128)S(1)}, f32[320,128]{1,0:T(8,128)S(1)}, u32[]{:S(2)}, u32[]{:S(2)}) collective-permute-start(f32[320,128]{1,0:T(8,128)S(1)} %get-tuple-element.42), channel_id=1, source_target_pairs={{4,8},{8,4},{12,16},{16,12},{20,24},{24,20},{28,32},{32,28},{36,40... | collective-permute-start | bytes 491528 | tf_op jit(solution)/shard_map/ppermute | solution.py:637
  46.7 0.7 collective-permute-start.7
  47.3 2.7 %collective-permute-start.6 = (f32[80,128]{1,0:T(8,128)S(1)}, f32[80,128]{1,0:T(8,128)S(1)}, u32[]{:S(2)}, u32[]{:S(2)}) collective-permute-start(f32[80,128]{1,0:T(8,128)S(1)} %get-tuple-element.43), channel_id=1, source_target_pairs={{0,1},{1,0},{2,3},{3,2},{4,5},{5,4},{6,7},{7,6},{8,9},{9,8},{10,11... | collective-permute-start | bytes 122888 | tf_op jit(solution)/shard_map/ppermute | solution.py:635
  50.0 0.0 copy-done.4
  50.0 2.8 %second.1 = (f32[16,320,128]{2,1,0:T(8,128)S(1)}, f32[360,128]{1,0:T(8,128)S(1)}) custom-call(f32[16,320,128]{2,1,0:T(8,128)S(1)} %get-tuple-element.39.x_ref, f32[16,128]{1,0:T(8,128)S(1)} %copy-done, f32[40,40]{1,0:T(8,128)S(1)} %copy-done.4, f32[8,40]{1,0:T(8,128)} %bitcast.12, f32[1,40]{1,0:T(1,128)} %bitcast.13), custom_call_target="tpu_custom_call" | custom-call | flops 60000000 | bytes 10000000 | tf_op jit(solution)/shard_map/second/pallas_call | solution.py:609
  52.9 0.0 collective-permute-done.7.lat_b_all.lat_b_ref
  52.9 0.0 collective-permute-done.6.lat_a_all.lat_a_ref
  52.9 0.0 collective-permute-done.4.lon_a_all.lon_a_ref
  52.9 0.0 collective-permute-done.5.lon_b_all.lon_b_ref
  52.9 0.9 %potential.1 = f32[16,8,128]{2,1,0:T(8,128)} custom-call(f32[16,320,128]{2,1,0:T(8,128)S(1)} %get-tuple-element.40.x_ref, f32[320,128]{1,0:T(8,128)S(1)} %collective-permute-done.4.lon_a_all.lon_a_ref, f32[320,128]{1,0:T(8,128)S(1)} %collective-permute-done.5.lon_b_all.lon_b_ref, f32[80,128]{1,0:T(8,128)S(1)} %collective-permute-done.6.lat_a_all.lat_a_ref, ...), custom_call_target="tpu_custom_call" | custom-call | tf_op jit(solution)/shard_map/potential/pallas_call | solution.py:609
  53.8 7.6 %all-to-all-start.1 = ((f32[16,8,128]{2,1,0:T(8,128)}), f32[16,8,128]{2,1,0:T(8,128)S(1)}, u32[]{:S(2)}, u32[]{:S(2)}) async-start(f32[16,8,128]{2,1,0:T(8,128)} %potential.1), calls=%async_computation.1 | async-start | bytes 131072 | tf_op jit(solution)/shard_map/all_to_all | solution.py:756
  61.4 1.6 %finish.1 = f32[40,8,16,128]{3,2,1,0:T(8,128)} custom-call(f32[16,320,128]{2,1,0:T(8,128)S(1)} %get-tuple-element.40.x_ref, f32[320,128]{1,0:T(8,128)S(1)} %collective-permute-done.4.lon_a_all.lon_a_ref, f32[320,128]{1,0:T(8,128)S(1)} %collective-permute-done.5.lon_b_all.lon_b_ref, f32[80,128]{1,0:T(8,128)S(1)} %collective-permute-done.6.lat_a_all.lat_a_ref, ...), custom_call_target="tpu_custom_call" | custom-call | bytes 8000000 | tf_op jit(solution)/shard_map/finish/pallas_call | solution.py:609
  63.0 2.6 %shell_rest.1 = f32[4096,128]{1,0:T(8,128)} custom-call(f32[4096,128]{1,0:T(8,128)} %get-tuple-element.47.half_ref, f32[4096,128]{1,0:T(8,128)} %bitcast.8, f32[4,80,128]{2,1,0:T(8,128)} %get-tuple-element.48.keep_ref), custom_call_target="tpu_custom_call", output_to_operand_aliasing={{}: (0, {})} | custom-call | flops 10000000 | bytes 8000000 | tf_op jit(solution)/shard_map/shell_rest/pallas_call | solution.py:609
  65.6 2.8 %all-to-all-done.1.got_ref = f32[16,8,128]{2,1,0:T(8,128)S(1)} async-done(((f32[16,8,128]{2,1,0:T(8,128)}), f32[16,8,128]{2,1,0:T(8,128)S(1)}, u32[]{:S(2)}, u32[]{:S(2)}) %all-to-all-start.1) | async-done | bytes 65568 | tf_op jit(solution)/shard_map/all_to_all | solution.py:756
  68.4 0.6 pick.1
Async XLA Ops:
  0.6 17.2 %copy-start.8 = (s32[1,16,1]{1,2,0:T(1,128)S(1)}, s32[1,16,1]{1,2,0:T(1,128)}, u32[]{:S(2)}) copy-start(s32[1,16,1]{1,2,0:T(1,128)} %param.15) | copy-start | bytes 196
  0.6 17.3 %copy-start = (f32[16,128]{1,0:T(8,128)S(1)}, f32[16,128]{1,0:T(8,128)}, u32[]{:S(2)}) copy-start(f32[16,128]{1,0:T(8,128)} %cond_ref.9) | copy-start | bytes 24580
  0.7 17.3 %copy-start.1 = (f32[3,8,8]{2,1,0:T(8,128)S(1)}, f32[3,8,8]{2,1,0:T(8,128)}, u32[]{:S(2)}) copy-start(f32[3,8,8]{2,1,0:T(8,128)} %jac_ref.5) | copy-start | bytes 2308
  0.7 17.3 %copy-start.3 = (f32[40,40]{1,0:T(8,128)S(1)}, f32[40,40]{1,0:T(8,128)}, u32[]{:S(2)}) copy-start(f32[40,40]{1,0:T(8,128)} %chem_ref.3) | copy-start | bytes 19204
  5.1 21.2 %copy-start.6 = (f32[8]{0:T(128)S(1)}, f32[8]{0:T(128)}, u32[]{:S(2)}) copy-start(f32[8]{0:T(128)} %weight_ref.1) | copy-start | bytes 100
  5.1 21.2 %copy-start.7 = (s32[1,16]{1,0:T(1,128)S(1)}, s32[1,16]{1,0:T(1,128)}, u32[]{:S(2)}) copy-start(s32[1,16]{1,0:T(1,128)} %row_ref.1) | copy-start | bytes 196
  5.1 21.2 %collective-permute-start = (f32[576,128]{1,0:T(8,128)}, f32[576,128]{1,0:T(8,128)S(1)}, u32[]{:S(2)}, u32[]{:S(2)}) collective-permute-start(f32[576,128]{1,0:T(8,128)} %get-tuple-element.28), channel_id=1, source_target_pairs={{0,4},{4,0},{8,12},{12,8},{16,20},{20,16},{24,28},{28,24},{32,36},... | collective-permute-start | bytes 884744 | tf_op jit(solution)/shard_map/ppermute | solution.py:637
  7.6 18.6 %collective-permute-start.1 = (f32[576,128]{1,0:T(8,128)}, f32[576,128]{1,0:T(8,128)S(1)}, u32[]{:S(2)}, u32[]{:S(2)}) collective-permute-start(f32[576,128]{1,0:T(8,128)} %get-tuple-element.29), channel_id=1, source_target_pairs={{4,8},{8,4},{12,16},{16,12},{20,24},{24,20},{28,32},{32,28},{36,40... | collective-permute-start | bytes 884744 | tf_op jit(solution)/shard_map/ppermute | solution.py:637
  13.5 12.8 %collective-permute-start.3 = (f32[208,128]{1,0:T(8,128)}, f32[208,128]{1,0:T(8,128)S(1)}, u32[]{:S(2)}, u32[]{:S(2)}) collective-permute-start(f32[208,128]{1,0:T(8,128)} %get-tuple-element.30), channel_id=1, source_target_pairs={{1,2},{2,1},{5,6},{6,5},{9,10},{10,9},{13,14},{14,13},{17,18},{18,... | collective-permute-start | bytes 319496 | tf_op jit(solution)/shard_map/ppermute | solution.py:635
  14.1 12.1 %collective-permute-start.2 = (f32[208,128]{1,0:T(8,128)}, f32[208,128]{1,0:T(8,128)S(1)}, u32[]{:S(2)}, u32[]{:S(2)}) collective-permute-start(f32[208,128]{1,0:T(8,128)} %get-tuple-element.30), channel_id=1, source_target_pairs={{0,1},{1,0},{2,3},{3,2},{4,5},{5,4},{6,7},{7,6},{8,9},{9,8},{10,11... | collective-permute-start | bytes 319496 | tf_op jit(solution)/shard_map/ppermute | solution.py:635
  27.4 0.6 copy-start.5
  28.0 11.8 %all-to-all-start = ((f32[16,8,128]{2,1,0:T(8,128)}), f32[16,8,128]{2,1,0:T(8,128)S(1)}, u32[]{:S(2)}, u32[]{:S(2)}) async-start(f32[16,8,128]{2,1,0:T(8,128)} %copy-done.5), calls=%async_computation | async-start | bytes 131072 | tf_op jit(solution)/shard_map/all_to_all | solution.py:704
  32.8 0.7 %copy-start.2 = (f32[3,8,8]{2,1,0:T(8,128)S(1)}, f32[3,8,8]{2,1,0:T(8,128)}, u32[]{:S(2)}) copy-start(f32[3,8,8]{2,1,0:T(8,128)} %jac_ref.5) | copy-start | bytes 2308
  36.8 13.2 %copy-start.4 = (f32[40,40]{1,0:T(8,128)S(1)}, f32[40,40]{1,0:T(8,128)}, u32[]{:S(2)}) copy-start(f32[40,40]{1,0:T(8,128)} %chem_ref.3) | copy-start | bytes 19204
  42.3 10.6 %collective-permute-start.4 = (f32[320,128]{1,0:T(8,128)S(1)}, f32[320,128]{1,0:T(8,128)S(1)}, u32[]{:S(2)}, u32[]{:S(2)}) collective-permute-start(f32[320,128]{1,0:T(8,128)S(1)} %get-tuple-element.41), channel_id=1, source_target_pairs={{0,4},{4,0},{8,12},{12,8},{16,20},{20,16},{24,28},{28,24},{32,36},... | collective-permute-start | bytes 491528 | tf_op jit(solution)/shard_map/ppermute | solution.py:637
  42.7 10.2 %collective-permute-start.5 = (f32[320,128]{1,0:T(8,128)S(1)}, f32[320,128]{1,0:T(8,128)S(1)}, u32[]{:S(2)}, u32[]{:S(2)}) collective-permute-start(f32[320,128]{1,0:T(8,128)S(1)} %get-tuple-element.42), channel_id=1, source_target_pairs={{4,8},{8,4},{12,16},{16,12},{20,24},{24,20},{28,32},{32,28},{36,40... | collective-permute-start | bytes 491528 | tf_op jit(solution)/shard_map/ppermute | solution.py:637
  46.7 6.2 %collective-permute-start.7 = (f32[80,128]{1,0:T(8,128)S(1)}, f32[80,128]{1,0:T(8,128)S(1)}, u32[]{:S(2)}, u32[]{:S(2)}) collective-permute-start(f32[80,128]{1,0:T(8,128)S(1)} %get-tuple-element.43), channel_id=1, source_target_pairs={{1,2},{2,1},{5,6},{6,5},{9,10},{10,9},{13,14},{14,13},{17,18},{18,... | collective-permute-start | bytes 122888 | tf_op jit(solution)/shard_map/ppermute | solution.py:635
  47.3 5.6 %collective-permute-start.6 = (f32[80,128]{1,0:T(8,128)S(1)}, f32[80,128]{1,0:T(8,128)S(1)}, u32[]{:S(2)}, u32[]{:S(2)}) collective-permute-start(f32[80,128]{1,0:T(8,128)S(1)} %get-tuple-element.43), channel_id=1, source_target_pairs={{0,1},{1,0},{2,3},{3,2},{4,5},{5,4},{6,7},{7,6},{8,9},{9,8},{10,11... | collective-permute-start | bytes 122888 | tf_op jit(solution)/shard_map/ppermute | solution.py:635
  53.8 14.6 %all-to-all-start.1 = ((f32[16,8,128]{2,1,0:T(8,128)}), f32[16,8,128]{2,1,0:T(8,128)S(1)}, u32[]{:S(2)}, u32[]{:S(2)}) async-start(f32[16,8,128]{2,1,0:T(8,128)} %potential.1), calls=%async_computation.1 | async-start | bytes 131072 | tf_op jit(solution)/shard_map/all_to_all | solution.py:756

commit v4 on v3

--- a/solution.py
+++ b/solution.py
@@ -272,7 +272,7 @@
 
 
 def interior_kernel(
-    slab_ref, shell_ref, res_ref, jac_ref, cond_ref, chem_ref,
+    slab_ref, shell_ref, res_ref, jac_ref, cond_ref, chem_ref, coupling_ref,
     m_ref, part_ref, first_ref, near_ref,
     s2_ref, sh_ref, so_ref, rs_ref, sems,
 ):
@@ -412,18 +412,17 @@
 
 
 def middle_kernel(
-    x_ref, lon_a_all, lon_b_all, lat_a_all, lat_b_all, cond_ref, level_all, got_ref,
+    x_ref, lon_a_all, lon_b_all, lat_a_all, lat_b_all, cond_ref, coupling_ref, got_ref,
     o_ref, source_ref, next_a_ref, next_b_ref, lat_ref,
-    level_ref, side_ref, end_ref, sem,
+    level_ref, side_ref, end_ref,
 ):
-    copy = go(level_all, level_ref, sem)
+    put_levels(coupling_ref, level_ref, LEV)
     lon_a_ref, lon_b_ref = lon_a_all.at[0:KF, :], lon_b_all.at[0:KF, :]
     lat_a_ref, lat_b_ref = lat_a_all.at[0 : 2 * NF, :], lat_b_all.at[0 : 2 * NF, :]
     source_ref[...] = gather_source(got_ref)
     put_edges(lon_a_ref, lon_b_ref, lat_a_ref, lat_b_ref, side_ref, end_ref)
     edge = edge_of(NF)
     slot = slot_of(NF)
-    copy.wait()
     for l in range(LON):
         c = 0.1 * cond_ref[l : l + 1, :]
         source = source_ref[l : l + 1, :]
@@ -526,11 +525,10 @@
 
 
 def shell_edge_kernel(
-    part_ref, near_ref, jac_ref, lon_a_all, lon_b_all, lat_a_all, lat_b_all, coupling_ref,
-    o_ref, keep_ref, level_all,
-    x_ref, y_ref, add_ref, cols_ref, level_ref, part_sems, sems,
+    part_ref, near_ref, jac_ref, lon_a_all, lon_b_all, lat_a_all, lat_b_all,
+    o_ref, keep_ref,
+    x_ref, y_ref, add_ref, part_sems, sems,
 ):
-    copy = go(coupling_ref, cols_ref, sems.at[2])
     loads = load_part(part_ref, x_ref, part_sems, range(NV // 2))
     lon_a_ref, lon_b_ref = lon_a_all.at[KF:, :], lon_b_all.at[KF:, :]
     lat_a_ref, lat_b_ref = lat_a_all.at[2 * NF :, :], lat_b_all.at[2 * NF :, :]
@@ -565,12 +563,8 @@
         corr = add_ref[u, 2 * RAD : 2 * RAD + PH, :]
         adds = [add_ref[u, last * RAD : (last + 1) * RAD, :] for last in range(2)]
         shell_edge_tile(u, x_ref, y_ref, o_ref, corr, adds, edge, sems.at[0])
-    copy.wait()
-    put_levels(cols_ref, level_ref, LEV)
-    copy = go(level_ref, level_all, sems.at[2])
     wait_half(y_ref, 0, sems.at[0])
     keep.wait()
-    copy.wait()
 
 
 def shell_rest_kernel(half_ref, part_ref, keep_ref, o_ref, x_ref, y_ref, add_ref, part_sems, sems):
@@ -679,9 +673,9 @@
     middle, part, first, near = call(
         interior_kernel,
         "interior",
-        (slab, shell, resistivity.reshape(RAD * PH, TH), jacobians, conductance, chemistry),
+        (slab, shell, resistivity.reshape(RAD * PH, TH), jacobians, conductance, chemistry, coupling),
         [(LON, KF, TH), shell.shape, (NV, PH, TH), (2 * PH + 2 * RAD, TH)],
-        [HBM, HBM, HBM, VMEM, VMEM, VMEM],
+        [HBM, HBM, HBM, VMEM, VMEM, VMEM, VMEM],
         kept=(1,),
         scratch=[
             slab_scratch,
@@ -703,34 +697,32 @@
     )
     got = lax.all_to_all(send, "lon", split_axis=0, concat_axis=0, tiled=True)
     part = part.reshape(SHELL_ROWS * PH, TH)
-    shell_next, keep, levels = call(
+    shell_next, keep = call(
         shell_edge_kernel,
         "shell_edge",
-        (part, near, jacobians, *halos, coupling),
-        [(SHELL_ROWS * PH, TH), (NV // 2, 2 * RAD + PH, TH), (KF, TH)],
-        [HBM, VMEM, SMEM] + [VMEM] * 4 + [HBM],
-        kept=(0, 1, 2),
+        (part, near, jacobians, *halos),
+        [(SHELL_ROWS * PH, TH), (NV // 2, 2 * RAD + PH, TH)],
+        [HBM, VMEM, SMEM] + [VMEM] * 4,
+        kept=(0, 1),
         scratch=[
             flat_scratch,
             flat_scratch,
             pltpu.VMEM((NV, 2 * RAD + PH, TH), F32),
-            pltpu.VMEM((LEV, NF), F32),
-            rows(KF),
             DMA((NV,)),
-            DMA((3,)),
+            DMA((2,)),
         ],
         flops=10_000_000,
         moved=8_000_000,
     )
-    got, shell_next, levels = lax.optimization_barrier((got, shell_next, levels))
+    got, shell_next = lax.optimization_barrier((got, shell_next))
     edges = [rows(2 * NF), pltpu.VMEM((2, KF, TH), F32)]
     middle, source, lon_a, lon_b, lat = call(
         middle_kernel,
         "middle",
-        (middle, *halos, conductance, levels, got),
+        (middle, *halos, conductance, coupling, got),
         [(LON, KF, TH), (LON, TH), (KF, TH), (KF, TH), (2 * NF, TH)],
-        [VMEM] * 6 + [HBM, VMEM],
-        scratch=[rows(KF), *edges, DMA],
+        [VMEM] * 8,
+        scratch=[rows(KF), *edges],
         moved=8_000_000,
     )
     ends = exchange(lon_a, lon_b, lat)

time: 69.4 us -> 69.1 us (level)
  Pallas kernels: 28 us -> 27 us
    pallas_call x10, Pallas kernels: 28 us -> 27 us  [call(): pl.pallas_call(kernel, out_shape=shapes[0] if single else shapes, in_spec...]
    unnamed x19 -> x25, local copies, waits for them, and re-layouts: 1.44 us -> 2.06 us
where the time goes in v4:
time: 69.1 us; the launch traced here: 68.8 us
  starting transfers between devices  32.8 us (47%)
  Pallas kernels  27 us (39%)
  waiting for transfers between devices  5.93 us (9%)
  local copies, waits for them, and re-layouts  2.06 us (3%)
  between operations  0.91 us (1%)
    pallas_call x10, Pallas kernels, call(): pl.pallas_call(kernel, out_shape=shapes[0] if single else shapes, in_spec...  27 us
    ppermute x4, starting transfers between devices, exchange(): lax.ppermute(block, ring, swaps(size, first, True))  12.8 us
    ppermute x4, starting transfers between devices, exchange(): lax.ppermute(lat, 'lat', swaps(width, first, False))  7.73 us
    all_to_all x1, starting transfers between devices, shards(): back = lax.all_to_all(asked, 'lon', split_axis=0, concat_axis=0, tiled=True)  7.56 us
    all_to_all x1, starting transfers between devices, shards(): got = lax.all_to_all(send, 'lon', split_axis=0, concat_axis=0, tiled=True)  4.79 us
    all_to_all x1, waiting for transfers between devices, shards(): got = lax.all_to_all(send, 'lon', split_axis=0, concat_axis=0, tiled=True)  3.11 us
    all_to_all x1, waiting for transfers between devices, shards(): back = lax.all_to_all(asked, 'lon', split_axis=0, concat_axis=0, tiled=True)  2.81 us
    unnamed x25, local copies, waits for them, and re-layouts  2.06 us
  transfers between devices with their start and end apart: 10, of which 2 were waited for; matrix products, arithmetic and copies ran while one was open for 0% of the time, Pallas kernels for 27%

profile of v4, /device:TPU:1, one launch (start us, length us, event | category | flops | bytes accessed | tf_op | source)
XLA Modules:
  0.0 68.8 jit_solution(16958378887481614725)
XLA Ops:
  0.6 0.0 copy-start.11
  0.6 0.0 copy-start
  0.7 0.0 copy-start.1
  0.7 0.0 copy-start.3
  0.7 0.0 copy-start.6
  0.7 4.4 %pack.1 = (f32[576,128]{1,0:T(8,128)}, f32[576,128]{1,0:T(8,128)}, f32[208,128]{1,0:T(8,128)}) custom-call(f32[40,8,16,128]{3,2,1,0:T(8,128)} %slab_ref.3, f32[4096,128]{1,0:T(8,128)} %bitcast.11), custom_call_target="tpu_custom_call" | custom-call | bytes 8000000 | tf_op jit(solution)/shard_map/pack/pallas_call | solution.py:603
  5.0 0.0 copy-start.9
  5.1 0.0 copy-start.10
  5.1 2.6 %collective-permute-start = (f32[576,128]{1,0:T(8,128)}, f32[576,128]{1,0:T(8,128)S(1)}, u32[]{:S(2)}, u32[]{:S(2)}) collective-permute-start(f32[576,128]{1,0:T(8,128)} %get-tuple-element.26), channel_id=1, source_target_pairs={{0,4},{4,0},{8,12},{12,8},{16,20},{20,16},{24,28},{28,24},{32,36},... | collective-permute-start | bytes 884744 | tf_op jit(solution)/shard_map/ppermute | solution.py:631
  7.6 5.8 %collective-permute-start.1 = (f32[576,128]{1,0:T(8,128)}, f32[576,128]{1,0:T(8,128)S(1)}, u32[]{:S(2)}, u32[]{:S(2)}) collective-permute-start(f32[576,128]{1,0:T(8,128)} %get-tuple-element.27), channel_id=1, source_target_pairs={{4,8},{8,4},{12,16},{16,12},{20,24},{24,20},{28,32},{32,28},{36,40... | collective-permute-start | bytes 884744 | tf_op jit(solution)/shard_map/ppermute | solution.py:631
  13.5 0.7 collective-permute-start.3
  14.1 3.7 %collective-permute-start.2 = (f32[208,128]{1,0:T(8,128)}, f32[208,128]{1,0:T(8,128)S(1)}, u32[]{:S(2)}, u32[]{:S(2)}) collective-permute-start(f32[208,128]{1,0:T(8,128)} %get-tuple-element.28), channel_id=1, source_target_pairs={{0,1},{1,0},{2,3},{3,2},{4,5},{5,4},{6,7},{7,6},{8,9},{9,8},{10,11... | collective-permute-start | bytes 319496 | tf_op jit(solution)/shard_map/ppermute | solution.py:629
  17.9 0.0 copy-done.11
  17.9 0.1 copy.15.fp_ref
  18.0 0.0 copy-done
  18.0 0.0 copy-done.1
  18.0 0.0 copy-done.3
  18.0 0.0 copy-done.6
  18.0 8.2 %interior.1 = (f32[16,320,128]{2,1,0:T(8,128)S(1)}, f32[8,32,16,128]{3,2,1,0:T(8,128)}, f32[8,16,128]{2,1,0:T(8,128)S(1)}, f32[96,128]{1,0:T(8,128)S(1)}) custom-call(f32[40,8,16,128]{3,2,1,0:T(8,128)} %slab_ref.3, f32[8,32,16,128]{3,2,1,0:T(8,128)} %shell_ref.1, f32[512,128]{1,0:T(8,128)} %bitcast.13, f32[3,8,8]{2,1,0:T(8,128)S(1)} %copy-done.1, ...), custom_call_target="tpu_custom_call" | custom-call | flops 90000000 | bytes 20000000 | tf_op jit(solution)/shard_map/interior/pallas_call | solution.py:603
  26.2 0.0 collective-permute-done.3.lat_b_all
  26.2 0.0 collective-permute-done.2.lat_a_all
  26.2 0.0 collective-permute-done.lon_a_all
  26.3 0.0 collective-permute-done.1.lon_b_all
  26.3 0.0 copy-done.9
  26.3 0.0 copy-done.10
  26.3 1.1 %current.1 = (f32[16,8,128]{2,1,0:T(8,128)S(1)}, f32[16,128]{1,0:T(8,128)S(1)}) custom-call(f32[8,16,128]{2,1,0:T(8,128)S(1)} %get-tuple-element.29.part_ref, f32[96,128]{1,0:T(8,128)S(1)} %get-tuple-element.30.res_all_ref.near_ref, f32[3,8,8]{2,1,0:T(8,128)S(1)} %copy-done.1, f32[8]{0:T(128)S(1)} %copy-done.9, s32[1,16,1]{2,1,0:T(8,128)S(1)} %copy.15.fp_ref, ...), custom_call_target="tpu_custom_call" | custom-call | tf_op jit(solution)/shard_map/current/pallas_call | solution.py:603
  27.4 0.0 copy-start.5
  27.4 0.6 copy-done.5
  28.0 0.0 copy-start.7
  28.0 0.6 copy-done.7
  28.6 4.8 %all-to-all-start = ((f32[16,8,128]{2,1,0:T(8,128)}), f32[16,8,128]{2,1,0:T(8,128)S(1)}, u32[]{:S(2)}, u32[]{:S(2)}) async-start(f32[16,8,128]{2,1,0:T(8,128)} %copy-done.5), calls=%async_computation | async-start | bytes 131072 | tf_op jit(solution)/shard_map/all_to_all | solution.py:698
  33.4 0.0 copy-start.2
  33.4 0.7 %copy-done.2 = f32[3,8,8]{2,1,0:T(8,128)S(1)} copy-done((f32[3,8,8]{2,1,0:T(8,128)S(1)}, f32[3,8,8]{2,1,0:T(8,128)}, u32[]{:S(2)}) %copy-start.2) | copy-done | bytes 792
  34.1 3.2 %shell_edge.1 = (f32[4096,128]{1,0:T(8,128)}, f32[4,80,128]{2,1,0:T(8,128)}) custom-call(f32[4096,128]{1,0:T(8,128)} %bitcast.9, f32[96,128]{1,0:T(8,128)S(1)} %get-tuple-element.30.res_all_ref.near_ref, f32[3,8,8]{2,1,0:T(8,128)S(1)} %copy-done.2, f32[576,128]{1,0:T(8,128)S(1)} %collective-permute-done.lon_a_all, ...), custom_call_target="tpu_custom_call" | custom-call | flops 10000000 | bytes 8000000 | tf_op jit(solution)/shard_map/shell_edge/pallas_call | solution.py:603
  37.3 0.0 copy-start.4
  37.3 3.1 %all-to-all-done.got_ref = f32[16,8,128]{2,1,0:T(8,128)S(1)} async-done(((f32[16,8,128]{2,1,0:T(8,128)}), f32[16,8,128]{2,1,0:T(8,128)S(1)}, u32[]{:S(2)}, u32[]{:S(2)}) %all-to-all-start) | async-done | bytes 65568 | tf_op jit(solution)/shard_map/all_to_all | solution.py:698
  40.4 1.6 %middle.1 = (f32[16,320,128]{2,1,0:T(8,128)S(1)}, f32[16,128]{1,0:T(8,128)S(1)}, f32[320,128]{1,0:T(8,128)S(1)}, f32[320,128]{1,0:T(8,128)S(1)}, f32[80,128]{1,0:T(8,128)S(1)}) custom-call(f32[16,320,128]{2,1,0:T(8,128)S(1)} %get-tuple-element.25.x_ref, f32[576,128]{1,0:T(8,128)S(1)} %collective-permute-done.lon_a_all, ...), custom_call_target="tpu_custom_call" | custom-call | bytes 8000000 | tf_op jit(solution)/shard_map/middle/pallas_call | solution.py:603
  42.0 0.4 collective-permute-start.4
  42.5 3.9 %collective-permute-start.5 = (f32[320,128]{1,0:T(8,128)S(1)}, f32[320,128]{1,0:T(8,128)S(1)}, u32[]{:S(2)}, u32[]{:S(2)}) collective-permute-start(f32[320,128]{1,0:T(8,128)S(1)} %get-tuple-element.38), channel_id=1, source_target_pairs={{4,8},{8,4},{12,16},{16,12},{20,24},{24,20},{28,32},{32,28},{36,40... | collective-permute-start | bytes 491528 | tf_op jit(solution)/shard_map/ppermute | solution.py:631
  46.4 0.7 collective-permute-start.7
  47.1 2.7 %collective-permute-start.6 = (f32[80,128]{1,0:T(8,128)S(1)}, f32[80,128]{1,0:T(8,128)S(1)}, u32[]{:S(2)}, u32[]{:S(2)}) collective-permute-start(f32[80,128]{1,0:T(8,128)S(1)} %get-tuple-element.39), channel_id=1, source_target_pairs={{0,1},{1,0},{2,3},{3,2},{4,5},{5,4},{6,7},{7,6},{8,9},{9,8},{10,11... | collective-permute-start | bytes 122888 | tf_op jit(solution)/shard_map/ppermute | solution.py:629
  49.7 0.0 copy-done.4
  49.7 2.8 %second.1 = (f32[16,320,128]{2,1,0:T(8,128)S(1)}, f32[360,128]{1,0:T(8,128)S(1)}) custom-call(f32[16,320,128]{2,1,0:T(8,128)S(1)} %get-tuple-element.35.x_ref, f32[16,128]{1,0:T(8,128)S(1)} %copy-done, f32[40,40]{1,0:T(8,128)S(1)} %copy-done.4, f32[8,40]{1,0:T(8,128)} %bitcast.6, f32[1,40]{1,0:T(1,128)} %bitcast.14), custom_call_target="tpu_custom_call" | custom-call | flops 60000000 | bytes 10000000 | tf_op jit(solution)/shard_map/second/pallas_call | solution.py:603
  52.6 0.0 collective-permute-done.7.lat_b_all.lat_b_ref
  52.6 0.0 collective-permute-done.6.lat_a_all.lat_a_ref
  52.6 0.0 collective-permute-done.4.lon_a_all.lon_a_ref
  52.6 0.0 collective-permute-done.5.lon_b_all.lon_b_ref
  52.6 0.9 %potential.1 = f32[16,8,128]{2,1,0:T(8,128)} custom-call(f32[16,320,128]{2,1,0:T(8,128)S(1)} %get-tuple-element.36.x_ref, f32[320,128]{1,0:T(8,128)S(1)} %collective-permute-done.4.lon_a_all.lon_a_ref, f32[320,128]{1,0:T(8,128)S(1)} %collective-permute-done.5.lon_b_all.lon_b_ref, f32[80,128]{1,0:T(8,128)S(1)} %collective-permute-done.6.lat_a_all.lat_a_ref, ...), custom_call_target="tpu_custom_call" | custom-call | tf_op jit(solution)/shard_map/potential/pallas_call | solution.py:603
  53.5 7.6 %all-to-all-start.1 = ((f32[16,8,128]{2,1,0:T(8,128)}), f32[16,8,128]{2,1,0:T(8,128)S(1)}, u32[]{:S(2)}, u32[]{:S(2)}) async-start(f32[16,8,128]{2,1,0:T(8,128)} %potential.1), calls=%async_computation.1 | async-start | bytes 131072 | tf_op jit(solution)/shard_map/all_to_all | solution.py:748
  61.1 1.6 %finish.1 = f32[40,8,16,128]{3,2,1,0:T(8,128)} custom-call(f32[16,320,128]{2,1,0:T(8,128)S(1)} %get-tuple-element.36.x_ref, f32[320,128]{1,0:T(8,128)S(1)} %collective-permute-done.4.lon_a_all.lon_a_ref, f32[320,128]{1,0:T(8,128)S(1)} %collective-permute-done.5.lon_b_all.lon_b_ref, f32[80,128]{1,0:T(8,128)S(1)} %collective-permute-done.6.lat_a_all.lat_a_ref, ...), custom_call_target="tpu_custom_call" | custom-call | bytes 8000000 | tf_op jit(solution)/shard_map/finish/pallas_call | solution.py:603
  62.7 0.0 copy-start.8
  62.7 2.6 %shell_rest.1 = f32[4096,128]{1,0:T(8,128)} custom-call(f32[4096,128]{1,0:T(8,128)} %get-tuple-element.43.half_ref, f32[4096,128]{1,0:T(8,128)} %bitcast.10, f32[4,80,128]{2,1,0:T(8,128)} %get-tuple-element.44.keep_ref), custom_call_target="tpu_custom_call", output_to_operand_aliasing={{}: (0, {})} | custom-call | flops 10000000 | bytes 8000000 | tf_op jit(solution)/shard_map/shell_rest/pallas_call | solution.py:603
  65.3 2.8 %all-to-all-done.1.got_ref = f32[16,8,128]{2,1,0:T(8,128)S(1)} async-done(((f32[16,8,128]{2,1,0:T(8,128)}), f32[16,8,128]{2,1,0:T(8,128)S(1)}, u32[]{:S(2)}, u32[]{:S(2)}) %all-to-all-start.1) | async-done | bytes 65568 | tf_op jit(solution)/shard_map/all_to_all | solution.py:748
  68.1 0.0 copy-done.8
  68.1 0.6 pick.1
Async XLA Ops:
  0.6 17.2 %copy-start.11 = (s32[1,16,1]{1,2,0:T(1,128)S(1)}, s32[1,16,1]{1,2,0:T(1,128)}, u32[]{:S(2)}) copy-start(s32[1,16,1]{1,2,0:T(1,128)} %param.15) | copy-start | bytes 196
  0.6 17.3 %copy-start = (f32[16,128]{1,0:T(8,128)S(1)}, f32[16,128]{1,0:T(8,128)}, u32[]{:S(2)}) copy-start(f32[16,128]{1,0:T(8,128)} %cond_ref.9) | copy-start | bytes 24580
  0.7 17.3 %copy-start.1 = (f32[3,8,8]{2,1,0:T(8,128)S(1)}, f32[3,8,8]{2,1,0:T(8,128)}, u32[]{:S(2)}) copy-start(f32[3,8,8]{2,1,0:T(8,128)} %jac_ref.5) | copy-start | bytes 2308
  0.7 17.3 %copy-start.3 = (f32[40,40]{1,0:T(8,128)S(1)}, f32[40,40]{1,0:T(8,128)}, u32[]{:S(2)}) copy-start(f32[40,40]{1,0:T(8,128)} %chem_ref.3) | copy-start | bytes 19204
  0.7 17.3 %copy-start.6 = (f32[40,8]{0,1:T(8,128)S(1)}, f32[40,8]{0,1:T(8,128)}, u32[]{:S(2)}) copy-start(f32[40,8]{0,1:T(8,128)} %param.20) | copy-start | bytes 3844
  5.0 21.2 %copy-start.9 = (f32[8]{0:T(128)S(1)}, f32[8]{0:T(128)}, u32[]{:S(2)}) copy-start(f32[8]{0:T(128)} %weight_ref.1) | copy-start | bytes 100
  5.1 21.2 %copy-start.10 = (s32[1,16]{1,0:T(1,128)S(1)}, s32[1,16]{1,0:T(1,128)}, u32[]{:S(2)}) copy-start(s32[1,16]{1,0:T(1,128)} %row_ref.1) | copy-start | bytes 196
  5.1 21.2 %collective-permute-start = (f32[576,128]{1,0:T(8,128)}, f32[576,128]{1,0:T(8,128)S(1)}, u32[]{:S(2)}, u32[]{:S(2)}) collective-permute-start(f32[576,128]{1,0:T(8,128)} %get-tuple-element.26), channel_id=1, source_target_pairs={{0,4},{4,0},{8,12},{12,8},{16,20},{20,16},{24,28},{28,24},{32,36},... | collective-permute-start | bytes 884744 | tf_op jit(solution)/shard_map/ppermute | solution.py:631
  7.6 18.6 %collective-permute-start.1 = (f32[576,128]{1,0:T(8,128)}, f32[576,128]{1,0:T(8,128)S(1)}, u32[]{:S(2)}, u32[]{:S(2)}) collective-permute-start(f32[576,128]{1,0:T(8,128)} %get-tuple-element.27), channel_id=1, source_target_pairs={{4,8},{8,4},{12,16},{16,12},{20,24},{24,20},{28,32},{32,28},{36,40... | collective-permute-start | bytes 884744 | tf_op jit(solution)/shard_map/ppermute | solution.py:631
  13.5 12.8 %collective-permute-start.3 = (f32[208,128]{1,0:T(8,128)}, f32[208,128]{1,0:T(8,128)S(1)}, u32[]{:S(2)}, u32[]{:S(2)}) collective-permute-start(f32[208,128]{1,0:T(8,128)} %get-tuple-element.28), channel_id=1, source_target_pairs={{1,2},{2,1},{5,6},{6,5},{9,10},{10,9},{13,14},{14,13},{17,18},{18,... | collective-permute-start | bytes 319496 | tf_op jit(solution)/shard_map/ppermute | solution.py:629
  14.1 12.1 %collective-permute-start.2 = (f32[208,128]{1,0:T(8,128)}, f32[208,128]{1,0:T(8,128)S(1)}, u32[]{:S(2)}, u32[]{:S(2)}) collective-permute-start(f32[208,128]{1,0:T(8,128)} %get-tuple-element.28), channel_id=1, source_target_pairs={{0,1},{1,0},{2,3},{3,2},{4,5},{5,4},{6,7},{7,6},{8,9},{9,8},{10,11... | collective-permute-start | bytes 319496 | tf_op jit(solution)/shard_map/ppermute | solution.py:629
  27.4 0.6 copy-start.5
  28.0 0.6 copy-start.7
  28.6 11.8 %all-to-all-start = ((f32[16,8,128]{2,1,0:T(8,128)}), f32[16,8,128]{2,1,0:T(8,128)S(1)}, u32[]{:S(2)}, u32[]{:S(2)}) async-start(f32[16,8,128]{2,1,0:T(8,128)} %copy-done.5), calls=%async_computation | async-start | bytes 131072 | tf_op jit(solution)/shard_map/all_to_all | solution.py:698
  33.4 0.7 %copy-start.2 = (f32[3,8,8]{2,1,0:T(8,128)S(1)}, f32[3,8,8]{2,1,0:T(8,128)}, u32[]{:S(2)}) copy-start(f32[3,8,8]{2,1,0:T(8,128)} %jac_ref.5) | copy-start | bytes 2308
  37.3 12.4 %copy-start.4 = (f32[40,40]{1,0:T(8,128)S(1)}, f32[40,40]{1,0:T(8,128)}, u32[]{:S(2)}) copy-start(f32[40,40]{1,0:T(8,128)} %chem_ref.3) | copy-start | bytes 19204
  42.0 10.6 %collective-permute-start.4 = (f32[320,128]{1,0:T(8,128)S(1)}, f32[320,128]{1,0:T(8,128)S(1)}, u32[]{:S(2)}, u32[]{:S(2)}) collective-permute-start(f32[320,128]{1,0:T(8,128)S(1)} %get-tuple-element.37), channel_id=1, source_target_pairs={{0,4},{4,0},{8,12},{12,8},{16,20},{20,16},{24,28},{28,24},{32,36},... | collective-permute-start | bytes 491528 | tf_op jit(solution)/shard_map/ppermute | solution.py:631
  42.5 10.2 %collective-permute-start.5 = (f32[320,128]{1,0:T(8,128)S(1)}, f32[320,128]{1,0:T(8,128)S(1)}, u32[]{:S(2)}, u32[]{:S(2)}) collective-permute-start(f32[320,128]{1,0:T(8,128)S(1)} %get-tuple-element.38), channel_id=1, source_target_pairs={{4,8},{8,4},{12,16},{16,12},{20,24},{24,20},{28,32},{32,28},{36,40... | collective-permute-start | bytes 491528 | tf_op jit(solution)/shard_map/ppermute | solution.py:631
  46.4 6.2 %collective-permute-start.7 = (f32[80,128]{1,0:T(8,128)S(1)}, f32[80,128]{1,0:T(8,128)S(1)}, u32[]{:S(2)}, u32[]{:S(2)}) collective-permute-start(f32[80,128]{1,0:T(8,128)S(1)} %get-tuple-element.39), channel_id=1, source_target_pairs={{1,2},{2,1},{5,6},{6,5},{9,10},{10,9},{13,14},{14,13},{17,18},{18,... | collective-permute-start | bytes 122888 | tf_op jit(solution)/shard_map/ppermute | solution.py:629
  47.1 5.5 %collective-permute-start.6 = (f32[80,128]{1,0:T(8,128)S(1)}, f32[80,128]{1,0:T(8,128)S(1)}, u32[]{:S(2)}, u32[]{:S(2)}) collective-permute-start(f32[80,128]{1,0:T(8,128)S(1)} %get-tuple-element.39), channel_id=1, source_target_pairs={{0,1},{1,0},{2,3},{3,2},{4,5},{5,4},{6,7},{7,6},{8,9},{9,8},{10,11... | collective-permute-start | bytes 122888 | tf_op jit(solution)/shard_map/ppermute | solution.py:629
  53.5 14.6 %all-to-all-start.1 = ((f32[16,8,128]{2,1,0:T(8,128)}), f32[16,8,128]{2,1,0:T(8,128)S(1)}, u32[]{:S(2)}, u32[]{:S(2)}) async-start(f32[16,8,128]{2,1,0:T(8,128)} %potential.1), calls=%async_computation.1 | async-start | bytes 131072 | tf_op jit(solution)/shard_map/all_to_all | solution.py:748
  62.7 5.4 %copy-start.8 = (f32[16,128]{1,0:T(8,128)S(1)}, f32[16,128]{1,0:T(8,128)}, u32[]{:S(2)}) copy-start(f32[16,128]{1,0:T(8,128)} %copy-done.7) | copy-start | bytes 24580
